TPU v7x, 256 devices: a whole 4x4x8 slice. The times are simulated.
256 devices in a mesh: img: 16 (over z, x_lo), txt: 16 (over y, x_hi, core).
Axes of the slice: x: 4 (x_hi: 2, x_lo: 2; x = x_hi * 2 + x_lo), y: 4, z: 8, core: 2. Of those that a mesh axis runs over, the one named last changes fastest.
Arguments:
- image_hidden: bfloat16 [8192, 1152], P(('img', 'txt')), may hold values from -12 to 12
- image_acts: bfloat16 [8192, 4304], P('img', 'txt'), may hold values from -6 to 6
- image_proj: bfloat16 [4304, 1152], P('txt'), may hold values from -0.09375 to 0.09375
- text_hidden: bfloat16 [8192, 1152], P(('txt', 'img')), may hold values from -12 to 12
- text_acts: bfloat16 [8192, 4304], P('txt', 'img'), may hold values from -6 to 6
- text_proj: bfloat16 [4304, 1152], P('img'), may hold values from -0.09375 to 0.09375
- positives: int32 [8192], P('img'), may hold values from 0 to 8191, each once
- log_scale: float32 [1], replicated, may hold values from 1.6 to 2.7
- bias: float32 [1], replicated, may hold values from -7 to -5
Outputs:
- loss: float32 [1], replicated
- image_grad: bfloat16 [8192, 1152], P(('img', 'txt'))
- text_grad: bfloat16 [8192, 1152], P(('txt', 'img'))
- image_act_grad: bfloat16 [8192, 4304], P('img', 'txt')
- text_act_grad: bfloat16 [8192, 4304], P('txt', 'img')
- image_proj_grad: float32 [4304, 1152], P('txt', 'img')
- text_proj_grad: float32 [4304, 1152], P('img', 'txt')
Inputs may be any that keep to these rules, and one draw needn't show every extreme that they name: `positives`: every text index is the positive of exactly one image.
All inputs are finite; a program needn't handle non-finite values.
Results may differ from a plain program's by a relative error of at most 0.007.
Values may be sent and summed in bfloat16 or wider, within the bound.
No kernel may reach another device: no remote copies, remote signals or barrier semaphores. Data moves between devices by JAX's collectives and lax.ppermute only.
A program may use at most 64 MiB of HBM per device.

v0:
```python
import functools

import jax
import jax.numpy as jnp
from jax import lax
from jax.experimental import pallas as pl
from jax.experimental.pallas import tpu as pltpu
from jax.sharding import Mesh, PartitionSpec as P

AXES = ("z", "xl", "y", "xh", "c")
SIZES = (8, 2, 4, 2, 2)
IMG = ("z", "xl")
TXT = ("y", "xh", "c")
PLANE = ("xl", "y", "xh")
SWAP = [(0, 1), (1, 0)]
f32 = jnp.float32
bf16 = jnp.bfloat16


def normalize(embed):
    values = embed.astype(f32)
    inverse = lax.rsqrt(jnp.sum(values * values, axis=-1, keepdims=True) + 1e-06)
    return (values * inverse, inverse)


def project(embed, upstream):
    unit, inverse = normalize(embed)
    return inverse * (upstream - unit * jnp.sum(unit * upstream, axis=-1, keepdims=True))


def dot(left, right):
    return jnp.dot(left, right, preferred_element_type=f32)


def contract_rows(left, right):
    return lax.dot_general(left, right, (((0,), (0,)), ((), ())), preferred_element_type=f32)


def contract_cols(left, right):
    return lax.dot_general(left, right, (((1,), (1,)), ((), ())), preferred_element_type=f32)


def pick(blocks, index, axis=0):
    return lax.dynamic_index_in_dim(blocks, index, axis, keepdims=False)


def swap(block, axis):
    return lax.ppermute(block, axis, SWAP)


def pair(mine, other, index):
    return jnp.where(index == 0, jnp.stack([mine, other]), jnp.stack([other, mine]))


def shift(block, axis, step, count=4):
    return lax.ppermute(block, axis, [(i, (i + step) % count) for i in range(count)])


def plane_pairs(step, first):
    pairs = []
    for x in range(4):
        for y in range(4):
            for c in range(2):
                x2, y2 = ((x + step) % 4, y) if (c == 0) == first else (x, (y + step) % 4)
                pairs.append(
                    (((x % 2) * 4 + y) * 4 + (x // 2) * 2 + c, ((x2 % 2) * 4 + y2) * 4 + (x2 // 2) * 2 + c)
                )
    return pairs


def plane_shift(block, step, first):
    return lax.ppermute(block, ("xl", "y", "xh", "c"), plane_pairs(step % 4, first))


def plane_gather(block, done):
    row = jnp.stack([block] + [plane_shift(block, d, True) for d in (1, 2, 3)])
    row = after(row, done)
    return jnp.stack([row] + [plane_shift(row, d, False) for d in (1, 2, 3)])


def plane_sum(slab):
    row = slab[0].astype(f32)
    for d in (1, 2, 3):
        row = row + plane_shift(slab[d], -d, False).astype(f32)
    row = row.astype(bf16)
    total = row[0].astype(f32)
    for d in (1, 2, 3):
        total = total + plane_shift(row[d], -d, True).astype(f32)
    return total


def exchange(blocks, axis):
    return lax.all_to_all(blocks, axis, 0, 0)


def gather(block, axis):
    return exchange(jnp.broadcast_to(block[None], (lax.axis_size(axis),) + block.shape), axis)


def scatter_sum(blocks, axis):
    return jnp.sum(exchange(blocks, axis).astype(f32), axis=0)


def two_halves(value):
    high = lax.reduce_precision(value, 8, 7)
    return jnp.stack([high, value - high]).astype(bf16)


CHUNK = 256
VMEM = pl.BlockSpec(memory_space=pltpu.VMEM)
SMEM = pl.BlockSpec(memory_space=pltpu.SMEM)


def score_rows(params, base, image, unit, labels, total, slope_out):
    scale, bias = params[0], params[1]
    index = lax.broadcasted_iota(jnp.int32, (unit.shape[0], 1), 0)
    columns = base[0] + index + (index & -32)
    loss = jnp.zeros((1, CHUNK), f32)
    for start in range(0, image.shape[0], CHUNK):
        part = pl.ds(start, CHUNK)
        image_unit = normalize(image[part, :])[0].astype(bf16)
        scores = scale * contract_cols(unit, image_unit) + bias
        hit = labels[:, part] == columns
        small = jnp.exp(-jnp.abs(scores))
        signed = jnp.where(hit, -scores, scores)
        terms = jnp.maximum(signed, 0.0) + jnp.log1p(small)
        loss = loss + jnp.sum(terms, axis=0, keepdims=True)
        sigmoid = jnp.where(scores >= 0.0, 1.0, small) / (1.0 + small)
        slope = (sigmoid - hit.astype(f32)).astype(bf16)
        slope_out[:, part] = slope
        total = total + dot(slope, image_unit)
    return total, loss


def score_kernel(params, base, image, text, labels, total_out, unit_out, slope_out, loss_out):
    unit = normalize(text[...])[0].astype(bf16)
    unit_out[...] = unit
    total = jnp.zeros(text.shape, f32)
    total, loss = score_rows(params, base, image, unit, labels, total, slope_out)
    total_out[...] = total
    loss_out[...] = loss


def rest_kernel(params, base, image, text, labels, total, unit, loss, parts_out, slope_out, loss_out):
    sums, more = score_rows(params, base, image, unit[...], labels, total[...], slope_out)
    parts_out[...] = project(text[...], params[0] * sums).astype(bf16)
    loss_out[...] = loss[...] + more


def image_kernel(params, slope, text_unit, image, image_parts):
    for start in range(0, image.shape[0], CHUNK):
        part = pl.ds(start, CHUNK)
        upstream = params[0] * contract_rows(slope[:, part], text_unit[...])
        image_parts[part, :] = project(image[part, :], upstream).astype(bf16)


def like(array, dtype):
    return jax.ShapeDtypeStruct(array.shape, dtype)


def score_call(params, base, image, text, labels):
    return pl.pallas_call(
        score_kernel,
        out_shape=(
            like(text, f32),
            like(text, bf16),
            jax.ShapeDtypeStruct((text.shape[0], image.shape[0]), bf16),
            jax.ShapeDtypeStruct((1, CHUNK), f32),
        ),
        in_specs=[SMEM, SMEM, VMEM, VMEM, VMEM],
        out_specs=(VMEM, VMEM, VMEM, VMEM),
        compiler_params=pltpu.CompilerParams(vmem_limit_bytes=24 * 2**20),
        name="score",
    )(params, base, image, text, labels)


def rest_call(params, base, image, text, labels, total, unit, loss):
    return pl.pallas_call(
        rest_kernel,
        out_shape=(
            like(text, bf16),
            jax.ShapeDtypeStruct((text.shape[0], image.shape[0]), bf16),
            like(loss, f32),
        ),
        in_specs=[SMEM, SMEM, VMEM, VMEM, VMEM, VMEM, VMEM, VMEM],
        out_specs=(VMEM, VMEM, VMEM),
        compiler_params=pltpu.CompilerParams(vmem_limit_bytes=24 * 2**20),
        name="score_rest",
    )(params, base, image, text, labels, total, unit, loss)


def weight_kernel(hidden, place, own, other, acts, back, blocks):
    y, c = place[0], place[1]
    rows, width = back.shape[-2:]
    loss = jnp.zeros((1, 128), f32)
    for d in range(4):
        at = lax.rem(y - d + 4, 4)
        for k in range(2):
            back[at, k, c] = own[d, k, :rows]
            back[at, k, 1 - c] = other[d, k, :rows]
            for part in (own, other):
                loss = loss + part[d, k, rows:].astype(f32)[:1, :128]
    total = jnp.sum(loss, axis=1, keepdims=True)
    high = total.astype(bf16).astype(f32)
    product = contract_rows(back[...].reshape(-1, width), acts[...])
    count, height = blocks.shape[:2]
    row = lax.broadcasted_iota(jnp.int32, (height, blocks.shape[2]), 0)
    lane = lax.broadcasted_iota(jnp.int32, (height, blocks.shape[2]), 1)
    first = jnp.where(lane == hidden, high, jnp.where(lane == hidden + 1, total - high, 0.0))
    first = jnp.where(row == 0, first, 0.0)
    for k in range(count):
        blocks[k] = (product[k * height : (k + 1) * height] + first).astype(bf16)


def weight_call(place, own, other, acts, rows, hidden):
    width = own.shape[-1]
    return pl.pallas_call(
        functools.partial(weight_kernel, hidden),
        out_shape=(
            jax.ShapeDtypeStruct((4, 2, 2, rows, width), bf16),
            jax.ShapeDtypeStruct((16, width // 16, acts.shape[1]), bf16),
        ),
        in_specs=[SMEM, VMEM, VMEM, VMEM],
        out_specs=(VMEM, VMEM),
        compiler_params=pltpu.CompilerParams(vmem_limit_bytes=24 * 2**20),
        name="image_weight",
    )(place, own, other, acts)


def text_weight_kernel(place, back, acts, mine, theirs):
    product = contract_rows(back[...], acts[...])
    height = mine.shape[2]
    for k in range(8):
        left = product[2 * k * height : (2 * k + 1) * height]
        right = product[(2 * k + 1) * height : (2 * k + 2) * height]
        mine[k // 2, k % 2] = jnp.where(place[1] == 0, left, right).astype(bf16)
        theirs[k // 2, k % 2] = jnp.where(place[1] == 0, right, left).astype(bf16)


def text_weight_call(place, back, acts):
    shape = jax.ShapeDtypeStruct((4, 2, back.shape[1] // 16, acts.shape[1]), bf16)
    return pl.pallas_call(
        text_weight_kernel,
        out_shape=(shape, shape),
        in_specs=[SMEM, VMEM, VMEM],
        out_specs=(VMEM, VMEM),
        compiler_params=pltpu.CompilerParams(vmem_limit_bytes=24 * 2**20),
        name="text_weight",
    )(place, back, acts)


def image_call(params, slope, text_unit, image):
    return pl.pallas_call(
        image_kernel,
        out_shape=jax.ShapeDtypeStruct(image.shape, bf16),
        in_specs=[SMEM, VMEM, VMEM, VMEM],
        out_specs=VMEM,
        compiler_params=pltpu.CompilerParams(vmem_limit_bytes=16 * 2**20),
        name="image_direction",
    )(params, slope, text_unit, image)


def after(value, done):
    return lax.optimization_barrier((value, done))[0]


def on_device(
    image_hidden,
    image_acts,
    image_proj,
    text_hidden,
    text_acts,
    text_proj,
    positives,
    log_scale,
    bias,
):
    z, xl, y, xh, c = [lax.axis_index(name) for name in AXES]
    x = xh * 2 + xl
    rows, width = image_hidden.shape
    hidden = text_proj.shape[0]
    total_rows = rows * 256
    scale = jnp.exp(log_scale[0])

    text_parts = dot(text_acts, text_proj).astype(bf16).reshape(16, rows, width)
    text_sum = scatter_sum(text_parts, IMG)
    text_embed = (text_hidden.astype(f32) + text_sum).astype(bf16)

    image_acts = after(image_acts, text_parts)
    parts = dot(image_acts, image_proj).astype(bf16).reshape(4, 2, 2, rows, width)
    parts = (pick(parts, c, 2).astype(f32) + swap(pick(parts, 1 - c, 2), "c").astype(f32)).astype(bf16)
    total = pick(parts, y).astype(f32)
    for d in (1, 2, 3):
        total = total + shift(pick(parts, (y + d) % 4), "y", d).astype(f32)
    total = total.astype(bf16)
    image_sum = pick(total, xh).astype(f32) + swap(pick(total, 1 - xh), "xh").astype(f32)
    image_embed = (image_hidden.astype(f32) + image_sum).astype(bf16)

    own_block = plane_gather(image_embed, text_embed).reshape(-1, width)
    text_block = gather(text_embed, "z").reshape(-1, width)
    near_block = swap(after(own_block, text_block), "c")

    positives_near = swap(positives, "xl")

    labels = pair(positives, positives_near, xl).reshape(2, 4, 2, 2, rows)
    order = []
    for k in range(2):
        core = c if k == 0 else 1 - c
        for e in range(4):
            for d in range(4):
                dx = jnp.where(core == 0, d, e)
                dy = jnp.where(core == 0, e, d)
                sx = (x - dx) % 4
                order.append((((sx % 2) * 4 + (y - dy) % 4) * 2 + sx // 2) * 2 + core)
    labels = jnp.take(labels.reshape(32, rows), jnp.stack(order), axis=0).reshape(1, -1)
    base = jnp.reshape(((y * 2 + xh) * 2 + c) * 512 + xl * rows, (1,)).astype(jnp.int32)
    params = jnp.stack([scale, bias[0]])
    half = 16 * rows
    text_total, text_unit, own_slope, losses = score_call(
        params, base, own_block, text_block, labels[:, :half]
    )
    text_parts, near_slope, losses = rest_call(
        params, base, near_block, text_block, labels[:, half:], text_total, text_unit, losses
    )
    text_grad = scatter_sum(text_parts.reshape(8, rows, width), "z").astype(bf16)

    theirs = swap(image_call(params, near_slope, text_unit, near_block), "c")
    mine = image_call(params, own_slope, text_unit, after(own_block, text_parts))
    halves = jnp.pad(two_halves(jnp.sum(losses))[None], ((0, 7), (0, width - 2)))
    slab = (mine.astype(f32) + theirs.astype(f32)).astype(bf16)
    image_grad = plane_sum(slab.reshape(4, 4, rows, width))
    image_grad = image_grad.astype(bf16)

    near = jnp.concatenate([image_grad, halves])
    near = pair(near, swap(near, "xh"), xh)
    ring = jnp.stack([near] + [shift(near, "y", d) for d in (1, 2, 3)])
    place = jnp.stack([y, c]).astype(jnp.int32)
    wide = ((0, 0), (0, 384 - hidden))
    image_back, blocks = weight_call(place, ring, swap(ring, "c"), jnp.pad(image_acts, wide), rows, hidden)
    image_back = image_back.reshape(-1, width)
    found = exchange(blocks, IMG)

    text_back = gather(after(text_grad, image_grad), IMG).reshape(-1, width)
    text_back = after(text_back, blocks)
    mine, theirs = text_weight_call(place, text_back, jnp.pad(text_acts, wide))
    parts = (mine.astype(f32) + swap(theirs, "c").astype(f32)).astype(bf16)
    total = pick(parts, y).astype(f32)
    for d in (1, 2, 3):
        total = total + shift(pick(parts, (y + d) % 4), "y", d).astype(f32)
    total = total.astype(bf16)
    text_proj_grad = pick(total, xh).astype(f32) + swap(pick(total, 1 - xh), "xh").astype(f32)
    text_proj_grad = text_proj_grad[:, :hidden].T

    image_act_grad = contract_cols(after(image_back, parts), image_proj).astype(bf16)
    text_act_grad = contract_cols(after(text_back, parts), text_proj).astype(bf16)

    found = after(found, total).astype(f32)
    image_proj_grad = jnp.sum(found, axis=0)[:, :hidden].T
    total_loss = jnp.sum(found[:, 0, hidden : hidden + 2])
    loss = jnp.reshape(total_loss / total_rows, (1,))
    return (
        loss,
        image_grad,
        text_grad,
        image_act_grad,
        text_act_grad,
        image_proj_grad,
        text_proj_grad,
    )


def solution(mesh):
    fine = Mesh(mesh.devices.reshape(SIZES), AXES)
    return jax.shard_map(
        on_device,
        mesh=fine,
        in_specs=(
            P(IMG + TXT, None),
            P(IMG, TXT),
            P(TXT, None),
            P(TXT + IMG, None),
            P(TXT, IMG),
            P(IMG, None),
            P(IMG),
            P(),
            P(),
        ),
        out_specs=(
            P(),
            P(IMG + TXT, None),
            P(TXT + IMG, None),
            P(IMG, TXT),
            P(TXT, IMG),
            P(TXT, IMG),
            P(IMG, TXT),
        ),
        check_vma=False,
    )
```

profile of v0, /device:TPU:1, one launch (start us, length us, event | category | flops | bytes accessed | tf_op | source)
XLA Modules:
  0.0 189.9 jit_solution(4742824476783819268)
XLA Ops:
  0.6 3.1 %convolution_convert_fusion.1 = bf16[512,1152]{1,0:T(8,128)(2,1)} fusion(bf16[512,269]{0,1:T(8,128)(2,1)} %param.13, bf16[269,1152]{1,0:T(8,128)(2,1)} %param.14), kind=kOutput, calls=%fused_computation.2 | convolution fusion | flops 317915136 | bytes 2074880 | tf_op jit(solution)/shard_map/dot_general | solution.py:32
  3.8 10.2 %all-to-all-start = ((bf16[16,32,1152]{2,1,0:T(8,128)(2,1)}), bf16[16,32,1152]{2,1,0:T(8,128)(2,1)S(1)}, u32[]{:S(2)}, u32[]{:S(2)}) async-start(bf16[16,32,1152]{2,1,0:T(8,128)(2,1)} %bitcast.3), calls=%async_computation | async-start | bytes 2359296 | tf_op jit(solution)/shard_map/all_to_all | solution.py:93
  14.0 1.9 convolution_convert_fusion
  18.0 1.6 collective-permute-done
  19.7 1.2 fusion
  21.0 2.8 %collective-permute-start.3 = (bf16[2,32,1152]{2,1,0:T(8,128)(2,1)S(1)}, bf16[2,32,1152]{2,1,0:T(8,128)(2,1)S(1)}, u32[]{:S(2)}, u32[]{:S(2)}) collective-permute-start(bf16[2,32,1152]{2,1,0:T(8,128)(2,1)S(1)} %get-tuple-element.52), channel_id=1, source_target_pairs={{0,12},{4,0},{8,4},{12,8},{1,13},{5,1},{9,5},{13,9},{2,14},{6,2},{... | collective-permute-start | bytes 442376 | tf_op jit(solution)/shard_map/ppermute | solution.py:56
  24.8 4.8 %collective-permute-done.3 = bf16[2,32,1152]{2,1,0:T(8,128)(2,1)S(1)} collective-permute-done((bf16[2,32,1152]{2,1,0:T(8,128)(2,1)S(1)}, bf16[2,32,1152]{2,1,0:T(8,128)(2,1)S(1)}, u32[]{:S(2)}, u32[]{:S(2)}) %collective-permute-start.3) | collective-permute-done | bytes 147488 | tf_op jit(solution)/shard_map/ppermute | solution.py:56
  30.1 4.1 %collective-permute-done.1 = bf16[2,32,1152]{2,1,0:T(8,128)(2,1)S(1)} collective-permute-done((bf16[2,32,1152]{2,1,0:T(8,128)(2,1)S(1)}, bf16[2,32,1152]{2,1,0:T(8,128)(2,1)S(1)}, u32[]{:S(2)}, u32[]{:S(2)}) %collective-permute-start.1) | collective-permute-done | bytes 147488 | tf_op jit(solution)/shard_map/ppermute | solution.py:56
  34.3 2.5 %collective-permute-start.4 = (bf16[32,1152]{1,0:T(8,128)(2,1)S(1)}, bf16[32,1152]{1,0:T(8,128)(2,1)S(1)}, u32[]{:S(2)}, u32[]{:S(2)}) collective-permute-start(bf16[32,1152]{1,0:T(8,128)(2,1)S(1)} %dynamic-slice_bitcast_fusion.7), channel_id=1, source_target_pairs={{0,2},{2,0},{1,3},{3,1},{4,6},{6,4},{5,7},{7,5},{8,10},{10,8},{9,1... | collective-permute-start | bytes 221192 | tf_op jit(solution)/shard_map/ppermute | solution.py:48
  36.9 4.7 %all-to-all-done = bf16[16,32,1152]{2,1,0:T(8,128)(2,1)S(1)} async-done(((bf16[16,32,1152]{2,1,0:T(8,128)(2,1)}), bf16[16,32,1152]{2,1,0:T(8,128)(2,1)S(1)}, u32[]{:S(2)}, u32[]{:S(2)}) %all-to-all-start) | async-done | bytes 1179680 | tf_op jit(solution)/shard_map/all_to_all | solution.py:93
  42.6 6.9 %all-to-all-start.1 = ((bf16[8,32,1152]{2,1,0:T(8,128)(2,1)}), bf16[8,32,1152]{2,1,0:T(8,128)(2,1)S(1)}, u32[]{:S(2)}, u32[]{:S(2)}) async-start(bf16[8,32,1152]{2,1,0:T(8,128)(2,1)} %broadcast_in_dim.14), calls=%async_computation.1 | async-start | bytes 1179648 | tf_op jit(solution)/shard_map/all_to_all | solution.py:93
  49.6 2.8 %collective-permute-start.7 = (bf16[32,1152]{1,0:T(8,128)(2,1)S(1)}, bf16[32,1152]{1,0:T(8,128)(2,1)S(1)}, u32[]{:S(2)}, u32[]{:S(2)}) collective-permute-start(bf16[32,1152]{1,0:T(8,128)(2,1)S(1)} %fusion.14), channel_id=1, source_target_pairs={{0,18},{1,13},{4,22},{5,1},{8,26},{9,5},{12,30},{13,9},{16,0},{17,... | collective-permute-start | bytes 221192 | tf_op jit(solution)/shard_map/ppermute | solution.py:72
  53.8 3.4 %collective-permute-done.6 = bf16[32,1152]{1,0:T(8,128)(2,1)S(1)} collective-permute-done((bf16[32,1152]{1,0:T(8,128)(2,1)S(1)}, bf16[32,1152]{1,0:T(8,128)(2,1)S(1)}, u32[]{:S(2)}, u32[]{:S(2)}) %collective-permute-start.6) | collective-permute-done | bytes 73760 | tf_op jit(solution)/shard_map/ppermute | solution.py:72
  58.3 1.6 collective-permute-start.10
  65.1 1.6 collective-permute-done.10
  67.3 3.2 %collective-permute-done.8 = bf16[4,32,1152]{2,1,0:T(8,128)(2,1)} collective-permute-done((bf16[4,32,1152]{2,1,0:T(8,128)(2,1)S(1)}, bf16[4,32,1152]{2,1,0:T(8,128)(2,1)}, u32[]{:S(2)}, u32[]{:S(2)}) %collective-permute-start.8) | collective-permute-done | bytes 294944 | tf_op jit(solution)/shard_map/ppermute | solution.py:72
  70.5 1.1 pad_maximum_fusion
  71.7 4.0 %collective-permute-start.12 = (bf16[512,1152]{1,0:T(8,128)(2,1)S(1)}, bf16[512,1152]{1,0:T(8,128)(2,1)}, u32[]{:S(2)}, u32[]{:S(2)}) collective-permute-start(bf16[512,1152]{1,0:T(8,128)(2,1)S(1)} %bitcast.161), channel_id=1, source_target_pairs={{0,1},{1,0},{2,3},{3,2},{4,5},{5,4},{6,7},{7,6},{8,9},{9,8},{10,11... | collective-permute-start | bytes 3538952 | tf_op jit(solution)/shard_map/ppermute | solution.py:48
  76.7 2.2 %score.1 = (f32[256,1152]{1,0:T(8,128)S(1)}, bf16[256,1152]{1,0:T(8,128)(2,1)S(1)}, bf16[256,512]{1,0:T(8,128)(2,1)S(1)}, f32[1,256]{1,0:T(1,128)S(1)}) custom-call(f32[2]{0:T(128)S(1)} %pad_maximum_fusion.4.params, s32[1]{0:T(128)} %bitcast.2.base, bf16[512,1152]{1,0:T(8,128)(2,1)S(1)} %bitcast.162, bf16[256,1152]{1,0:T(8,128)(2,1)S(1)} %bitcast.164, ...), custom_call_target="tpu_custom_call" | custom-call | tf_op jit(solution)/shard_map/score/pallas_call | solution.py:162
  78.9 4.5 %score_rest.1 = (bf16[256,1152]{1,0:T(8,128)(2,1)}, bf16[256,512]{1,0:T(8,128)(2,1)S(1)}, f32[1,256]{1,0:T(1,128)S(1)}) custom-call(f32[2]{0:T(128)S(1)} %pad_maximum_fusion.4.params, s32[1]{0:T(128)} %bitcast.2.base, bf16[512,1152]{1,0:T(8,128)(2,1)} %collective-permute-done.12.image, bf16[256,1152]{1,0:T(8,128)(2,1)S(1)} %bitcast.165, ...), custom_call_target="tpu_custom_call" | custom-call | tf_op jit(solution)/shard_map/score_rest/pallas_call | solution.py:178
  83.3 2.4 %image_direction.3 = bf16[512,1152]{1,0:T(8,128)(2,1)S(1)} custom-call(f32[2]{0:T(128)S(1)} %pad_maximum_fusion.4.params, bf16[256,512]{1,0:T(8,128)(2,1)S(1)} %get-tuple-element.36.slope, bf16[256,1152]{1,0:T(8,128)(2,1)S(1)} %get-tuple-element.30.unit.text_unit, bf16[512,1152]{1,0:T(8,128)(2,1)} %collective-permute-done.12.image), custom_call_target="tpu_custom_call" | custom-call | tf_op jit(solution)/shard_map/image_direction/pallas_call | solution.py:253
  85.8 1.6 image_direction.2
  87.5 1.2 collective-permute-done.13
  89.1 1.5 collective-permute-start.15
  90.6 1.6 collective-permute-start.14
  92.1 6.8 %all-to-all-start.3 = ((bf16[8,32,1152]{2,1,0:T(8,128)(2,1)}), bf16[8,32,1152]{2,1,0:T(8,128)(2,1)S(1)}, u32[]{:S(2)}, u32[]{:S(2)}) async-start(bf16[8,32,1152]{2,1,0:T(8,128)(2,1)} %bitcast.107), calls=%async_computation.3 | async-start | bytes 1179648 | tf_op jit(solution)/shard_map/all_to_all | solution.py:93
  100.1 1.1 fusion.3
  101.5 1.5 collective-permute-start.18
  103.0 1.2 collective-permute-start.17
  104.2 14.1 %all-to-all-done.3 = bf16[8,32,1152]{2,1,0:T(8,128)(2,1)S(1)} async-done(((bf16[8,32,1152]{2,1,0:T(8,128)(2,1)}), bf16[8,32,1152]{2,1,0:T(8,128)(2,1)S(1)}, u32[]{:S(2)}, u32[]{:S(2)}) %all-to-all-start.3) | async-done | bytes 589856 | tf_op jit(solution)/shard_map/all_to_all | solution.py:93
  119.6 3.7 %all-to-all-start.4 = ((bf16[16,32,1152]{2,1,0:T(8,128)(2,1)}), bf16[16,32,1152]{2,1,0:T(8,128)(2,1)S(1)}, u32[]{:S(2)}, u32[]{:S(2)}) async-start(bf16[16,32,1152]{2,1,0:T(8,128)(2,1)} %broadcast_in_dim.26), calls=%async_computation.4 | async-start | bytes 2359296 | tf_op jit(solution)/shard_map/all_to_all | solution.py:93
  127.2 2.2 %collective-permute-start.20 = (bf16[40,1152]{1,0:T(8,128)(2,1)S(1)}, bf16[40,1152]{1,0:T(8,128)(2,1)S(1)}, u32[]{:S(2)}, u32[]{:S(2)}) collective-permute-start(bf16[40,1152]{1,0:T(8,128)(2,1)S(1)} %get-tuple-element.64), channel_id=1, source_target_pairs={{0,2},{2,0},{1,3},{3,1},{4,6},{6,4},{5,7},{7,5},{8,10},{10,8},{9,1... | collective-permute-start | bytes 276488 | tf_op jit(solution)/shard_map/ppermute | solution.py:48
  129.4 3.1 %collective-permute-done.20 = bf16[40,1152]{1,0:T(8,128)(2,1)S(1)} collective-permute-done((bf16[40,1152]{1,0:T(8,128)(2,1)S(1)}, bf16[40,1152]{1,0:T(8,128)(2,1)S(1)}, u32[]{:S(2)}, u32[]{:S(2)}) %collective-permute-start.20) | collective-permute-done | bytes 92192 | tf_op jit(solution)/shard_map/ppermute | solution.py:48
  133.0 1.1 collective-permute-start.21
  134.2 3.3 %collective-permute-done.23 = bf16[2,40,1152]{2,1,0:T(8,128)(2,1)S(1)} collective-permute-done((bf16[2,40,1152]{2,1,0:T(8,128)(2,1)S(1)}, bf16[2,40,1152]{2,1,0:T(8,128)(2,1)S(1)}, u32[]{:S(2)}, u32[]{:S(2)}) %collective-permute-start.23) | collective-permute-done | bytes 184352 | tf_op jit(solution)/shard_map/ppermute | solution.py:56
  137.4 1.7 collective-permute-done.22
  139.2 5.4 %collective-permute-done.21 = bf16[2,40,1152]{2,1,0:T(8,128)(2,1)S(1)} collective-permute-done((bf16[2,40,1152]{2,1,0:T(8,128)(2,1)S(1)}, bf16[2,40,1152]{2,1,0:T(8,128)(2,1)S(1)}, u32[]{:S(2)}, u32[]{:S(2)}) %collective-permute-start.21) | collective-permute-done | bytes 184352 | tf_op jit(solution)/shard_map/ppermute | solution.py:56
  145.7 1.9 %copy.17 = bf16[512,269]{1,0:T(8,128)(2,1)} copy(bf16[512,269]{0,1:T(8,128)(2,1)} %param.10) | data formatting | bytes 550912 | tf_op jit(solution)/shard_map/optimization_barrier | solution.py:264
  148.7 2.4 %image_weight.1 = (bf16[4,2,2,32,1152]{4,3,2,1,0:T(8,128)(2,1)S(1)}, bf16[16,72,384]{2,1,0:T(8,128)(2,1)}) custom-call(s32[2]{0:T(128)S(1)} %pad_add_fusion.place, bf16[4,2,40,1152]{3,2,1,0:T(8,128)(2,1)S(1)} %pad_maximum_fusion.1.own, bf16[4,2,40,1152]{3,2,1,0:T(8,128)(2,1)S(1)} %collective-permute-done.24.other, bf16[512,384]{1,0:T(8,128)(2,1)S(1)} %pad.12.acts), custom_call_target="tpu_custom_call" | custom-call | tf_op jit(solution)/shard_map/image_weight/pallas_call | solution.py:217
  152.1 7.6 %all-to-all-start.2 = ((bf16[16,72,384]{2,1,0:T(8,128)(2,1)}), bf16[16,72,384]{2,1,0:T(8,128)(2,1)S(1)}, u32[]{:S(2)}, u32[]{:S(2)}) async-start(bf16[16,72,384]{2,1,0:T(8,128)(2,1)} %get-tuple-element.38), calls=%async_computation.2 | async-start | bytes 1769472 | tf_op jit(solution)/shard_map/all_to_all | solution.py:93
  160.0 1.3 text_weight.1
  161.7 1.5 collective-permute-done.25
  164.9 1.3 convolution_convert_fusion.3
  166.2 1.3 convolution_convert_fusion.2
  167.8 1.7 collective-permute-done.27
  169.6 3.3 %collective-permute-done.26 = bf16[2,72,384]{2,1,0:T(8,128)(2,1)S(1)} collective-permute-done((bf16[2,72,384]{2,1,0:T(8,128)(2,1)S(1)}, bf16[2,72,384]{2,1,0:T(8,128)(2,1)S(1)}, u32[]{:S(2)}, u32[]{:S(2)}) %collective-permute-start.26) | collective-permute-done | bytes 110624 | tf_op jit(solution)/shard_map/ppermute | solution.py:56
  173.0 9.7 %all-to-all-done.2 = bf16[16,72,384]{2,1,0:T(8,128)(2,1)S(1)} async-done(((bf16[16,72,384]{2,1,0:T(8,128)(2,1)}), bf16[16,72,384]{2,1,0:T(8,128)(2,1)S(1)}, u32[]{:S(2)}, u32[]{:S(2)}) %all-to-all-start.2) | async-done | bytes 884768 | tf_op jit(solution)/shard_map/all_to_all | solution.py:93
  183.6 2.1 %collective-permute-start.29 = (bf16[72,384]{1,0:T(8,128)(2,1)S(1)}, bf16[72,384]{1,0:T(8,128)(2,1)S(1)}, u32[]{:S(2)}, u32[]{:S(2)}) collective-permute-start(bf16[72,384]{1,0:T(8,128)(2,1)S(1)} %get-tuple-element.60), channel_id=1, source_target_pairs={{0,2},{2,0},{1,3},{3,1},{4,6},{6,4},{5,7},{7,5},{8,10},{10,8},{9,1... | collective-permute-start | bytes 165896 | tf_op jit(solution)/shard_map/ppermute | solution.py:48
  (104 shorter events, 25.5 us)
Async XLA Ops:
  0.6 13.3 %copy-start = (bf16[269,1152]{1,0:T(8,128)(2,1)S(1)}, bf16[269,1152]{1,0:T(8,128)(2,1)}, u32[]{:S(2)}) copy-start(bf16[269,1152]{1,0:T(8,128)(2,1)} %param.11) | copy-start | bytes 1859332
  3.8 10.2 %copy-start.5 = (bf16[512,269]{0,1:T(8,128)(2,1)S(1)}, bf16[512,269]{0,1:T(8,128)(2,1)}, u32[]{:S(2)}) copy-start(bf16[512,269]{0,1:T(8,128)(2,1)} %param.10) | copy-start | bytes 826372
  3.8 37.8 %all-to-all-start = ((bf16[16,32,1152]{2,1,0:T(8,128)(2,1)}), bf16[16,32,1152]{2,1,0:T(8,128)(2,1)S(1)}, u32[]{:S(2)}, u32[]{:S(2)}) async-start(bf16[16,32,1152]{2,1,0:T(8,128)(2,1)} %bitcast.3), calls=%async_computation | async-start | bytes 2359296 | tf_op jit(solution)/shard_map/all_to_all | solution.py:93
  17.0 2.7 %collective-permute-start = (bf16[4,2,32,1152]{3,2,1,0:T(8,128)(2,1)S(1)}, bf16[4,2,32,1152]{3,2,1,0:T(8,128)(2,1)S(1)}, u32[]{:S(2)}, u32[]{:S(2)}) collective-permute-start(bf16[4,2,32,1152]{3,2,1,0:T(8,128)(2,1)S(1)} %dynamic-slice_bitcast_fusion), channel_id=1, source_target_pairs={{0,1},{1,0},{2,3},{3,2},{4,5},{5,4},{6,7},{7,6},{8,9},{9,8},{10,11... | collective-permute-start | bytes 1769480 | tf_op jit(solution)/shard_map/ppermute | solution.py:48
  21.0 20.8 %copy-start.7 = (bf16[32,1152]{1,0:T(8,128)(2,1)S(1)}, bf16[32,1152]{1,0:T(8,128)(2,1)}, u32[]{:S(2)}) copy-start(bf16[32,1152]{1,0:T(8,128)(2,1)} %param.12) | copy-start | bytes 221188
  21.0 8.7 %collective-permute-start.3 = (bf16[2,32,1152]{2,1,0:T(8,128)(2,1)S(1)}, bf16[2,32,1152]{2,1,0:T(8,128)(2,1)S(1)}, u32[]{:S(2)}, u32[]{:S(2)}) collective-permute-start(bf16[2,32,1152]{2,1,0:T(8,128)(2,1)S(1)} %get-tuple-element.52), channel_id=1, source_target_pairs={{0,12},{4,0},{8,4},{12,8},{1,13},{5,1},{9,5},{13,9},{2,14},{6,2},{... | collective-permute-start | bytes 442376 | tf_op jit(solution)/shard_map/ppermute | solution.py:56
  23.8 6.3 %collective-permute-start.2 = (bf16[2,32,1152]{2,1,0:T(8,128)(2,1)S(1)}, bf16[2,32,1152]{2,1,0:T(8,128)(2,1)S(1)}, u32[]{:S(2)}, u32[]{:S(2)}) collective-permute-start(bf16[2,32,1152]{2,1,0:T(8,128)(2,1)S(1)} %get-tuple-element.53), channel_id=1, source_target_pairs={{0,8},{4,12},{8,0},{12,4},{1,9},{5,13},{9,1},{13,5},{2,10},{6,14},... | collective-permute-start | bytes 442376 | tf_op jit(solution)/shard_map/ppermute | solution.py:56
  24.1 10.1 %collective-permute-start.1 = (bf16[2,32,1152]{2,1,0:T(8,128)(2,1)S(1)}, bf16[2,32,1152]{2,1,0:T(8,128)(2,1)S(1)}, u32[]{:S(2)}, u32[]{:S(2)}) collective-permute-start(bf16[2,32,1152]{2,1,0:T(8,128)(2,1)S(1)} %get-tuple-element.51), channel_id=1, source_target_pairs={{0,4},{4,8},{8,12},{12,0},{1,5},{5,9},{9,13},{13,1},{2,6},{6,10},{... | collective-permute-start | bytes 442376 | tf_op jit(solution)/shard_map/ppermute | solution.py:56
  34.3 15.2 %collective-permute-start.4 = (bf16[32,1152]{1,0:T(8,128)(2,1)S(1)}, bf16[32,1152]{1,0:T(8,128)(2,1)S(1)}, u32[]{:S(2)}, u32[]{:S(2)}) collective-permute-start(bf16[32,1152]{1,0:T(8,128)(2,1)S(1)} %dynamic-slice_bitcast_fusion.7), channel_id=1, source_target_pairs={{0,2},{2,0},{1,3},{3,1},{4,6},{6,4},{5,7},{7,5},{8,10},{10,8},{9,1... | collective-permute-start | bytes 221192 | tf_op jit(solution)/shard_map/ppermute | solution.py:48
  41.7 7.8 %copy-start.8 = (bf16[32,1152]{1,0:T(8,128)(2,1)S(1)}, bf16[32,1152]{1,0:T(8,128)(2,1)}, u32[]{:S(2)}) copy-start(bf16[32,1152]{1,0:T(8,128)(2,1)} %param.9) | copy-start | bytes 221188
  42.6 19.0 %copy-start.9 = (s32[512]{0:T(512)S(1)}, s32[512]{0:T(512)}, u32[]{:S(2)}) copy-start(s32[512]{0:T(512)} %param.15) | copy-start | bytes 6148
  42.6 29.0 %all-to-all-start.1 = ((bf16[8,32,1152]{2,1,0:T(8,128)(2,1)}), bf16[8,32,1152]{2,1,0:T(8,128)(2,1)S(1)}, u32[]{:S(2)}, u32[]{:S(2)}) async-start(bf16[8,32,1152]{2,1,0:T(8,128)(2,1)} %broadcast_in_dim.14), calls=%async_computation.1 | async-start | bytes 1179648 | tf_op jit(solution)/shard_map/all_to_all | solution.py:93
  49.6 4.2 %collective-permute-start.7 = (bf16[32,1152]{1,0:T(8,128)(2,1)S(1)}, bf16[32,1152]{1,0:T(8,128)(2,1)S(1)}, u32[]{:S(2)}, u32[]{:S(2)}) collective-permute-start(bf16[32,1152]{1,0:T(8,128)(2,1)S(1)} %fusion.14), channel_id=1, source_target_pairs={{0,18},{1,13},{4,22},{5,1},{8,26},{9,5},{12,30},{13,9},{16,0},{17,... | collective-permute-start | bytes 221192 | tf_op jit(solution)/shard_map/ppermute | solution.py:72
  52.4 4.8 %collective-permute-start.6 = (bf16[32,1152]{1,0:T(8,128)(2,1)S(1)}, bf16[32,1152]{1,0:T(8,128)(2,1)S(1)}, u32[]{:S(2)}, u32[]{:S(2)}) collective-permute-start(bf16[32,1152]{1,0:T(8,128)(2,1)S(1)} %fusion.14), channel_id=1, source_target_pairs={{0,2},{1,9},{4,6},{5,13},{8,10},{9,1},{12,14},{13,5},{16,18},{17,2... | collective-permute-start | bytes 221192 | tf_op jit(solution)/shard_map/ppermute | solution.py:72
  52.8 5.4 %collective-permute-start.5 = (bf16[32,1152]{1,0:T(8,128)(2,1)S(1)}, bf16[32,1152]{1,0:T(8,128)(2,1)S(1)}, u32[]{:S(2)}, u32[]{:S(2)}) collective-permute-start(bf16[32,1152]{1,0:T(8,128)(2,1)S(1)} %fusion.14), channel_id=1, source_target_pairs={{0,16},{1,5},{4,20},{5,9},{8,24},{9,13},{12,28},{13,1},{16,2},{17,... | collective-permute-start | bytes 221192 | tf_op jit(solution)/shard_map/ppermute | solution.py:72
  58.3 8.5 %collective-permute-start.10 = (bf16[4,32,1152]{2,1,0:T(8,128)(2,1)S(1)}, bf16[4,32,1152]{2,1,0:T(8,128)(2,1)S(1)}, u32[]{:S(2)}, u32[]{:S(2)}) collective-permute-start(bf16[4,32,1152]{2,1,0:T(8,128)(2,1)S(1)} %pad_maximum_fusion.2), channel_id=1, source_target_pairs={{0,12},{1,19},{4,0},{5,23},{8,4},{9,27},{12,8},{13,31},{16,28},{17... | collective-permute-start | bytes 884744 | tf_op jit(solution)/shard_map/ppermute | solution.py:72
  59.9 7.4 %collective-permute-start.9 = (bf16[4,32,1152]{2,1,0:T(8,128)(2,1)S(1)}, bf16[4,32,1152]{2,1,0:T(8,128)(2,1)S(1)}, u32[]{:S(2)}, u32[]{:S(2)}) collective-permute-start(bf16[4,32,1152]{2,1,0:T(8,128)(2,1)S(1)} %pad_maximum_fusion.2), channel_id=1, source_target_pairs={{0,8},{1,3},{4,12},{5,7},{8,0},{9,11},{12,4},{13,15},{16,24},{17,1... | collective-permute-start | bytes 884744 | tf_op jit(solution)/shard_map/ppermute | solution.py:72
  60.9 9.6 %collective-permute-start.8 = (bf16[4,32,1152]{2,1,0:T(8,128)(2,1)S(1)}, bf16[4,32,1152]{2,1,0:T(8,128)(2,1)}, u32[]{:S(2)}, u32[]{:S(2)}) collective-permute-start(bf16[4,32,1152]{2,1,0:T(8,128)(2,1)S(1)} %pad_maximum_fusion.2), channel_id=1, source_target_pairs={{0,4},{1,17},{4,8},{5,21},{8,12},{9,25},{12,0},{13,29},{16,20},{17... | collective-permute-start | bytes 884744 | tf_op jit(solution)/shard_map/ppermute | solution.py:72
  61.6 14.2 %collective-permute-start.11 = (s32[512]{0:T(512)S(1)}, s32[512]{0:T(512)S(1)}, u32[]{:S(2)}, u32[]{:S(2)}) collective-permute-start(s32[512]{0:T(512)S(1)} %copy-done.9), channel_id=1, source_target_pairs={{0,16},{16,0},{1,17},{17,1},{2,18},{18,2},{3,19},{19,3},{4,20},{20... | collective-permute-start | bytes 6152 | tf_op jit(solution)/shard_map/ppermute | solution.py:48
  71.7 7.2 %collective-permute-start.12 = (bf16[512,1152]{1,0:T(8,128)(2,1)S(1)}, bf16[512,1152]{1,0:T(8,128)(2,1)}, u32[]{:S(2)}, u32[]{:S(2)}) collective-permute-start(bf16[512,1152]{1,0:T(8,128)(2,1)S(1)} %bitcast.161), channel_id=1, source_target_pairs={{0,1},{1,0},{2,3},{3,2},{4,5},{5,4},{6,7},{7,6},{8,9},{9,8},{10,11... | collective-permute-start | bytes 3538952 | tf_op jit(solution)/shard_map/ppermute | solution.py:48
  85.7 2.9 %collective-permute-start.13 = (bf16[512,1152]{1,0:T(8,128)(2,1)S(1)}, bf16[512,1152]{1,0:T(8,128)(2,1)S(1)}, u32[]{:S(2)}, u32[]{:S(2)}) collective-permute-start(bf16[512,1152]{1,0:T(8,128)(2,1)S(1)} %image_direction.3), channel_id=1, source_target_pairs={{0,1},{1,0},{2,3},{3,2},{4,5},{5,4},{6,7},{7,6},{8,9},{9,8},{10,11... | collective-permute-start | bytes 3538952 | tf_op jit(solution)/shard_map/ppermute | solution.py:48
  89.0 10.3 %collective-permute-start.16 = (bf16[4,32,1152]{2,1,0:T(8,128)(2,1)S(1)}, bf16[4,32,1152]{2,1,0:T(8,128)(2,1)S(1)}, u32[]{:S(2)}, u32[]{:S(2)}) collective-permute-start(bf16[4,32,1152]{2,1,0:T(8,128)(2,1)S(1)} %bitcast.179), channel_id=1, source_target_pairs={{0,4},{1,17},{4,8},{5,21},{8,12},{9,25},{12,0},{13,29},{16,20},{17... | collective-permute-start | bytes 884744 | tf_op jit(solution)/shard_map/ppermute | solution.py:72
  89.1 10.2 %collective-permute-start.15 = (bf16[4,32,1152]{2,1,0:T(8,128)(2,1)S(1)}, bf16[4,32,1152]{2,1,0:T(8,128)(2,1)S(1)}, u32[]{:S(2)}, u32[]{:S(2)}) collective-permute-start(bf16[4,32,1152]{2,1,0:T(8,128)(2,1)S(1)} %bitcast.178), channel_id=1, source_target_pairs={{0,8},{1,3},{4,12},{5,7},{8,0},{9,11},{12,4},{13,15},{16,24},{17,1... | collective-permute-start | bytes 884744 | tf_op jit(solution)/shard_map/ppermute | solution.py:72
  90.6 9.5 %collective-permute-start.14 = (bf16[4,32,1152]{2,1,0:T(8,128)(2,1)S(1)}, bf16[4,32,1152]{2,1,0:T(8,128)(2,1)}, u32[]{:S(2)}, u32[]{:S(2)}) collective-permute-start(bf16[4,32,1152]{2,1,0:T(8,128)(2,1)S(1)} %bitcast.177), channel_id=1, source_target_pairs={{0,12},{1,19},{4,0},{5,23},{8,4},{9,27},{12,8},{13,31},{16,28},{17... | collective-permute-start | bytes 884744 | tf_op jit(solution)/shard_map/ppermute | solution.py:72
  92.1 26.2 %all-to-all-start.3 = ((bf16[8,32,1152]{2,1,0:T(8,128)(2,1)}), bf16[8,32,1152]{2,1,0:T(8,128)(2,1)S(1)}, u32[]{:S(2)}, u32[]{:S(2)}) async-start(bf16[8,32,1152]{2,1,0:T(8,128)(2,1)} %bitcast.107), calls=%async_computation.3 | async-start | bytes 1179648 | tf_op jit(solution)/shard_map/all_to_all | solution.py:93
  101.2 17.2 %collective-permute-start.19 = (bf16[32,1152]{1,0:T(8,128)(2,1)S(1)}, bf16[32,1152]{1,0:T(8,128)(2,1)S(1)}, u32[]{:S(2)}, u32[]{:S(2)}) collective-permute-start(bf16[32,1152]{1,0:T(8,128)(2,1)S(1)} %get-tuple-element.58), channel_id=1, source_target_pairs={{0,16},{1,5},{4,20},{5,9},{8,24},{9,13},{12,28},{13,1},{16,2},{17,... | collective-permute-start | bytes 221192 | tf_op jit(solution)/shard_map/ppermute | solution.py:72
  101.5 16.9 %collective-permute-start.18 = (bf16[32,1152]{1,0:T(8,128)(2,1)S(1)}, bf16[32,1152]{1,0:T(8,128)(2,1)S(1)}, u32[]{:S(2)}, u32[]{:S(2)}) collective-permute-start(bf16[32,1152]{1,0:T(8,128)(2,1)S(1)} %get-tuple-element.59), channel_id=1, source_target_pairs={{0,2},{1,9},{4,6},{5,13},{8,10},{9,1},{12,14},{13,5},{16,18},{17,2... | collective-permute-start | bytes 221192 | tf_op jit(solution)/shard_map/ppermute | solution.py:72
  103.0 15.4 %collective-permute-start.17 = (bf16[32,1152]{1,0:T(8,128)(2,1)S(1)}, bf16[32,1152]{1,0:T(8,128)(2,1)S(1)}, u32[]{:S(2)}, u32[]{:S(2)}) collective-permute-start(bf16[32,1152]{1,0:T(8,128)(2,1)S(1)} %get-tuple-element.57), channel_id=1, source_target_pairs={{0,18},{1,13},{4,22},{5,1},{8,26},{9,5},{12,30},{13,9},{16,0},{17,... | collective-permute-start | bytes 221192 | tf_op jit(solution)/shard_map/ppermute | solution.py:72
  118.4 1.2 copy-start.3
  118.5 8.6 %copy-start.4 = (bf16[32,1152]{1,0:T(8,128)(2,1)}, bf16[32,1152]{1,0:T(8,128)(2,1)S(1)}, u32[]{:S(2)}) copy-start(bf16[32,1152]{1,0:T(8,128)(2,1)S(1)} %fusion.12) | copy-start | bytes 221188
  119.6 32.4 %all-to-all-start.4 = ((bf16[16,32,1152]{2,1,0:T(8,128)(2,1)}), bf16[16,32,1152]{2,1,0:T(8,128)(2,1)S(1)}, u32[]{:S(2)}, u32[]{:S(2)}) async-start(bf16[16,32,1152]{2,1,0:T(8,128)(2,1)} %broadcast_in_dim.26), calls=%async_computation.4 | async-start | bytes 2359296 | tf_op jit(solution)/shard_map/all_to_all | solution.py:93
  127.2 5.3 %collective-permute-start.20 = (bf16[40,1152]{1,0:T(8,128)(2,1)S(1)}, bf16[40,1152]{1,0:T(8,128)(2,1)S(1)}, u32[]{:S(2)}, u32[]{:S(2)}) collective-permute-start(bf16[40,1152]{1,0:T(8,128)(2,1)S(1)} %get-tuple-element.64), channel_id=1, source_target_pairs={{0,2},{2,0},{1,3},{3,1},{4,6},{6,4},{5,7},{7,5},{8,10},{10,8},{9,1... | collective-permute-start | bytes 276488 | tf_op jit(solution)/shard_map/ppermute | solution.py:48
  132.6 4.9 %collective-permute-start.23 = (bf16[2,40,1152]{2,1,0:T(8,128)(2,1)S(1)}, bf16[2,40,1152]{2,1,0:T(8,128)(2,1)S(1)}, u32[]{:S(2)}, u32[]{:S(2)}) collective-permute-start(bf16[2,40,1152]{2,1,0:T(8,128)(2,1)S(1)} %maximum_select_fusion.1), channel_id=1, source_target_pairs={{0,12},{4,0},{8,4},{12,8},{1,13},{5,1},{9,5},{13,9},{2,14},{6,2},{... | collective-permute-start | bytes 552968 | tf_op jit(solution)/shard_map/ppermute | solution.py:56
  133.0 6.2 %collective-permute-start.22 = (bf16[2,40,1152]{2,1,0:T(8,128)(2,1)S(1)}, bf16[2,40,1152]{2,1,0:T(8,128)(2,1)S(1)}, u32[]{:S(2)}, u32[]{:S(2)}) collective-permute-start(bf16[2,40,1152]{2,1,0:T(8,128)(2,1)S(1)} %maximum_select_fusion.1), channel_id=1, source_target_pairs={{0,8},{4,12},{8,0},{12,4},{1,9},{5,13},{9,1},{13,5},{2,10},{6,14},... | collective-permute-start | bytes 552968 | tf_op jit(solution)/shard_map/ppermute | solution.py:56
  133.0 11.6 %collective-permute-start.21 = (bf16[2,40,1152]{2,1,0:T(8,128)(2,1)S(1)}, bf16[2,40,1152]{2,1,0:T(8,128)(2,1)S(1)}, u32[]{:S(2)}, u32[]{:S(2)}) collective-permute-start(bf16[2,40,1152]{2,1,0:T(8,128)(2,1)S(1)} %maximum_select_fusion.1), channel_id=1, source_target_pairs={{0,4},{4,8},{8,12},{12,0},{1,5},{5,9},{9,13},{13,1},{2,6},{6,10},{... | collective-permute-start | bytes 552968 | tf_op jit(solution)/shard_map/ppermute | solution.py:56
  144.7 4.0 %collective-permute-start.24 = (bf16[4,2,40,1152]{3,2,1,0:T(8,128)(2,1)S(1)}, bf16[4,2,40,1152]{3,2,1,0:T(8,128)(2,1)S(1)}, u32[]{:S(2)}, u32[]{:S(2)}) collective-permute-start(bf16[4,2,40,1152]{3,2,1,0:T(8,128)(2,1)S(1)} %pad_maximum_fusion.1.own), channel_id=1, source_target_pairs={{0,1},{1,0},{2,3},{3,2},{4,5},{5,4},{6,7},{7,6},{8,9},{9,8},{10,11... | collective-permute-start | bytes 2211848 | tf_op jit(solution)/shard_map/ppermute | solution.py:48
  151.1 1.0 copy-start.1
  152.1 7.6 %copy-start.6 = (bf16[512,269]{0,1:T(8,128)(2,1)S(1)}, bf16[512,269]{0,1:T(8,128)(2,1)}, u32[]{:S(2)}) copy-start(bf16[512,269]{0,1:T(8,128)(2,1)} %param.13) | copy-start | bytes 826372
  152.1 30.5 %all-to-all-start.2 = ((bf16[16,72,384]{2,1,0:T(8,128)(2,1)}), bf16[16,72,384]{2,1,0:T(8,128)(2,1)S(1)}, u32[]{:S(2)}, u32[]{:S(2)}) async-start(bf16[16,72,384]{2,1,0:T(8,128)(2,1)} %get-tuple-element.38), calls=%async_computation.2 | async-start | bytes 1769472 | tf_op jit(solution)/shard_map/all_to_all | solution.py:93
  161.3 3.6 %copy-start.2 = (bf16[4,2,2,32,1152]{4,3,2,1,0:T(8,128)(2,1)S(1)}, bf16[4,2,2,32,1152]{4,3,2,1,0:T(8,128)(2,1)}, u32[]{:S(2)}) copy-start(bf16[4,2,2,32,1152]{4,3,2,1,0:T(8,128)(2,1)} %copy-done.1) | copy-start | bytes 3538948
  161.3 1.9 collective-permute-start.25
  163.4 2.8 %copy-start.10 = (bf16[269,1152]{1,0:T(8,128)(2,1)S(1)}, bf16[269,1152]{1,0:T(8,128)(2,1)}, u32[]{:S(2)}) copy-start(bf16[269,1152]{1,0:T(8,128)(2,1)} %param.14) | copy-start | bytes 1859332
  163.4 4.4 %collective-permute-start.28 = (bf16[2,72,384]{2,1,0:T(8,128)(2,1)S(1)}, bf16[2,72,384]{2,1,0:T(8,128)(2,1)S(1)}, u32[]{:S(2)}, u32[]{:S(2)}) collective-permute-start(bf16[2,72,384]{2,1,0:T(8,128)(2,1)S(1)} %get-tuple-element.55), channel_id=1, source_target_pairs={{0,12},{4,0},{8,4},{12,8},{1,13},{5,1},{9,5},{13,9},{2,14},{6,2},{... | collective-permute-start | bytes 331784 | tf_op jit(solution)/shard_map/ppermute | solution.py:56
  164.0 5.5 %collective-permute-start.27 = (bf16[2,72,384]{2,1,0:T(8,128)(2,1)S(1)}, bf16[2,72,384]{2,1,0:T(8,128)(2,1)S(1)}, u32[]{:S(2)}, u32[]{:S(2)}) collective-permute-start(bf16[2,72,384]{2,1,0:T(8,128)(2,1)S(1)} %get-tuple-element.56), channel_id=1, source_target_pairs={{0,8},{4,12},{8,0},{12,4},{1,9},{5,13},{9,1},{13,5},{2,10},{6,14},... | collective-permute-start | bytes 331784 | tf_op jit(solution)/shard_map/ppermute | solution.py:56
  164.0 8.9 %collective-permute-start.26 = (bf16[2,72,384]{2,1,0:T(8,128)(2,1)S(1)}, bf16[2,72,384]{2,1,0:T(8,128)(2,1)S(1)}, u32[]{:S(2)}, u32[]{:S(2)}) collective-permute-start(bf16[2,72,384]{2,1,0:T(8,128)(2,1)S(1)} %get-tuple-element.54), channel_id=1, source_target_pairs={{0,4},{4,8},{8,12},{12,0},{1,5},{5,9},{9,13},{13,1},{2,6},{6,10},{... | collective-permute-start | bytes 331784 | tf_op jit(solution)/shard_map/ppermute | solution.py:56
  183.6 4.5 %collective-permute-start.29 = (bf16[72,384]{1,0:T(8,128)(2,1)S(1)}, bf16[72,384]{1,0:T(8,128)(2,1)S(1)}, u32[]{:S(2)}, u32[]{:S(2)}) collective-permute-start(bf16[72,384]{1,0:T(8,128)(2,1)S(1)} %get-tuple-element.60), channel_id=1, source_target_pairs={{0,2},{2,0},{1,3},{3,1},{4,6},{6,4},{5,7},{7,5},{8,10},{10,8},{9,1... | collective-permute-start | bytes 165896 | tf_op jit(solution)/shard_map/ppermute | solution.py:48
where the time goes:
time: 193 us; the launch traced here: 190 us
  waiting for transfers between devices  73.4 us (38%)
  starting transfers between devices  69.8 us (36%)
  Pallas kernels  14.4 us (7%)
  local copies, waits for them, and re-layouts  9.27 us (5%)
  between operations  8.23 us (4%)
  matrix products  7.57 us (4%)
  other arithmetic  7.2 us (4%)
    all_to_all x5, starting transfers between devices, exchange(): return lax.all_to_all(blocks, axis, 0, 0)  35.2 us
    all_to_all x5, waiting for transfers between devices, exchange(): return lax.all_to_all(blocks, axis, 0, 0)  28.5 us
    ppermute x9, waiting for transfers between devices, shift(): lax.ppermute(block, axis, [(i, (i + step) % count) for i in range(count)])  25.2 us
    ppermute x9, starting transfers between devices, swap(): return lax.ppermute(block, axis, SWAP)  14.3 us
    ppermute x12, starting transfers between devices, plane_shift(): lax.ppermute(block, ('xl', 'y', 'xh', 'c'), plane_pairs(step % 4, first))  13.3 us
    ppermute x12, waiting for transfers between devices, plane_shift(): lax.ppermute(block, ('xl', 'y', 'xh', 'c'), plane_pairs(step % 4, first))  11.3 us
    ppermute x9, waiting for transfers between devices, swap(): return lax.ppermute(block, axis, SWAP)  8.45 us
    ppermute x9, starting transfers between devices, shift(): lax.ppermute(block, axis, [(i, (i + step) % count) for i in range(count)])  6.94 us
  transfers between devices with their start and end apart: 35, of which 25 were waited for; matrix products, arithmetic and copies ran while one was open for 9% of the time, Pallas kernels for 4%

commit v1 on v0

v1 whole, which is shorter than its diff:
```python
import functools

import jax
import jax.numpy as jnp
from jax import lax
from jax.experimental import pallas as pl
from jax.experimental.pallas import tpu as pltpu
from jax.sharding import Mesh, PartitionSpec as P

AXES = ("z", "xl", "y", "xh", "c")
SIZES = (8, 2, 4, 2, 2)
IMG = ("z", "xl")
TXT = ("y", "xh", "c")
PLANE = ("xl", "y", "xh")
SWAP = [(0, 1), (1, 0)]
f32 = jnp.float32
bf16 = jnp.bfloat16


def normalize(embed):
    values = embed.astype(f32)
    inverse = lax.rsqrt(jnp.sum(values * values, axis=-1, keepdims=True) + 1e-06)
    return (values * inverse, inverse)


def project(embed, upstream):
    unit, inverse = normalize(embed)
    return inverse * (upstream - unit * jnp.sum(unit * upstream, axis=-1, keepdims=True))


def dot(left, right):
    return jnp.dot(left, right, preferred_element_type=f32)


def contract_rows(left, right):
    return lax.dot_general(left, right, (((0,), (0,)), ((), ())), preferred_element_type=f32)


def contract_cols(left, right):
    return lax.dot_general(left, right, (((1,), (1,)), ((), ())), preferred_element_type=f32)


def pick(blocks, index, axis=0):
    return lax.dynamic_index_in_dim(blocks, index, axis, keepdims=False)


def swap(block, axis):
    return lax.ppermute(block, axis, SWAP)


def pair(mine, other, index):
    return jnp.where(index == 0, jnp.stack([mine, other]), jnp.stack([other, mine]))


def shift(block, axis, step, count=4):
    return lax.ppermute(block, axis, [(i, (i + step) % count) for i in range(count)])


def plane_pairs(step, first):
    pairs = []
    for x in range(4):
        for y in range(4):
            for c in range(2):
                x2, y2 = ((x + step) % 4, y) if (c == 0) == first else (x, (y + step) % 4)
                pairs.append(
                    (((x % 2) * 4 + y) * 4 + (x // 2) * 2 + c, ((x2 % 2) * 4 + y2) * 4 + (x2 // 2) * 2 + c)
                )
    return pairs


def plane_shift(block, step, first):
    return lax.ppermute(block, ("xl", "y", "xh", "c"), plane_pairs(step % 4, first))


def gather_first(block):
    return jnp.stack([block] + [plane_shift(block, d, True) for d in (1, 2, 3)])


def gather_second(row):
    return jnp.stack([row] + [plane_shift(row, d, False) for d in (1, 2, 3)])


def sum_second(slab):
    total = slab[0].astype(f32)
    for d in (1, 2, 3):
        total = total + plane_shift(slab[d], -d, False).astype(f32)
    return total.astype(bf16)


def sum_first(row):
    total = row[0].astype(f32)
    for d in (1, 2, 3):
        total = total + plane_shift(row[d], -d, True).astype(f32)
    return total.astype(bf16)


def exchange(blocks, axis):
    return lax.all_to_all(blocks, axis, 0, 0)


def gather(block, axis):
    return exchange(jnp.broadcast_to(block[None], (lax.axis_size(axis),) + block.shape), axis)


def scatter_sum(blocks, axis):
    return jnp.sum(exchange(blocks, axis).astype(f32), axis=0)


CHUNK = 256
VMEM = pl.BlockSpec(memory_space=pltpu.VMEM)
SMEM = pl.BlockSpec(memory_space=pltpu.SMEM)


def score_rows(params, base, image, unit, labels, total, image_parts):
    scale, bias = params[0], params[1]
    index = lax.broadcasted_iota(jnp.int32, (unit.shape[0], 1), 0)
    columns = base[0] + index + (index & -32)
    loss = jnp.zeros((1, CHUNK), f32)
    for start in range(0, image.shape[0], CHUNK):
        part = pl.ds(start, CHUNK)
        wide_unit, inverse = normalize(image[part, :])
        image_unit = wide_unit.astype(bf16)
        scores = scale * contract_cols(unit, image_unit) + bias
        hit = labels[:, part] == columns
        small = jnp.exp(-jnp.abs(scores))
        signed = jnp.where(hit, -scores, scores)
        terms = jnp.maximum(signed, 0.0) + jnp.log1p(small)
        loss = loss + jnp.sum(terms, axis=0, keepdims=True)
        sigmoid = jnp.where(scores >= 0.0, 1.0, small) / (1.0 + small)
        slope = (sigmoid - hit.astype(f32)).astype(bf16)
        total = total + dot(slope, image_unit)
        upstream = scale * contract_rows(slope, unit)
        along = jnp.sum(wide_unit * upstream, axis=-1, keepdims=True)
        image_parts[part, :] = (inverse * (upstream - wide_unit * along)).astype(bf16)
    return total, loss


def score_kernel(params, base, image, text, labels, total_out, unit_out, image_parts, loss_out):
    unit = normalize(text[...])[0].astype(bf16)
    unit_out[...] = unit
    total = jnp.zeros(text.shape, f32)
    total, loss = score_rows(params, base, image, unit, labels, total, image_parts)
    total_out[...] = total
    loss_out[...] = loss


def rest_kernel(params, base, image, text, labels, total, unit, loss, text_parts, image_parts, halves):
    sums, more = score_rows(params, base, image, unit[...], labels, total[...], image_parts)
    text_parts[...] = project(text[...], params[0] * sums).astype(bf16)
    sums = jnp.sum(loss[...] + more, axis=1, keepdims=True)
    high = sums.astype(bf16).astype(f32)
    lane = lax.broadcasted_iota(jnp.int32, halves.shape, 1)
    values = jnp.where(lane == 0, high, jnp.where(lane == 1, sums - high, 0.0))
    halves[...] = values.astype(bf16)


def like(array, dtype):
    return jax.ShapeDtypeStruct(array.shape, dtype)


def score_call(params, base, image, text, labels):
    return pl.pallas_call(
        score_kernel,
        out_shape=(
            like(text, f32),
            like(text, bf16),
            like(image, bf16),
            jax.ShapeDtypeStruct((1, CHUNK), f32),
        ),
        in_specs=[SMEM, SMEM, VMEM, VMEM, VMEM],
        out_specs=(VMEM, VMEM, VMEM, VMEM),
        compiler_params=pltpu.CompilerParams(vmem_limit_bytes=24 * 2**20),
        name="score",
    )(params, base, image, text, labels)


def rest_call(params, base, image, text, labels, total, unit, loss):
    return pl.pallas_call(
        rest_kernel,
        out_shape=(
            like(text, bf16),
            like(image, bf16),
            jax.ShapeDtypeStruct((8, text.shape[1]), bf16),
        ),
        in_specs=[SMEM, SMEM, VMEM, VMEM, VMEM, VMEM, VMEM, VMEM],
        out_specs=(VMEM, VMEM, VMEM),
        compiler_params=pltpu.CompilerParams(vmem_limit_bytes=24 * 2**20),
        name="score_rest",
    )(params, base, image, text, labels, total, unit, loss)


def packed(grad, acts, hidden, high, low):
    main = lax.dot_general(
        grad, acts[:256, :], (((0,), (1,)), ((), ())), preferred_element_type=f32
    )
    tail = dot(acts[256:, :], grad)
    row = lax.broadcasted_iota(jnp.int32, tail.shape, 0)
    tail = jnp.where(row == hidden - 256, high, jnp.where(row == hidden - 255, low, tail))
    width = grad.shape[1]
    height = width // 16
    for k in range(16):
        left, right = [
            pltpu.roll(half, (width - k * height) % width, 1)[:, :128] for half in (tail[:8], tail[8:])
        ]
        below = jnp.concatenate([left, right], axis=1)
        yield jnp.concatenate([main[k * height : (k + 1) * height], below], axis=0)


def finish_kernel(hidden, blocks, grad, value):
    total = jnp.zeros(blocks.shape[1:], f32)
    for k in range(blocks.shape[0]):
        total = total + blocks[k].astype(f32)
    height = grad.shape[0]
    grad[:, :256] = total[:height]
    tail = jnp.concatenate([total[height:, :128], total[height:, 128:]])
    grad[:, 256:] = tail.T[:height, : hidden - 256]
    value[...] = tail[hidden - 256 : hidden - 255, :1] + tail[hidden - 255 : hidden - 254, :1]


def finish_call(blocks, hidden):
    grad, value = pl.pallas_call(
        functools.partial(finish_kernel, hidden),
        out_shape=(
            jax.ShapeDtypeStruct((blocks.shape[1] - 8, hidden), f32),
            jax.ShapeDtypeStruct((1, 1), f32),
        ),
        in_specs=[VMEM],
        out_specs=(VMEM, VMEM),
        compiler_params=pltpu.CompilerParams(vmem_limit_bytes=16 * 2**20),
        name="finish",
    )(blocks)
    return grad.T, value


def weight_kernel(hidden, place, own, other, acts, back, blocks):
    y, c = place[0], place[1]
    rows, width = back.shape[-2:]
    loss = jnp.zeros((1, 128), f32)
    for d in range(4):
        at = lax.rem(y - d + 4, 4)
        for k in range(2):
            back[at, k, c] = own[d, k, :rows]
            back[at, k, 1 - c] = other[d, k, :rows]
            for part in (own, other):
                loss = loss + part[d, k, rows:].astype(f32)[:1, :128]
    total = jnp.sum(loss, axis=1, keepdims=True)
    high = total.astype(bf16).astype(f32)
    for k, block in enumerate(packed(back[...].reshape(-1, width), acts, hidden, high, total - high)):
        blocks[k] = block.astype(bf16)


def weight_call(place, own, other, acts, rows, hidden):
    width = own.shape[-1]
    return pl.pallas_call(
        functools.partial(weight_kernel, hidden),
        out_shape=(
            jax.ShapeDtypeStruct((4, 2, 2, rows, width), bf16),
            jax.ShapeDtypeStruct((16, width // 16 + 8, 256), bf16),
        ),
        in_specs=[SMEM, VMEM, VMEM, VMEM],
        out_specs=(VMEM, VMEM),
        compiler_params=pltpu.CompilerParams(vmem_limit_bytes=24 * 2**20),
        name="image_weight",
    )(place, own, other, acts)


def text_weight_kernel(hidden, place, back, acts, mine, theirs):
    blocks = list(packed(back[...], acts, hidden, 0.0, 0.0))
    for k in range(8):
        left, right = blocks[2 * k], blocks[2 * k + 1]
        mine[k // 2, k % 2] = jnp.where(place[1] == 0, left, right).astype(bf16)
        theirs[k // 2, k % 2] = jnp.where(place[1] == 0, right, left).astype(bf16)


def text_weight_call(place, back, acts, hidden):
    shape = jax.ShapeDtypeStruct((4, 2, back.shape[1] // 16 + 8, 256), bf16)
    return pl.pallas_call(
        functools.partial(text_weight_kernel, hidden),
        out_shape=(shape, shape),
        in_specs=[SMEM, VMEM, VMEM],
        out_specs=(VMEM, VMEM),
        compiler_params=pltpu.CompilerParams(vmem_limit_bytes=24 * 2**20),
        name="text_weight",
    )(place, back, acts)


def after(value, done):
    return lax.optimization_barrier((value, done))[0]


def on_device(
    image_hidden,
    image_acts,
    image_proj,
    text_hidden,
    text_acts,
    text_proj,
    positives,
    log_scale,
    bias,
):
    z, xl, y, xh, c = [lax.axis_index(name) for name in AXES]
    x = xh * 2 + xl
    rows, width = image_hidden.shape
    hidden = text_proj.shape[0]
    total_rows = rows * 256
    scale = jnp.exp(log_scale[0])

    text_parts = dot(text_acts, text_proj).astype(bf16).reshape(16, rows, width)
    text_sum = scatter_sum(text_parts, IMG)
    text_embed = (text_hidden.astype(f32) + text_sum).astype(bf16)

    image_acts = after(image_acts, text_parts)
    parts = dot(image_acts, image_proj).astype(bf16).reshape(4, 2, 2, rows, width)
    parts = (pick(parts, c, 2).astype(f32) + swap(pick(parts, 1 - c, 2), "c").astype(f32)).astype(bf16)
    total = pick(parts, y).astype(f32)
    for d in (1, 2, 3):
        total = total + shift(pick(parts, (y + d) % 4), "y", d).astype(f32)
    total = total.astype(bf16)
    image_sum = pick(total, xh).astype(f32) + swap(pick(total, 1 - xh), "xh").astype(f32)
    image_embed = (image_hidden.astype(f32) + image_sum).astype(bf16)

    positives_near = swap(positives, "xl")
    labels = pair(positives, positives_near, xl).reshape(2, 4, 2, 2, rows)
    n = jnp.arange(32, dtype=jnp.int32)
    core = jnp.where(n < 16, c, 1 - c)
    e, d = n // 4 % 4, n % 4
    from_x = (x - jnp.where(core == 0, d, e)) & 3
    from_y = (y - jnp.where(core == 0, e, d)) & 3
    order = (((from_x % 2) * 4 + from_y) * 2 + from_x // 2) * 2 + core
    labels = jnp.take(labels.reshape(32, rows), order, axis=0).reshape(1, -1)
    base = jnp.reshape(((y * 2 + xh) * 2 + c) * 512 + xl * rows, (1,)).astype(jnp.int32)
    image_row = gather_first(image_embed)
    text_block = gather(after(text_embed, (image_row, labels)), "z").reshape(-1, width)
    own_block = gather_second(after(image_row, text_embed)).reshape(-1, width)
    near_block = swap(after(own_block, text_block), "c")

    params = jnp.stack([scale, bias[0]])
    half = 16 * rows
    text_total, text_unit, mine, losses = score_call(
        params, base, own_block, text_block, labels[:, :half]
    )
    text_parts, theirs, halves = rest_call(
        params, base, near_block, text_block, labels[:, half:], text_total, text_unit, losses
    )
    text_grad = scatter_sum(text_parts.reshape(8, rows, width), "z").astype(bf16)
    theirs = swap(theirs, "c")
    slab = (mine.astype(f32) + theirs.astype(f32)).astype(bf16)
    image_row = sum_second(slab.reshape(4, 4, rows, width))
    image_grad = sum_first(image_row)

    near = jnp.concatenate([image_grad, halves])
    near = pair(near, swap(near, "xh"), xh)
    ring = jnp.stack([near] + [shift(near, "y", d) for d in (1, 2, 3)])
    place = jnp.stack([y, c]).astype(jnp.int32)
    wide = ((0, 272 - hidden), (0, 0))
    image_back, blocks = weight_call(place, ring, swap(ring, "c"), jnp.pad(image_acts.T, wide), rows, hidden)
    image_back = image_back.reshape(-1, width)
    found = exchange(blocks, IMG)

    text_back = gather(after(text_grad, image_row), IMG).reshape(-1, width)
    text_back = after(text_back, blocks)
    mine, theirs = text_weight_call(place, text_back, jnp.pad(text_acts.T, wide), hidden)
    parts = (mine.astype(f32) + swap(theirs, "c").astype(f32)).astype(bf16)
    total = pick(parts, y).astype(f32)
    for d in (1, 2, 3):
        total = total + shift(pick(parts, (y + d) % 4), "y", d).astype(f32)
    total = total.astype(bf16)
    last = jnp.stack([pick(total, xh), swap(pick(total, 1 - xh), "xh")])

    image_act_grad = contract_cols(after(image_back, parts), image_proj).astype(bf16)
    text_act_grad = contract_cols(after(text_back, parts), text_proj).astype(bf16)

    text_proj_grad = finish_call(last, hidden)[0]
    image_proj_grad, total_loss = finish_call(after(found, last), hidden)
    loss = jnp.reshape(total_loss / total_rows, (1,))
    return (
        loss,
        image_grad,
        text_grad,
        image_act_grad,
        text_act_grad,
        image_proj_grad,
        text_proj_grad,
    )


def solution(mesh):
    fine = Mesh(mesh.devices.reshape(SIZES), AXES)
    return jax.shard_map(
        on_device,
        mesh=fine,
        in_specs=(
            P(IMG + TXT, None),
            P(IMG, TXT),
            P(TXT, None),
            P(TXT + IMG, None),
            P(TXT, IMG),
            P(IMG, None),
            P(IMG),
            P(),
            P(),
        ),
        out_specs=(
            P(),
            P(IMG + TXT, None),
            P(TXT + IMG, None),
            P(IMG, TXT),
            P(TXT, IMG),
            P(TXT, IMG),
            P(IMG, TXT),
        ),
        check_vma=False,
    )
```

time: 193 us -> 183 us (0.948)
  local copies, waits for them, and re-layouts: 9.27 us -> 4.16 us
  waiting for transfers between devices: 73.4 us -> 77.7 us
  other arithmetic: 7.2 us -> 3.02 us
  between operations: 8.23 us -> 4.22 us
  starting transfers between devices: 69.8 us -> 72.5 us
    ppermute x9, waiting for transfers between devices: 8.45 us -> 20.7 us  [swap(): return lax.ppermute(block, axis, SWAP)]
    all_to_all x5, starting transfers between devices: 35.2 us -> 26.8 us  [exchange(): return lax.all_to_all(blocks, axis, 0, 0)]
    ppermute x9, starting transfers between devices: 14.3 us -> 21 us  [swap(): return lax.ppermute(block, axis, SWAP)]
    all_to_all x5, waiting for transfers between devices: 28.5 us -> 23.6 us  [exchange(): return lax.all_to_all(blocks, axis, 0, 0)]
    ppermute x9, waiting for transfers between devices: 25.2 us -> 20.6 us  [shift(): lax.ppermute(block, axis, [(i, (i + step) % count) for i in range(count)])]
    ppermute x9, starting transfers between devices: 6.94 us -> 9.75 us  [shift(): lax.ppermute(block, axis, [(i, (i + step) % count) for i in range(count)])]
    pallas_call x4, Pallas kernels: 9.82 us -> 7.64 us  [the longest x1 4.9 us: rest_call(): pl.pallas_call(rest_kernel, out_shape=(like(text, bf16), like(image, bf16...]
  transfers between devices with their start and end apart: 35 -> 35, of which waited for: 25 -> 24; matrix products, arithmetic and copies ran while one was open for 9% -> 4% of each run, Pallas kernels for 4% -> 4%
where the time goes in v1:
time: 183 us; the launch traced here: 181 us
  waiting for transfers between devices  77.7 us (42%)
  starting transfers between devices  72.5 us (40%)
  Pallas kernels  13.3 us (7%)
  matrix products  6.54 us (4%)
  between operations  4.22 us (2%)
  local copies, waits for them, and re-layouts  4.16 us (2%)
  other arithmetic  3.02 us (2%)
    all_to_all x5, starting transfers between devices, exchange(): return lax.all_to_all(blocks, axis, 0, 0)  26.8 us
    all_to_all x5, waiting for transfers between devices, exchange(): return lax.all_to_all(blocks, axis, 0, 0)  23.6 us
    ppermute x9, starting transfers between devices, swap(): return lax.ppermute(block, axis, SWAP)  21 us
    ppermute x9, waiting for transfers between devices, swap(): return lax.ppermute(block, axis, SWAP)  20.7 us
    ppermute x9, waiting for transfers between devices, shift(): lax.ppermute(block, axis, [(i, (i + step) % count) for i in range(count)])  20.6 us
    ppermute x12, starting transfers between devices, plane_shift(): lax.ppermute(block, ('xl', 'y', 'xh', 'c'), plane_pairs(step % 4, first))  15 us
    ppermute x12, waiting for transfers between devices, plane_shift(): lax.ppermute(block, ('xl', 'y', 'xh', 'c'), plane_pairs(step % 4, first))  12.7 us
    ppermute x9, starting transfers between devices, shift(): lax.ppermute(block, axis, [(i, (i + step) % count) for i in range(count)])  9.75 us
  transfers between devices with their start and end apart: 35, of which 24 were waited for; matrix products, arithmetic and copies ran while one was open for 4% of the time, Pallas kernels for 4%

profile of v1, /device:TPU:1, one launch (start us, length us, event | category | flops | bytes accessed | tf_op | source)
XLA Modules:
  0.0 181.4 jit_solution(17819005050286067381)
XLA Ops:
  0.7 3.1 %convolution_convert_fusion.1 = bf16[512,1152]{1,0:T(8,128)(2,1)} fusion(bf16[512,269]{0,1:T(8,128)(2,1)} %param.13, bf16[269,1152]{1,0:T(8,128)(2,1)} %param.14), kind=kOutput, calls=%fused_computation.2 | convolution fusion | flops 317915136 | bytes 2074880 | tf_op jit(solution)/shard_map/dot_general | solution.py:32
  4.8 3.3 %collective-permute-start = (bf16[4,2,32,1152]{3,2,1,0:T(8,128)(2,1)S(1)}, bf16[4,2,32,1152]{3,2,1,0:T(8,128)(2,1)S(1)}, u32[]{:S(2)}, u32[]{:S(2)}) collective-permute-start(bf16[4,2,32,1152]{3,2,1,0:T(8,128)(2,1)S(1)} %dynamic-slice_bitcast_fusion), channel_id=1, source_target_pairs={{0,1},{1,0},{2,3},{3,2},{4,5},{5,4},{6,7},{7,6},{8,9},{9,8},{10,11... | collective-permute-start | bytes 1769480 | tf_op jit(solution)/shard_map/ppermute | solution.py:48
  8.1 7.7 %all-to-all-start = ((bf16[16,32,1152]{2,1,0:T(8,128)(2,1)}), bf16[16,32,1152]{2,1,0:T(8,128)(2,1)S(1)}, u32[]{:S(2)}, u32[]{:S(2)}) async-start(bf16[16,32,1152]{2,1,0:T(8,128)(2,1)} %bitcast.3), calls=%async_computation | async-start | bytes 2359296 | tf_op jit(solution)/shard_map/all_to_all | solution.py:98
  15.8 1.4 collective-permute-start.11
  18.6 2.8 %collective-permute-start.3 = (bf16[2,32,1152]{2,1,0:T(8,128)(2,1)S(1)}, bf16[2,32,1152]{2,1,0:T(8,128)(2,1)S(1)}, u32[]{:S(2)}, u32[]{:S(2)}) collective-permute-start(bf16[2,32,1152]{2,1,0:T(8,128)(2,1)S(1)} %get-tuple-element.58), channel_id=1, source_target_pairs={{0,12},{4,0},{8,4},{12,8},{1,13},{5,1},{9,5},{13,9},{2,14},{6,2},{... | collective-permute-start | bytes 442376 | tf_op jit(solution)/shard_map/ppermute | solution.py:56
  22.5 1.7 collective-permute-done.3
  24.2 3.0 %collective-permute-done.2 = bf16[2,32,1152]{2,1,0:T(8,128)(2,1)S(1)} collective-permute-done((bf16[2,32,1152]{2,1,0:T(8,128)(2,1)S(1)}, bf16[2,32,1152]{2,1,0:T(8,128)(2,1)S(1)}, u32[]{:S(2)}, u32[]{:S(2)}) %collective-permute-start.2) | collective-permute-done | bytes 147488 | tf_op jit(solution)/shard_map/ppermute | solution.py:56
  27.2 3.8 %collective-permute-done.1 = bf16[2,32,1152]{2,1,0:T(8,128)(2,1)S(1)} collective-permute-done((bf16[2,32,1152]{2,1,0:T(8,128)(2,1)S(1)}, bf16[2,32,1152]{2,1,0:T(8,128)(2,1)S(1)}, u32[]{:S(2)}, u32[]{:S(2)}) %collective-permute-start.1) | collective-permute-done | bytes 147488 | tf_op jit(solution)/shard_map/ppermute | solution.py:56
  31.1 2.5 %collective-permute-start.4 = (bf16[32,1152]{1,0:T(8,128)(2,1)S(1)}, bf16[32,1152]{1,0:T(8,128)(2,1)S(1)}, u32[]{:S(2)}, u32[]{:S(2)}) collective-permute-start(bf16[32,1152]{1,0:T(8,128)(2,1)S(1)} %dynamic-slice_bitcast_fusion.7), channel_id=1, source_target_pairs={{0,2},{2,0},{1,3},{3,1},{4,6},{6,4},{5,7},{7,5},{8,10},{10,8},{9,1... | collective-permute-start | bytes 221192 | tf_op jit(solution)/shard_map/ppermute | solution.py:48
  34.3 6.5 %collective-permute-done.4 = bf16[32,1152]{1,0:T(8,128)(2,1)S(1)} collective-permute-done((bf16[32,1152]{1,0:T(8,128)(2,1)S(1)}, bf16[32,1152]{1,0:T(8,128)(2,1)S(1)}, u32[]{:S(2)}, u32[]{:S(2)}) %collective-permute-start.4) | collective-permute-done | bytes 73760 | tf_op jit(solution)/shard_map/ppermute | solution.py:48
  41.0 1.4 collective-permute-start.5
  42.6 1.9 %collective-permute-done.7 = bf16[32,1152]{1,0:T(8,128)(2,1)S(1)} collective-permute-done((bf16[32,1152]{1,0:T(8,128)(2,1)S(1)}, bf16[32,1152]{1,0:T(8,128)(2,1)S(1)}, u32[]{:S(2)}, u32[]{:S(2)}) %collective-permute-start.7) | collective-permute-done | bytes 73760 | tf_op jit(solution)/shard_map/ppermute | solution.py:72
  44.4 1.6 collective-permute-done.6
  48.0 8.3 %all-to-all-start.1 = ((bf16[8,32,1152]{2,1,0:T(8,128)(2,1)}), bf16[8,32,1152]{2,1,0:T(8,128)(2,1)S(1)}, u32[]{:S(2)}, u32[]{:S(2)}) async-start(bf16[8,32,1152]{2,1,0:T(8,128)(2,1)} %broadcast_in_dim.40), calls=%async_computation.1 | async-start | bytes 1179648 | tf_op jit(solution)/shard_map/all_to_all | solution.py:98
  56.3 3.8 %collective-permute-start.9 = (bf16[4,32,1152]{2,1,0:T(8,128)(2,1)S(1)}, bf16[4,32,1152]{2,1,0:T(8,128)(2,1)S(1)}, u32[]{:S(2)}, u32[]{:S(2)}) collective-permute-start(bf16[4,32,1152]{2,1,0:T(8,128)(2,1)S(1)} %pad_maximum_fusion.2), channel_id=1, source_target_pairs={{0,8},{1,3},{4,12},{5,7},{8,0},{9,11},{12,4},{13,15},{16,24},{17,1... | collective-permute-start | bytes 884744 | tf_op jit(solution)/shard_map/ppermute | solution.py:72
  61.8 2.4 %collective-permute-done.9 = bf16[4,32,1152]{2,1,0:T(8,128)(2,1)S(1)} collective-permute-done((bf16[4,32,1152]{2,1,0:T(8,128)(2,1)S(1)}, bf16[4,32,1152]{2,1,0:T(8,128)(2,1)S(1)}, u32[]{:S(2)}, u32[]{:S(2)}) %collective-permute-start.9) | collective-permute-done | bytes 294944 | tf_op jit(solution)/shard_map/ppermute | solution.py:72
  64.2 3.4 %collective-permute-done.8 = bf16[4,32,1152]{2,1,0:T(8,128)(2,1)S(1)} collective-permute-done((bf16[4,32,1152]{2,1,0:T(8,128)(2,1)S(1)}, bf16[4,32,1152]{2,1,0:T(8,128)(2,1)S(1)}, u32[]{:S(2)}, u32[]{:S(2)}) %collective-permute-start.8) | collective-permute-done | bytes 294944 | tf_op jit(solution)/shard_map/ppermute | solution.py:72
  67.8 1.3 all-to-all-done.1
  69.1 7.1 %collective-permute-start.12 = (bf16[512,1152]{1,0:T(8,128)(2,1)S(1)}, bf16[512,1152]{1,0:T(8,128)(2,1)}, u32[]{:S(2)}, u32[]{:S(2)}) collective-permute-start(bf16[512,1152]{1,0:T(8,128)(2,1)S(1)} %bitcast.97), channel_id=1, source_target_pairs={{0,1},{1,0},{2,3},{3,2},{4,5},{5,4},{6,7},{7,6},{8,9},{9,8},{10,11... | collective-permute-start | bytes 3538952 | tf_op jit(solution)/shard_map/ppermute | solution.py:48
  77.6 3.5 %score.1 = (f32[256,1152]{1,0:T(8,128)S(1)}, bf16[256,1152]{1,0:T(8,128)(2,1)S(1)}, bf16[512,1152]{1,0:T(8,128)(2,1)S(1)}, f32[1,256]{1,0:T(1,128)S(1)}) custom-call(f32[2]{0:T(128)S(1)} %pad_maximum_fusion.5.params, s32[1]{0:T(128)} %bitcast.2.base, bf16[512,1152]{1,0:T(8,128)(2,1)S(1)} %bitcast.98, bf16[256,1152]{1,0:T(8,128)(2,1)S(1)} %bitcast.93, ...), custom_call_target="tpu_custom_call" | custom-call | tf_op jit(solution)/shard_map/score/pallas_call | solution.py:162
  81.1 4.9 %score_rest.1 = (bf16[256,1152]{1,0:T(8,128)(2,1)}, bf16[512,1152]{1,0:T(8,128)(2,1)S(1)}, bf16[8,1152]{1,0:T(8,128)(2,1)S(1)}) custom-call(f32[2]{0:T(128)S(1)} %pad_maximum_fusion.5.params, s32[1]{0:T(128)} %bitcast.2.base, bf16[512,1152]{1,0:T(8,128)(2,1)} %collective-permute-done.12.image, bf16[256,1152]{1,0:T(8,128)(2,1)S(1)} %bitcast.94, ...), custom_call_target="tpu_custom_call" | custom-call | tf_op jit(solution)/shard_map/score_rest/pallas_call | solution.py:178
  86.0 2.8 %collective-permute-done.13 = bf16[512,1152]{1,0:T(8,128)(2,1)S(1)} collective-permute-done((bf16[512,1152]{1,0:T(8,128)(2,1)S(1)}, bf16[512,1152]{1,0:T(8,128)(2,1)S(1)}, u32[]{:S(2)}, u32[]{:S(2)}) %collective-permute-start.13) | collective-permute-done | bytes 1179680 | tf_op jit(solution)/shard_map/ppermute | solution.py:48
  89.3 3.7 %collective-permute-start.15 = (bf16[4,32,1152]{2,1,0:T(8,128)(2,1)S(1)}, bf16[4,32,1152]{2,1,0:T(8,128)(2,1)S(1)}, u32[]{:S(2)}, u32[]{:S(2)}) collective-permute-start(bf16[4,32,1152]{2,1,0:T(8,128)(2,1)S(1)} %bitcast.107), channel_id=1, source_target_pairs={{0,8},{1,3},{4,12},{5,7},{8,0},{9,11},{12,4},{13,15},{16,24},{17,1... | collective-permute-start | bytes 884744 | tf_op jit(solution)/shard_map/ppermute | solution.py:72
  93.0 2.0 %collective-permute-start.14 = (bf16[4,32,1152]{2,1,0:T(8,128)(2,1)S(1)}, bf16[4,32,1152]{2,1,0:T(8,128)(2,1)S(1)}, u32[]{:S(2)}, u32[]{:S(2)}) collective-permute-start(bf16[4,32,1152]{2,1,0:T(8,128)(2,1)S(1)} %bitcast.106), channel_id=1, source_target_pairs={{0,12},{1,19},{4,0},{5,23},{8,4},{9,27},{12,8},{13,31},{16,28},{17... | collective-permute-start | bytes 884744 | tf_op jit(solution)/shard_map/ppermute | solution.py:72
  95.0 3.5 %all-to-all-start.3 = ((bf16[8,32,1152]{2,1,0:T(8,128)(2,1)}), bf16[8,32,1152]{2,1,0:T(8,128)(2,1)S(1)}, u32[]{:S(2)}, u32[]{:S(2)}) async-start(bf16[8,32,1152]{2,1,0:T(8,128)(2,1)} %bitcast.42), calls=%async_computation.3 | async-start | bytes 1179648 | tf_op jit(solution)/shard_map/all_to_all | solution.py:98
  98.6 1.7 collective-permute-done.15
  101.1 2.3 %collective-permute-start.18 = (bf16[32,1152]{1,0:T(8,128)(2,1)S(1)}, bf16[32,1152]{1,0:T(8,128)(2,1)S(1)}, u32[]{:S(2)}, u32[]{:S(2)}) collective-permute-start(bf16[32,1152]{1,0:T(8,128)(2,1)S(1)} %get-tuple-element.65), channel_id=1, source_target_pairs={{0,2},{1,9},{4,6},{5,13},{8,10},{9,1},{12,14},{13,5},{16,18},{17,2... | collective-permute-start | bytes 221192 | tf_op jit(solution)/shard_map/ppermute | solution.py:72
  103.6 14.0 %all-to-all-done.3 = bf16[8,32,1152]{2,1,0:T(8,128)(2,1)S(1)} async-done(((bf16[8,32,1152]{2,1,0:T(8,128)(2,1)}), bf16[8,32,1152]{2,1,0:T(8,128)(2,1)S(1)}, u32[]{:S(2)}, u32[]{:S(2)}) %all-to-all-start.3) | async-done | bytes 589856 | tf_op jit(solution)/shard_map/all_to_all | solution.py:98
  118.8 3.7 %all-to-all-start.4 = ((bf16[16,32,1152]{2,1,0:T(8,128)(2,1)}), bf16[16,32,1152]{2,1,0:T(8,128)(2,1)S(1)}, u32[]{:S(2)}, u32[]{:S(2)}) async-start(bf16[16,32,1152]{2,1,0:T(8,128)(2,1)} %broadcast_in_dim.41), calls=%async_computation.4 | async-start | bytes 2359296 | tf_op jit(solution)/shard_map/all_to_all | solution.py:98
  122.8 5.3 %collective-permute-done.20 = bf16[40,1152]{1,0:T(8,128)(2,1)S(1)} collective-permute-done((bf16[40,1152]{1,0:T(8,128)(2,1)S(1)}, bf16[40,1152]{1,0:T(8,128)(2,1)S(1)}, u32[]{:S(2)}, u32[]{:S(2)}) %collective-permute-start.20) | collective-permute-done | bytes 92192 | tf_op jit(solution)/shard_map/ppermute | solution.py:48
  128.9 2.4 %collective-permute-start.22 = (bf16[2,40,1152]{2,1,0:T(8,128)(2,1)S(1)}, bf16[2,40,1152]{2,1,0:T(8,128)(2,1)S(1)}, u32[]{:S(2)}, u32[]{:S(2)}) collective-permute-start(bf16[2,40,1152]{2,1,0:T(8,128)(2,1)S(1)} %maximum_select_fusion.1), channel_id=1, source_target_pairs={{0,8},{4,12},{8,0},{12,4},{1,9},{5,13},{9,1},{13,5},{2,10},{6,14},... | collective-permute-start | bytes 552968 | tf_op jit(solution)/shard_map/ppermute | solution.py:56
  131.3 2.1 %collective-permute-done.23 = bf16[2,40,1152]{2,1,0:T(8,128)(2,1)S(1)} collective-permute-done((bf16[2,40,1152]{2,1,0:T(8,128)(2,1)S(1)}, bf16[2,40,1152]{2,1,0:T(8,128)(2,1)S(1)}, u32[]{:S(2)}, u32[]{:S(2)}) %collective-permute-start.23) | collective-permute-done | bytes 184352 | tf_op jit(solution)/shard_map/ppermute | solution.py:56
  133.4 1.7 collective-permute-done.22
  135.1 4.8 %collective-permute-done.21 = bf16[2,40,1152]{2,1,0:T(8,128)(2,1)S(1)} collective-permute-done((bf16[2,40,1152]{2,1,0:T(8,128)(2,1)S(1)}, bf16[2,40,1152]{2,1,0:T(8,128)(2,1)S(1)}, u32[]{:S(2)}, u32[]{:S(2)}) %collective-permute-start.21) | collective-permute-done | bytes 184352 | tf_op jit(solution)/shard_map/ppermute | solution.py:56
  140.0 1.7 collective-permute-start.24
  141.8 1.7 collective-permute-done.24.other
  143.5 2.2 %image_weight.1 = (bf16[4,2,2,32,1152]{4,3,2,1,0:T(8,128)(2,1)S(1)}, bf16[16,80,256]{2,1,0:T(8,128)(2,1)}) custom-call(s32[2]{0:T(128)S(1)} %pad_add_fusion.place, bf16[4,2,40,1152]{3,2,1,0:T(8,128)(2,1)S(1)} %pad_maximum_fusion.1.own, bf16[4,2,40,1152]{3,2,1,0:T(8,128)(2,1)S(1)} %collective-permute-done.24.other, bf16[272,512]{1,0:T(8,128)(2,1)S(1)} %pad.7.acts), custom_call_target="tpu_custom_call" | custom-call | tf_op jit(solution)/shard_map/image_weight/pallas_call | solution.py:254
  146.7 4.2 %all-to-all-done.4 = bf16[16,32,1152]{2,1,0:T(8,128)(2,1)S(1)} async-done(((bf16[16,32,1152]{2,1,0:T(8,128)(2,1)}), bf16[16,32,1152]{2,1,0:T(8,128)(2,1)S(1)}, u32[]{:S(2)}, u32[]{:S(2)}) %all-to-all-start.4) | async-done | bytes 1179680 | tf_op jit(solution)/shard_map/all_to_all | solution.py:98
  150.9 1.3 text_weight.1
  152.1 4.1 %collective-permute-start.25 = (bf16[4,2,80,256]{3,2,1,0:T(8,128)(2,1)S(1)}, bf16[4,2,80,256]{3,2,1,0:T(8,128)(2,1)S(1)}, u32[]{:S(2)}, u32[]{:S(2)}) collective-permute-start(bf16[4,2,80,256]{3,2,1,0:T(8,128)(2,1)S(1)} %get-tuple-element.45), channel_id=1, source_target_pairs={{0,1},{1,0},{2,3},{3,2},{4,5},{5,4},{6,7},{7,6},{8,9},{9,8},{10,11... | collective-permute-start | bytes 983048 | tf_op jit(solution)/shard_map/ppermute | solution.py:48
  156.3 3.6 %all-to-all-start.2 = ((bf16[16,80,256]{2,1,0:T(8,128)(2,1)}), bf16[16,80,256]{2,1,0:T(8,128)(2,1)S(1)}, u32[]{:S(2)}, u32[]{:S(2)}) async-start(bf16[16,80,256]{2,1,0:T(8,128)(2,1)} %get-tuple-element.40), calls=%async_computation.2 | async-start | bytes 1310720 | tf_op jit(solution)/shard_map/all_to_all | solution.py:98
  160.5 2.4 %collective-permute-start.27 = (bf16[2,80,256]{2,1,0:T(8,128)(2,1)S(1)}, bf16[2,80,256]{2,1,0:T(8,128)(2,1)S(1)}, u32[]{:S(2)}, u32[]{:S(2)}) collective-permute-start(bf16[2,80,256]{2,1,0:T(8,128)(2,1)S(1)} %get-tuple-element.62), channel_id=1, source_target_pairs={{0,8},{4,12},{8,0},{12,4},{1,9},{5,13},{9,1},{13,5},{2,10},{6,14},... | collective-permute-start | bytes 245768 | tf_op jit(solution)/shard_map/ppermute | solution.py:56
  162.9 1.3 convolution_convert_fusion.3
  164.2 1.5 collective-permute-done.27
  165.7 2.0 %collective-permute-done.26 = bf16[2,80,256]{2,1,0:T(8,128)(2,1)S(1)} collective-permute-done((bf16[2,80,256]{2,1,0:T(8,128)(2,1)S(1)}, bf16[2,80,256]{2,1,0:T(8,128)(2,1)S(1)}, u32[]{:S(2)}, u32[]{:S(2)}) %collective-permute-start.26) | collective-permute-done | bytes 81952 | tf_op jit(solution)/shard_map/ppermute | solution.py:56
  168.4 1.3 convolution_convert_fusion.2
  169.7 4.3 %collective-permute-done.29 = bf16[80,256]{1,0:T(8,128)(2,1)S(1)} collective-permute-done((bf16[80,256]{1,0:T(8,128)(2,1)S(1)}, bf16[80,256]{1,0:T(8,128)(2,1)S(1)}, u32[]{:S(2)}, u32[]{:S(2)}) %collective-permute-start.29) | collective-permute-done | bytes 40992 | tf_op jit(solution)/shard_map/ppermute | solution.py:48
  174.8 4.2 %all-to-all-done.2.blocks = bf16[16,80,256]{2,1,0:T(8,128)(2,1)S(1)} async-done(((bf16[16,80,256]{2,1,0:T(8,128)(2,1)}), bf16[16,80,256]{2,1,0:T(8,128)(2,1)S(1)}, u32[]{:S(2)}, u32[]{:S(2)}) %all-to-all-start.2) | async-done | bytes 655392 | tf_op jit(solution)/shard_map/all_to_all | solution.py:98
  (98 shorter events, 16.2 us)
Async XLA Ops:
  0.6 3.2 %copy-start = (bf16[269,1152]{1,0:T(8,128)(2,1)S(1)}, bf16[269,1152]{1,0:T(8,128)(2,1)}, u32[]{:S(2)}) copy-start(bf16[269,1152]{1,0:T(8,128)(2,1)} %param.11) | copy-start | bytes 1859332
  0.6 3.2 %copy-start.6 = (bf16[512,269]{0,1:T(8,128)(2,1)S(1)}, bf16[512,269]{0,1:T(8,128)(2,1)}, u32[]{:S(2)}) copy-start(bf16[512,269]{0,1:T(8,128)(2,1)} %param.10) | copy-start | bytes 826372
  4.7 3.4 %copy-start.3 = (bf16[512,1152]{1,0:T(8,128)(2,1)}, bf16[512,1152]{1,0:T(8,128)(2,1)S(1)}, u32[]{:S(2)}) copy-start(bf16[512,1152]{1,0:T(8,128)(2,1)S(1)} %convolution_convert_fusion) | copy-start | bytes 3538948
  4.8 11.0 %copy-start.11 = (s32[512]{0:T(512)S(1)}, s32[512]{0:T(512)}, u32[]{:S(2)}) copy-start(s32[512]{0:T(512)} %param.15) | copy-start | bytes 6148
  4.8 12.5 %collective-permute-start = (bf16[4,2,32,1152]{3,2,1,0:T(8,128)(2,1)S(1)}, bf16[4,2,32,1152]{3,2,1,0:T(8,128)(2,1)S(1)}, u32[]{:S(2)}, u32[]{:S(2)}) collective-permute-start(bf16[4,2,32,1152]{3,2,1,0:T(8,128)(2,1)S(1)} %dynamic-slice_bitcast_fusion), channel_id=1, source_target_pairs={{0,1},{1,0},{2,3},{3,2},{4,5},{5,4},{6,7},{7,6},{8,9},{9,8},{10,11... | collective-permute-start | bytes 1769480 | tf_op jit(solution)/shard_map/ppermute | solution.py:48
  8.1 38.8 %all-to-all-start = ((bf16[16,32,1152]{2,1,0:T(8,128)(2,1)}), bf16[16,32,1152]{2,1,0:T(8,128)(2,1)S(1)}, u32[]{:S(2)}, u32[]{:S(2)}) async-start(bf16[16,32,1152]{2,1,0:T(8,128)(2,1)} %bitcast.3), calls=%async_computation | async-start | bytes 2359296 | tf_op jit(solution)/shard_map/all_to_all | solution.py:98
  15.8 17.9 %collective-permute-start.11 = (s32[512]{0:T(512)S(1)}, s32[512]{0:T(512)S(1)}, u32[]{:S(2)}, u32[]{:S(2)}) collective-permute-start(s32[512]{0:T(512)S(1)} %copy-done.11), channel_id=1, source_target_pairs={{0,16},{16,0},{1,17},{17,1},{2,18},{18,2},{3,19},{19,3},{4,20},{20... | collective-permute-start | bytes 6152 | tf_op jit(solution)/shard_map/ppermute | solution.py:48
  18.5 22.3 %copy-start.9 = (bf16[32,1152]{1,0:T(8,128)(2,1)S(1)}, bf16[32,1152]{1,0:T(8,128)(2,1)}, u32[]{:S(2)}) copy-start(bf16[32,1152]{1,0:T(8,128)(2,1)} %param.9) | copy-start | bytes 221188
  18.6 5.6 %collective-permute-start.3 = (bf16[2,32,1152]{2,1,0:T(8,128)(2,1)S(1)}, bf16[2,32,1152]{2,1,0:T(8,128)(2,1)S(1)}, u32[]{:S(2)}, u32[]{:S(2)}) collective-permute-start(bf16[2,32,1152]{2,1,0:T(8,128)(2,1)S(1)} %get-tuple-element.58), channel_id=1, source_target_pairs={{0,12},{4,0},{8,4},{12,8},{1,13},{5,1},{9,5},{13,9},{2,14},{6,2},{... | collective-permute-start | bytes 442376 | tf_op jit(solution)/shard_map/ppermute | solution.py:56
  21.4 5.8 %collective-permute-start.2 = (bf16[2,32,1152]{2,1,0:T(8,128)(2,1)S(1)}, bf16[2,32,1152]{2,1,0:T(8,128)(2,1)S(1)}, u32[]{:S(2)}, u32[]{:S(2)}) collective-permute-start(bf16[2,32,1152]{2,1,0:T(8,128)(2,1)S(1)} %get-tuple-element.59), channel_id=1, source_target_pairs={{0,8},{4,12},{8,0},{12,4},{1,9},{5,13},{9,1},{13,5},{2,10},{6,14},... | collective-permute-start | bytes 442376 | tf_op jit(solution)/shard_map/ppermute | solution.py:56
  21.7 9.2 %collective-permute-start.1 = (bf16[2,32,1152]{2,1,0:T(8,128)(2,1)S(1)}, bf16[2,32,1152]{2,1,0:T(8,128)(2,1)S(1)}, u32[]{:S(2)}, u32[]{:S(2)}) collective-permute-start(bf16[2,32,1152]{2,1,0:T(8,128)(2,1)S(1)} %get-tuple-element.57), channel_id=1, source_target_pairs={{0,4},{4,8},{8,12},{12,0},{1,5},{5,9},{9,13},{13,1},{2,6},{6,10},{... | collective-permute-start | bytes 442376 | tf_op jit(solution)/shard_map/ppermute | solution.py:56
  31.1 9.7 %collective-permute-start.4 = (bf16[32,1152]{1,0:T(8,128)(2,1)S(1)}, bf16[32,1152]{1,0:T(8,128)(2,1)S(1)}, u32[]{:S(2)}, u32[]{:S(2)}) collective-permute-start(bf16[32,1152]{1,0:T(8,128)(2,1)S(1)} %dynamic-slice_bitcast_fusion.7), channel_id=1, source_target_pairs={{0,2},{2,0},{1,3},{3,1},{4,6},{6,4},{5,7},{7,5},{8,10},{10,8},{9,1... | collective-permute-start | bytes 221192 | tf_op jit(solution)/shard_map/ppermute | solution.py:48
  33.7 13.3 %copy-start.10 = (bf16[32,1152]{1,0:T(8,128)(2,1)S(1)}, bf16[32,1152]{1,0:T(8,128)(2,1)}, u32[]{:S(2)}) copy-start(bf16[32,1152]{1,0:T(8,128)(2,1)} %param.12) | copy-start | bytes 221188
  40.9 3.6 %collective-permute-start.7 = (bf16[32,1152]{1,0:T(8,128)(2,1)S(1)}, bf16[32,1152]{1,0:T(8,128)(2,1)S(1)}, u32[]{:S(2)}, u32[]{:S(2)}) collective-permute-start(bf16[32,1152]{1,0:T(8,128)(2,1)S(1)} %fusion.14), channel_id=1, source_target_pairs={{0,18},{1,13},{4,22},{5,1},{8,26},{9,5},{12,30},{13,9},{16,0},{17,... | collective-permute-start | bytes 221192 | tf_op jit(solution)/shard_map/ppermute | solution.py:72
  40.9 5.1 %collective-permute-start.6 = (bf16[32,1152]{1,0:T(8,128)(2,1)S(1)}, bf16[32,1152]{1,0:T(8,128)(2,1)S(1)}, u32[]{:S(2)}, u32[]{:S(2)}) collective-permute-start(bf16[32,1152]{1,0:T(8,128)(2,1)S(1)} %fusion.14), channel_id=1, source_target_pairs={{0,2},{1,9},{4,6},{5,13},{8,10},{9,1},{12,14},{13,5},{16,18},{17,2... | collective-permute-start | bytes 221192 | tf_op jit(solution)/shard_map/ppermute | solution.py:72
  41.0 5.8 %collective-permute-start.5 = (bf16[32,1152]{1,0:T(8,128)(2,1)S(1)}, bf16[32,1152]{1,0:T(8,128)(2,1)S(1)}, u32[]{:S(2)}, u32[]{:S(2)}) collective-permute-start(bf16[32,1152]{1,0:T(8,128)(2,1)S(1)} %fusion.14), channel_id=1, source_target_pairs={{0,16},{1,5},{4,20},{5,9},{8,24},{9,13},{12,28},{13,1},{16,2},{17,... | collective-permute-start | bytes 221192 | tf_op jit(solution)/shard_map/ppermute | solution.py:72
  48.0 21.1 %all-to-all-start.1 = ((bf16[8,32,1152]{2,1,0:T(8,128)(2,1)}), bf16[8,32,1152]{2,1,0:T(8,128)(2,1)S(1)}, u32[]{:S(2)}, u32[]{:S(2)}) async-start(bf16[8,32,1152]{2,1,0:T(8,128)(2,1)} %broadcast_in_dim.40), calls=%async_computation.1 | async-start | bytes 1179648 | tf_op jit(solution)/shard_map/all_to_all | solution.py:98
  56.3 5.6 %collective-permute-start.10 = (bf16[4,32,1152]{2,1,0:T(8,128)(2,1)S(1)}, bf16[4,32,1152]{2,1,0:T(8,128)(2,1)S(1)}, u32[]{:S(2)}, u32[]{:S(2)}) collective-permute-start(bf16[4,32,1152]{2,1,0:T(8,128)(2,1)S(1)} %pad_maximum_fusion.2), channel_id=1, source_target_pairs={{0,12},{1,19},{4,0},{5,23},{8,4},{9,27},{12,8},{13,31},{16,28},{17... | collective-permute-start | bytes 884744 | tf_op jit(solution)/shard_map/ppermute | solution.py:72
  56.3 8.0 %collective-permute-start.9 = (bf16[4,32,1152]{2,1,0:T(8,128)(2,1)S(1)}, bf16[4,32,1152]{2,1,0:T(8,128)(2,1)S(1)}, u32[]{:S(2)}, u32[]{:S(2)}) collective-permute-start(bf16[4,32,1152]{2,1,0:T(8,128)(2,1)S(1)} %pad_maximum_fusion.2), channel_id=1, source_target_pairs={{0,8},{1,3},{4,12},{5,7},{8,0},{9,11},{12,4},{13,15},{16,24},{17,1... | collective-permute-start | bytes 884744 | tf_op jit(solution)/shard_map/ppermute | solution.py:72
  60.1 7.6 %collective-permute-start.8 = (bf16[4,32,1152]{2,1,0:T(8,128)(2,1)S(1)}, bf16[4,32,1152]{2,1,0:T(8,128)(2,1)S(1)}, u32[]{:S(2)}, u32[]{:S(2)}) collective-permute-start(bf16[4,32,1152]{2,1,0:T(8,128)(2,1)S(1)} %pad_maximum_fusion.2), channel_id=1, source_target_pairs={{0,4},{1,17},{4,8},{5,21},{8,12},{9,25},{12,0},{13,29},{16,20},{17... | collective-permute-start | bytes 884744 | tf_op jit(solution)/shard_map/ppermute | solution.py:72
  69.1 12.0 %collective-permute-start.12 = (bf16[512,1152]{1,0:T(8,128)(2,1)S(1)}, bf16[512,1152]{1,0:T(8,128)(2,1)}, u32[]{:S(2)}, u32[]{:S(2)}) collective-permute-start(bf16[512,1152]{1,0:T(8,128)(2,1)S(1)} %bitcast.97), channel_id=1, source_target_pairs={{0,1},{1,0},{2,3},{3,2},{4,5},{5,4},{6,7},{7,6},{8,9},{9,8},{10,11... | collective-permute-start | bytes 3538952 | tf_op jit(solution)/shard_map/ppermute | solution.py:48
  86.0 2.8 %collective-permute-start.13 = (bf16[512,1152]{1,0:T(8,128)(2,1)S(1)}, bf16[512,1152]{1,0:T(8,128)(2,1)S(1)}, u32[]{:S(2)}, u32[]{:S(2)}) collective-permute-start(bf16[512,1152]{1,0:T(8,128)(2,1)S(1)} %get-tuple-element.38), channel_id=1, source_target_pairs={{0,1},{1,0},{2,3},{3,2},{4,5},{5,4},{6,7},{7,6},{8,9},{9,8},{10,11... | collective-permute-start | bytes 3538952 | tf_op jit(solution)/shard_map/ppermute | solution.py:48
  89.2 9.3 %collective-permute-start.16 = (bf16[4,32,1152]{2,1,0:T(8,128)(2,1)S(1)}, bf16[4,32,1152]{2,1,0:T(8,128)(2,1)S(1)}, u32[]{:S(2)}, u32[]{:S(2)}) collective-permute-start(bf16[4,32,1152]{2,1,0:T(8,128)(2,1)S(1)} %bitcast.108), channel_id=1, source_target_pairs={{0,4},{1,17},{4,8},{5,21},{8,12},{9,25},{12,0},{13,29},{16,20},{17... | collective-permute-start | bytes 884744 | tf_op jit(solution)/shard_map/ppermute | solution.py:72
  89.3 10.9 %collective-permute-start.15 = (bf16[4,32,1152]{2,1,0:T(8,128)(2,1)S(1)}, bf16[4,32,1152]{2,1,0:T(8,128)(2,1)S(1)}, u32[]{:S(2)}, u32[]{:S(2)}) collective-permute-start(bf16[4,32,1152]{2,1,0:T(8,128)(2,1)S(1)} %bitcast.107), channel_id=1, source_target_pairs={{0,8},{1,3},{4,12},{5,7},{8,0},{9,11},{12,4},{13,15},{16,24},{17,1... | collective-permute-start | bytes 884744 | tf_op jit(solution)/shard_map/ppermute | solution.py:72
  93.0 7.2 %collective-permute-start.14 = (bf16[4,32,1152]{2,1,0:T(8,128)(2,1)S(1)}, bf16[4,32,1152]{2,1,0:T(8,128)(2,1)S(1)}, u32[]{:S(2)}, u32[]{:S(2)}) collective-permute-start(bf16[4,32,1152]{2,1,0:T(8,128)(2,1)S(1)} %bitcast.106), channel_id=1, source_target_pairs={{0,12},{1,19},{4,0},{5,23},{8,4},{9,27},{12,8},{13,31},{16,28},{17... | collective-permute-start | bytes 884744 | tf_op jit(solution)/shard_map/ppermute | solution.py:72
  95.0 22.6 %all-to-all-start.3 = ((bf16[8,32,1152]{2,1,0:T(8,128)(2,1)}), bf16[8,32,1152]{2,1,0:T(8,128)(2,1)S(1)}, u32[]{:S(2)}, u32[]{:S(2)}) async-start(bf16[8,32,1152]{2,1,0:T(8,128)(2,1)} %bitcast.42), calls=%async_computation.3 | async-start | bytes 1179648 | tf_op jit(solution)/shard_map/all_to_all | solution.py:98
  100.4 22.1 %collective-permute-start.19 = (bf16[32,1152]{1,0:T(8,128)(2,1)S(1)}, bf16[32,1152]{1,0:T(8,128)(2,1)S(1)}, u32[]{:S(2)}, u32[]{:S(2)}) collective-permute-start(bf16[32,1152]{1,0:T(8,128)(2,1)S(1)} %get-tuple-element.64), channel_id=1, source_target_pairs={{0,16},{1,5},{4,20},{5,9},{8,24},{9,13},{12,28},{13,1},{16,2},{17,... | collective-permute-start | bytes 221192 | tf_op jit(solution)/shard_map/ppermute | solution.py:72
  101.1 21.5 %collective-permute-start.18 = (bf16[32,1152]{1,0:T(8,128)(2,1)S(1)}, bf16[32,1152]{1,0:T(8,128)(2,1)S(1)}, u32[]{:S(2)}, u32[]{:S(2)}) collective-permute-start(bf16[32,1152]{1,0:T(8,128)(2,1)S(1)} %get-tuple-element.65), channel_id=1, source_target_pairs={{0,2},{1,9},{4,6},{5,13},{8,10},{9,1},{12,14},{13,5},{16,18},{17,2... | collective-permute-start | bytes 221192 | tf_op jit(solution)/shard_map/ppermute | solution.py:72
  103.4 19.2 %collective-permute-start.17 = (bf16[32,1152]{1,0:T(8,128)(2,1)S(1)}, bf16[32,1152]{1,0:T(8,128)(2,1)S(1)}, u32[]{:S(2)}, u32[]{:S(2)}) collective-permute-start(bf16[32,1152]{1,0:T(8,128)(2,1)S(1)} %get-tuple-element.63), channel_id=1, source_target_pairs={{0,18},{1,13},{4,22},{5,1},{8,26},{9,5},{12,30},{13,9},{16,0},{17,... | collective-permute-start | bytes 221192 | tf_op jit(solution)/shard_map/ppermute | solution.py:72
  117.7 1.1 copy-start.4
  118.8 32.0 %all-to-all-start.4 = ((bf16[16,32,1152]{2,1,0:T(8,128)(2,1)}), bf16[16,32,1152]{2,1,0:T(8,128)(2,1)S(1)}, u32[]{:S(2)}, u32[]{:S(2)}) async-start(bf16[16,32,1152]{2,1,0:T(8,128)(2,1)} %broadcast_in_dim.41), calls=%async_computation.4 | async-start | bytes 2359296 | tf_op jit(solution)/shard_map/all_to_all | solution.py:98
  122.6 17.3 %copy-start.5 = (bf16[32,1152]{1,0:T(8,128)(2,1)}, bf16[32,1152]{1,0:T(8,128)(2,1)S(1)}, u32[]{:S(2)}) copy-start(bf16[32,1152]{1,0:T(8,128)(2,1)S(1)} %fusion.12) | copy-start | bytes 221188
  122.7 19.0 %copy-start.7 = (bf16[512,269]{0,1:T(8,128)(2,1)S(1)}, bf16[512,269]{0,1:T(8,128)(2,1)}, u32[]{:S(2)}) copy-start(bf16[512,269]{0,1:T(8,128)(2,1)} %param.10) | copy-start | bytes 826372
  122.7 5.4 %collective-permute-start.20 = (bf16[40,1152]{1,0:T(8,128)(2,1)S(1)}, bf16[40,1152]{1,0:T(8,128)(2,1)S(1)}, u32[]{:S(2)}, u32[]{:S(2)}) collective-permute-start(bf16[40,1152]{1,0:T(8,128)(2,1)S(1)} %get-tuple-element.68), channel_id=1, source_target_pairs={{0,2},{2,0},{1,3},{3,1},{4,6},{6,4},{5,7},{7,5},{8,10},{10,8},{9,1... | collective-permute-start | bytes 276488 | tf_op jit(solution)/shard_map/ppermute | solution.py:48
  128.2 5.2 %collective-permute-start.23 = (bf16[2,40,1152]{2,1,0:T(8,128)(2,1)S(1)}, bf16[2,40,1152]{2,1,0:T(8,128)(2,1)S(1)}, u32[]{:S(2)}, u32[]{:S(2)}) collective-permute-start(bf16[2,40,1152]{2,1,0:T(8,128)(2,1)S(1)} %maximum_select_fusion.1), channel_id=1, source_target_pairs={{0,12},{4,0},{8,4},{12,8},{1,13},{5,1},{9,5},{13,9},{2,14},{6,2},{... | collective-permute-start | bytes 552968 | tf_op jit(solution)/shard_map/ppermute | solution.py:56
  128.9 6.2 %collective-permute-start.22 = (bf16[2,40,1152]{2,1,0:T(8,128)(2,1)S(1)}, bf16[2,40,1152]{2,1,0:T(8,128)(2,1)S(1)}, u32[]{:S(2)}, u32[]{:S(2)}) collective-permute-start(bf16[2,40,1152]{2,1,0:T(8,128)(2,1)S(1)} %maximum_select_fusion.1), channel_id=1, source_target_pairs={{0,8},{4,12},{8,0},{12,4},{1,9},{5,13},{9,1},{13,5},{2,10},{6,14},... | collective-permute-start | bytes 552968 | tf_op jit(solution)/shard_map/ppermute | solution.py:56
  131.2 8.6 %collective-permute-start.21 = (bf16[2,40,1152]{2,1,0:T(8,128)(2,1)S(1)}, bf16[2,40,1152]{2,1,0:T(8,128)(2,1)S(1)}, u32[]{:S(2)}, u32[]{:S(2)}) collective-permute-start(bf16[2,40,1152]{2,1,0:T(8,128)(2,1)S(1)} %maximum_select_fusion.1), channel_id=1, source_target_pairs={{0,4},{4,8},{8,12},{12,0},{1,5},{5,9},{9,13},{13,1},{2,6},{6,10},{... | collective-permute-start | bytes 552968 | tf_op jit(solution)/shard_map/ppermute | solution.py:56
  131.2 10.5 %copy-start.8 = (bf16[512,269]{0,1:T(8,128)(2,1)S(1)}, bf16[512,269]{0,1:T(8,128)(2,1)}, u32[]{:S(2)}) copy-start(bf16[512,269]{0,1:T(8,128)(2,1)} %param.13) | copy-start | bytes 826372
  140.0 3.5 %collective-permute-start.24 = (bf16[4,2,40,1152]{3,2,1,0:T(8,128)(2,1)S(1)}, bf16[4,2,40,1152]{3,2,1,0:T(8,128)(2,1)S(1)}, u32[]{:S(2)}, u32[]{:S(2)}) collective-permute-start(bf16[4,2,40,1152]{3,2,1,0:T(8,128)(2,1)S(1)} %pad_maximum_fusion.1.own), channel_id=1, source_target_pairs={{0,1},{1,0},{2,3},{3,2},{4,5},{5,4},{6,7},{7,6},{8,9},{9,8},{10,11... | collective-permute-start | bytes 2211848 | tf_op jit(solution)/shard_map/ppermute | solution.py:48
  145.7 1.0 copy-start.1
  152.1 7.8 %collective-permute-start.25 = (bf16[4,2,80,256]{3,2,1,0:T(8,128)(2,1)S(1)}, bf16[4,2,80,256]{3,2,1,0:T(8,128)(2,1)S(1)}, u32[]{:S(2)}, u32[]{:S(2)}) collective-permute-start(bf16[4,2,80,256]{3,2,1,0:T(8,128)(2,1)S(1)} %get-tuple-element.45), channel_id=1, source_target_pairs={{0,1},{1,0},{2,3},{3,2},{4,5},{5,4},{6,7},{7,6},{8,9},{9,8},{10,11... | collective-permute-start | bytes 983048 | tf_op jit(solution)/shard_map/ppermute | solution.py:48
  156.3 22.6 %all-to-all-start.2 = ((bf16[16,80,256]{2,1,0:T(8,128)(2,1)}), bf16[16,80,256]{2,1,0:T(8,128)(2,1)S(1)}, u32[]{:S(2)}, u32[]{:S(2)}) async-start(bf16[16,80,256]{2,1,0:T(8,128)(2,1)} %get-tuple-element.40), calls=%async_computation.2 | async-start | bytes 1310720 | tf_op jit(solution)/shard_map/all_to_all | solution.py:98
  159.9 3.0 %copy-start.2 = (bf16[4,2,2,32,1152]{4,3,2,1,0:T(8,128)(2,1)S(1)}, bf16[4,2,2,32,1152]{4,3,2,1,0:T(8,128)(2,1)}, u32[]{:S(2)}) copy-start(bf16[4,2,2,32,1152]{4,3,2,1,0:T(8,128)(2,1)} %copy-done.1) | copy-start | bytes 3538948
  160.0 4.1 %collective-permute-start.28 = (bf16[2,80,256]{2,1,0:T(8,128)(2,1)S(1)}, bf16[2,80,256]{2,1,0:T(8,128)(2,1)S(1)}, u32[]{:S(2)}, u32[]{:S(2)}) collective-permute-start(bf16[2,80,256]{2,1,0:T(8,128)(2,1)S(1)} %get-tuple-element.61), channel_id=1, source_target_pairs={{0,12},{4,0},{8,4},{12,8},{1,13},{5,1},{9,5},{13,9},{2,14},{6,2},{... | collective-permute-start | bytes 245768 | tf_op jit(solution)/shard_map/ppermute | solution.py:56
  160.5 5.2 %collective-permute-start.27 = (bf16[2,80,256]{2,1,0:T(8,128)(2,1)S(1)}, bf16[2,80,256]{2,1,0:T(8,128)(2,1)S(1)}, u32[]{:S(2)}, u32[]{:S(2)}) collective-permute-start(bf16[2,80,256]{2,1,0:T(8,128)(2,1)S(1)} %get-tuple-element.62), channel_id=1, source_target_pairs={{0,8},{4,12},{8,0},{12,4},{1,9},{5,13},{9,1},{13,5},{2,10},{6,14},... | collective-permute-start | bytes 245768 | tf_op jit(solution)/shard_map/ppermute | solution.py:56
  162.9 4.8 %collective-permute-start.26 = (bf16[2,80,256]{2,1,0:T(8,128)(2,1)S(1)}, bf16[2,80,256]{2,1,0:T(8,128)(2,1)S(1)}, u32[]{:S(2)}, u32[]{:S(2)}) collective-permute-start(bf16[2,80,256]{2,1,0:T(8,128)(2,1)S(1)} %get-tuple-element.60), channel_id=1, source_target_pairs={{0,4},{4,8},{8,12},{12,0},{1,5},{5,9},{9,13},{13,1},{2,6},{6,10},{... | collective-permute-start | bytes 245768 | tf_op jit(solution)/shard_map/ppermute | solution.py:56
  162.9 5.5 %copy-start.12 = (bf16[269,1152]{1,0:T(8,128)(2,1)S(1)}, bf16[269,1152]{1,0:T(8,128)(2,1)}, u32[]{:S(2)}) copy-start(bf16[269,1152]{1,0:T(8,128)(2,1)} %param.14) | copy-start | bytes 1859332
  167.7 6.3 %collective-permute-start.29 = (bf16[80,256]{1,0:T(8,128)(2,1)S(1)}, bf16[80,256]{1,0:T(8,128)(2,1)S(1)}, u32[]{:S(2)}, u32[]{:S(2)}) collective-permute-start(bf16[80,256]{1,0:T(8,128)(2,1)S(1)} %get-tuple-element.70), channel_id=1, source_target_pairs={{0,2},{2,0},{1,3},{3,1},{4,6},{6,4},{5,7},{7,5},{8,10},{10,8},{9,1... | collective-permute-start | bytes 122888 | tf_op jit(solution)/shard_map/ppermute | solution.py:48

commit v2 on v1

--- a/solution.py
+++ b/solution.py
@@ -56,54 +56,47 @@
     return lax.ppermute(block, axis, [(i, (i + step) % count) for i in range(count)])
 
 
-def plane_pairs(step, first):
-    pairs = []
-    for x in range(4):
-        for y in range(4):
-            for c in range(2):
-                x2, y2 = ((x + step) % 4, y) if (c == 0) == first else (x, (y + step) % 4)
-                pairs.append(
-                    (((x % 2) * 4 + y) * 4 + (x // 2) * 2 + c, ((x2 % 2) * 4 + y2) * 4 + (x2 // 2) * 2 + c)
-                )
-    return pairs
-
-
-def plane_shift(block, step, first):
-    return lax.ppermute(block, ("xl", "y", "xh", "c"), plane_pairs(step % 4, first))
-
-
-def gather_first(block):
-    return jnp.stack([block] + [plane_shift(block, d, True) for d in (1, 2, 3)])
-
-
-def gather_second(row):
-    return jnp.stack([row] + [plane_shift(row, d, False) for d in (1, 2, 3)])
-
-
-def sum_second(slab):
-    total = slab[0].astype(f32)
+def gather_y(block):
+    return jnp.stack([block] + [shift(block, "y", d) for d in (1, 2, 3)])
+
+
+def sum_y(blocks):
+    total = blocks[0].astype(f32)
     for d in (1, 2, 3):
-        total = total + plane_shift(slab[d], -d, False).astype(f32)
+        total = total + shift(blocks[d], "y", 4 - d).astype(f32)
     return total.astype(bf16)
 
 
-def sum_first(row):
-    total = row[0].astype(f32)
-    for d in (1, 2, 3):
-        total = total + plane_shift(row[d], -d, True).astype(f32)
-    return total.astype(bf16)
+def turn_x(block, a, b):
+    return lax.ppermute(block, ("xl", "xh"), [(i, i ^ (2 * a + b)) for i in range(4)])
 
 
 def exchange(blocks, axis):
     return lax.all_to_all(blocks, axis, 0, 0)
 
 
-def gather(block, axis):
-    return exchange(jnp.broadcast_to(block[None], (lax.axis_size(axis),) + block.shape), axis)
-
-
-def scatter_sum(blocks, axis):
-    return jnp.sum(exchange(blocks, axis).astype(f32), axis=0)
+def spread_kernel(parts, base, row, copies):
+    total = base[...].astype(f32)
+    for k in range(parts.shape[0]):
+        total = total + parts[k].astype(f32)
+    total = total.astype(bf16)
+    row[...] = total
+    for k in range(copies.shape[0]):
+        copies[k] = total
+
+
+def spread_call(parts, base, count):
+    return pl.pallas_call(
+        spread_kernel,
+        out_shape=(
+            jax.ShapeDtypeStruct(base.shape, bf16),
+            jax.ShapeDtypeStruct((count,) + base.shape, bf16),
+        ),
+        in_specs=[VMEM, VMEM],
+        out_specs=(VMEM, VMEM),
+        compiler_params=pltpu.CompilerParams(vmem_limit_bytes=8 * 2**20),
+        name="spread",
+    )(parts, base)
 
 
 CHUNK = 256
@@ -150,8 +143,9 @@
     sums = jnp.sum(loss[...] + more, axis=1, keepdims=True)
     high = sums.astype(bf16).astype(f32)
     lane = lax.broadcasted_iota(jnp.int32, halves.shape, 1)
+    row = lax.broadcasted_iota(jnp.int32, halves.shape, 0)
     values = jnp.where(lane == 0, high, jnp.where(lane == 1, sums - high, 0.0))
-    halves[...] = values.astype(bf16)
+    halves[...] = jnp.where(row == base[1], values, 0.0).astype(bf16)
 
 
 def like(array, dtype):
@@ -169,7 +163,7 @@
         ),
         in_specs=[SMEM, SMEM, VMEM, VMEM, VMEM],
         out_specs=(VMEM, VMEM, VMEM, VMEM),
-        compiler_params=pltpu.CompilerParams(vmem_limit_bytes=24 * 2**20),
+        compiler_params=pltpu.CompilerParams(vmem_limit_bytes=14 * 2**20),
         name="score",
     )(params, base, image, text, labels)
 
@@ -184,7 +178,7 @@
         ),
         in_specs=[SMEM, SMEM, VMEM, VMEM, VMEM, VMEM, VMEM, VMEM],
         out_specs=(VMEM, VMEM, VMEM),
-        compiler_params=pltpu.CompilerParams(vmem_limit_bytes=24 * 2**20),
+        compiler_params=pltpu.CompilerParams(vmem_limit_bytes=14 * 2**20),
         name="score_rest",
     )(params, base, image, text, labels, total, unit, loss)
 
@@ -226,62 +220,67 @@
         ),
         in_specs=[VMEM],
         out_specs=(VMEM, VMEM),
-        compiler_params=pltpu.CompilerParams(vmem_limit_bytes=16 * 2**20),
+        compiler_params=pltpu.CompilerParams(vmem_limit_bytes=6 * 2**20),
         name="finish",
     )(blocks)
     return grad.T, value
 
 
-def weight_kernel(hidden, place, own, other, acts, back, blocks):
+def weight_kernel(hidden, place, own, other, acts, proj, act_grad, blocks, back):
     y, c = place[0], place[1]
     rows, width = back.shape[-2:]
-    loss = jnp.zeros((1, 128), f32)
+    loss = jnp.zeros((8, 128), f32)
     for d in range(4):
         at = lax.rem(y - d + 4, 4)
         for k in range(2):
             back[at, k, c] = own[d, k, :rows]
             back[at, k, 1 - c] = other[d, k, :rows]
             for part in (own, other):
-                loss = loss + part[d, k, rows:].astype(f32)[:1, :128]
-    total = jnp.sum(loss, axis=1, keepdims=True)
+                loss = loss + part[d, k, rows:].astype(f32)[:, :128]
+    total = jnp.sum(jnp.sum(loss, axis=1, keepdims=True), axis=0, keepdims=True)
     high = total.astype(bf16).astype(f32)
-    for k, block in enumerate(packed(back[...].reshape(-1, width), acts, hidden, high, total - high)):
+    grad = back[...].reshape(-1, width)
+    for k, block in enumerate(packed(grad, acts, hidden, high, total - high)):
         blocks[k] = block.astype(bf16)
-
-
-def weight_call(place, own, other, acts, rows, hidden):
-    width = own.shape[-1]
+    act_grad[...] = contract_cols(proj[...], grad).astype(bf16)
+
+
+def weight_call(place, own, other, acts, proj, rows):
+    hidden, width = proj.shape
     return pl.pallas_call(
         functools.partial(weight_kernel, hidden),
         out_shape=(
-            jax.ShapeDtypeStruct((4, 2, 2, rows, width), bf16),
+            jax.ShapeDtypeStruct((hidden, acts.shape[1]), bf16),
             jax.ShapeDtypeStruct((16, width // 16 + 8, 256), bf16),
         ),
-        in_specs=[SMEM, VMEM, VMEM, VMEM],
+        in_specs=[SMEM, VMEM, VMEM, VMEM, VMEM],
         out_specs=(VMEM, VMEM),
-        compiler_params=pltpu.CompilerParams(vmem_limit_bytes=24 * 2**20),
+        scratch_shapes=[pltpu.VMEM((4, 2, 2, rows, width), bf16)],
+        compiler_params=pltpu.CompilerParams(vmem_limit_bytes=16 * 2**20),
         name="image_weight",
-    )(place, own, other, acts)
-
-
-def text_weight_kernel(hidden, place, back, acts, mine, theirs):
+    )(place, own, other, acts, proj)
+
+
+def text_weight_kernel(hidden, place, back, acts, proj, act_grad, mine, theirs):
     blocks = list(packed(back[...], acts, hidden, 0.0, 0.0))
     for k in range(8):
         left, right = blocks[2 * k], blocks[2 * k + 1]
         mine[k // 2, k % 2] = jnp.where(place[1] == 0, left, right).astype(bf16)
         theirs[k // 2, k % 2] = jnp.where(place[1] == 0, right, left).astype(bf16)
-
-
-def text_weight_call(place, back, acts, hidden):
-    shape = jax.ShapeDtypeStruct((4, 2, back.shape[1] // 16 + 8, 256), bf16)
+    act_grad[...] = contract_cols(proj[...], back[...]).astype(bf16)
+
+
+def text_weight_call(place, back, acts, proj):
+    hidden, width = proj.shape
+    shape = jax.ShapeDtypeStruct((4, 2, width // 16 + 8, 256), bf16)
     return pl.pallas_call(
         functools.partial(text_weight_kernel, hidden),
-        out_shape=(shape, shape),
-        in_specs=[SMEM, VMEM, VMEM],
-        out_specs=(VMEM, VMEM),
-        compiler_params=pltpu.CompilerParams(vmem_limit_bytes=24 * 2**20),
+        out_shape=(jax.ShapeDtypeStruct((hidden, acts.shape[1]), bf16), shape, shape),
+        in_specs=[SMEM, VMEM, VMEM, VMEM],
+        out_specs=(VMEM, VMEM, VMEM),
+        compiler_params=pltpu.CompilerParams(vmem_limit_bytes=16 * 2**20),
         name="text_weight",
-    )(place, back, acts)
+    )(place, back, acts, proj)
 
 
 def after(value, done):
@@ -300,15 +299,13 @@
     bias,
 ):
     z, xl, y, xh, c = [lax.axis_index(name) for name in AXES]
-    x = xh * 2 + xl
     rows, width = image_hidden.shape
     hidden = text_proj.shape[0]
     total_rows = rows * 256
     scale = jnp.exp(log_scale[0])
 
     text_parts = dot(text_acts, text_proj).astype(bf16).reshape(16, rows, width)
-    text_sum = scatter_sum(text_parts, IMG)
-    text_embed = (text_hidden.astype(f32) + text_sum).astype(bf16)
+    text_embed, copies = spread_call(exchange(text_parts, IMG), text_hidden, 8)
 
     image_acts = after(image_acts, text_parts)
     parts = dot(image_acts, image_proj).astype(bf16).reshape(4, 2, 2, rows, width)
@@ -316,26 +313,28 @@
     total = pick(parts, y).astype(f32)
     for d in (1, 2, 3):
         total = total + shift(pick(parts, (y + d) % 4), "y", d).astype(f32)
-    total = total.astype(bf16)
-    image_sum = pick(total, xh).astype(f32) + swap(pick(total, 1 - xh), "xh").astype(f32)
-    image_embed = (image_hidden.astype(f32) + image_sum).astype(bf16)
+    here = (jnp.arange(2, dtype=jnp.int32) == xh)[:, None, None]
+    total = (total + jnp.where(here, image_hidden.astype(f32)[None], 0.0)).astype(bf16)
+    image_row = jnp.stack(
+        [
+            total.astype(f32) + turn_x(total, 0, 1).astype(f32),
+            turn_x(total, 1, 0).astype(f32) + turn_x(total, 1, 1).astype(f32),
+        ]
+    ).astype(bf16)
 
     positives_near = swap(positives, "xl")
     labels = pair(positives, positives_near, xl).reshape(2, 4, 2, 2, rows)
     n = jnp.arange(32, dtype=jnp.int32)
     core = jnp.where(n < 16, c, 1 - c)
-    e, d = n // 4 % 4, n % 4
-    from_x = (x - jnp.where(core == 0, d, e)) & 3
-    from_y = (y - jnp.where(core == 0, e, d)) & 3
-    order = (((from_x % 2) * 4 + from_y) * 2 + from_x // 2) * 2 + core
+    from_y = (y - n // 4 % 4) & 3
+    order = (((xl ^ (n // 2 % 2)) * 4 + from_y) * 2 + n % 2) * 2 + core
     labels = jnp.take(labels.reshape(32, rows), order, axis=0).reshape(1, -1)
-    base = jnp.reshape(((y * 2 + xh) * 2 + c) * 512 + xl * rows, (1,)).astype(jnp.int32)
-    image_row = gather_first(image_embed)
-    text_block = gather(after(text_embed, (image_row, labels)), "z").reshape(-1, width)
-    own_block = gather_second(after(image_row, text_embed)).reshape(-1, width)
+    base = jnp.stack([((y * 2 + xh) * 2 + c) * 512 + xl * rows, xl * 2 + xh]).astype(jnp.int32)
+    params = jnp.stack([scale, bias[0]])
+    text_block = exchange(after(copies, (image_row, labels, params, base)), "z").reshape(-1, width)
+    own_block = gather_y(after(image_row, text_embed)).reshape(-1, width)
     near_block = swap(after(own_block, text_block), "c")
 
-    params = jnp.stack([scale, bias[0]])
     half = 16 * rows
     text_total, text_unit, mine, losses = score_call(
         params, base, own_block, text_block, labels[:, :half]
@@ -343,24 +342,33 @@
     text_parts, theirs, halves = rest_call(
         params, base, near_block, text_block, labels[:, half:], text_total, text_unit, losses
     )
-    text_grad = scatter_sum(text_parts.reshape(8, rows, width), "z").astype(bf16)
+    text_grad, copies = spread_call(
+        exchange(text_parts.reshape(8, rows, width), "z"), jnp.zeros((rows, width), bf16), 16
+    )
     theirs = swap(theirs, "c")
     slab = (mine.astype(f32) + theirs.astype(f32)).astype(bf16)
-    image_row = sum_second(slab.reshape(4, 4, rows, width))
-    image_grad = sum_first(image_row)
-
-    near = jnp.concatenate([image_grad, halves])
-    near = pair(near, swap(near, "xh"), xh)
-    ring = jnp.stack([near] + [shift(near, "y", d) for d in (1, 2, 3)])
+    image_row = sum_y(slab.reshape(4, 4, rows, width)).reshape(2, 2, rows, width)
+
+    image_row = after(image_row, text_grad)
+    halves = jnp.broadcast_to(halves, (2, 2) + halves.shape)
+    image_row = jnp.concatenate([image_row, halves], axis=2)
+    near = image_row[0].astype(f32) + turn_x(image_row[0], 0, 1).astype(f32)
+    near = near + turn_x(image_row[1], 1, 0).astype(f32) + turn_x(image_row[1], 1, 1).astype(f32)
+    near = near.astype(bf16)
+    image_grad = pick(near, xh)[:rows]
+    ring = gather_y(near)
     place = jnp.stack([y, c]).astype(jnp.int32)
     wide = ((0, 272 - hidden), (0, 0))
-    image_back, blocks = weight_call(place, ring, swap(ring, "c"), jnp.pad(image_acts.T, wide), rows, hidden)
-    image_back = image_back.reshape(-1, width)
+    image_act_grad, blocks = weight_call(
+        place, ring, swap(ring, "c"), jnp.pad(image_acts.T, wide), image_proj, rows
+    )
     found = exchange(blocks, IMG)
 
-    text_back = gather(after(text_grad, image_row), IMG).reshape(-1, width)
+    text_back = exchange(after(copies, image_row), IMG).reshape(-1, width)
     text_back = after(text_back, blocks)
-    mine, theirs = text_weight_call(place, text_back, jnp.pad(text_acts.T, wide), hidden)
+    text_act_grad, mine, theirs = text_weight_call(
+        place, text_back, jnp.pad(text_acts.T, wide), text_proj
+    )
     parts = (mine.astype(f32) + swap(theirs, "c").astype(f32)).astype(bf16)
     total = pick(parts, y).astype(f32)
     for d in (1, 2, 3):
@@ -368,18 +376,15 @@
     total = total.astype(bf16)
     last = jnp.stack([pick(total, xh), swap(pick(total, 1 - xh), "xh")])
 
-    image_act_grad = contract_cols(after(image_back, parts), image_proj).astype(bf16)
-    text_act_grad = contract_cols(after(text_back, parts), text_proj).astype(bf16)
-
     text_proj_grad = finish_call(last, hidden)[0]
     image_proj_grad, total_loss = finish_call(after(found, last), hidden)
-    loss = jnp.reshape(total_loss / total_rows, (1,))
+    loss = jnp.reshape(0.25 * total_loss / total_rows, (1,))
     return (
         loss,
         image_grad,
         text_grad,
-        image_act_grad,
-        text_act_grad,
+        image_act_grad.T,
+        text_act_grad.T,
         image_proj_grad,
         text_proj_grad,
     )

time: 183 us -> 176 us (0.962)
  starting transfers between devices: 72.5 us -> 55.5 us
  waiting for transfers between devices: 77.7 us -> 88.1 us
  Pallas kernels: 13.3 us -> 16.6 us
  matrix products: 6.54 us -> 4.02 us
  local copies, waits for them, and re-layouts: 4.16 us -> 1.72 us
    ppermute x9 -> x15, waiting for transfers between devices: 20.6 us -> 40.1 us  [shift(): lax.ppermute(block, axis, [(i, (i + step) % count) for i in range(count)])]
    ppermute x9 -> x7, waiting for transfers between devices: 20.7 us -> 3.38 us  [swap(): return lax.ppermute(block, axis, SWAP)]
    ppermute x9 -> x7, starting transfers between devices: 21 us -> 11 us  [swap(): return lax.ppermute(block, axis, SWAP)]
    ppermute x12 -> x6, waiting for transfers between devices: 12.7 us -> 22.5 us  [turn_x(): lax.ppermute(block, ('xl', 'xh'), [(i, i ^ 2 * a + b) for i in range(4)])]
    ppermute x12 -> x6, starting transfers between devices: 15 us -> 6.83 us  [turn_x(): lax.ppermute(block, ('xl', 'xh'), [(i, i ^ 2 * a + b) for i in range(4)])]
    dot_general x2 -> x0, matrix products: 2.54 us -> none  [contract_cols(): lax.dot_general(left, right, (((1,), (1,)), ((), ())), preferred_element_...]
    pallas_call x0 -> x2, Pallas kernels: none -> 2.22 us  [spread_call(): pl.pallas_call(spread_kernel, out_shape=(jax.ShapeDtypeStruct(base.shape,...]
    broadcast_in_dim x2, local copies, waits for them, and re-layouts: 2.01 us -> 0.02 us  [the longest x1 0.01 us: on_device(): jnp.zeros((rows, width), bf16)]
  transfers between devices with their start and end apart: 35 -> 33, of which waited for: 24 -> 22; matrix products, arithmetic and copies ran while one was open for 4% -> 3% of each run, Pallas kernels for 4% -> 4%
where the time goes in v2:
time: 176 us; the launch traced here: 174 us
  waiting for transfers between devices  88.1 us (50%)
  starting transfers between devices  55.5 us (32%)
  Pallas kernels  16.6 us (9%)
  between operations  4.16 us (2%)
  other arithmetic  4.11 us (2%)
  matrix products  4.02 us (2%)
    ppermute x15, waiting for transfers between devices, shift(): lax.ppermute(block, axis, [(i, (i + step) % count) for i in range(count)])  40.1 us
    all_to_all x5, starting transfers between devices, exchange(): return lax.all_to_all(blocks, axis, 0, 0)  26.2 us
    ppermute x6, waiting for transfers between devices, turn_x(): lax.ppermute(block, ('xl', 'xh'), [(i, i ^ 2 * a + b) for i in range(4)])  22.5 us
    all_to_all x5, waiting for transfers between devices, exchange(): return lax.all_to_all(blocks, axis, 0, 0)  22.1 us
    ppermute x15, starting transfers between devices, shift(): lax.ppermute(block, axis, [(i, (i + step) % count) for i in range(count)])  11.5 us
    ppermute x7, starting transfers between devices, swap(): return lax.ppermute(block, axis, SWAP)  11 us
    ppermute x6, starting transfers between devices, turn_x(): lax.ppermute(block, ('xl', 'xh'), [(i, i ^ 2 * a + b) for i in range(4)])  6.83 us
    pallas_call x1, Pallas kernels, rest_call(): pl.pallas_call(rest_kernel, out_shape=(like(text, bf16), like(image, bf16...  4.7 us
  transfers between devices with their start and end apart: 33, of which 22 were waited for; matrix products, arithmetic and copies ran while one was open for 3% of the time, Pallas kernels for 4%

profile of v2, /device:TPU:1, one launch (start us, length us, event | category | flops | bytes accessed | tf_op | source)
XLA Modules:
  0.0 174.2 jit_solution(10781771880198303210)
XLA Ops:
  0.7 3.2 %convolution_convert_fusion.1 = bf16[512,1152]{1,0:T(8,128)(2,1)} fusion(bf16[512,269]{0,1:T(8,128)(2,1)} %param.13, bf16[269,1152]{1,0:T(8,128)(2,1)} %proj.3), kind=kOutput, calls=%fused_computation.2 | convolution fusion | flops 317915136 | bytes 2074880 | tf_op jit(solution)/shard_map/dot_general | solution.py:32
  4.8 3.3 %collective-permute-start = (bf16[4,2,32,1152]{3,2,1,0:T(8,128)(2,1)S(1)}, bf16[4,2,32,1152]{3,2,1,0:T(8,128)(2,1)S(1)}, u32[]{:S(2)}, u32[]{:S(2)}) collective-permute-start(bf16[4,2,32,1152]{3,2,1,0:T(8,128)(2,1)S(1)} %dynamic-slice_bitcast_fusion), channel_id=1, source_target_pairs={{0,1},{1,0},{2,3},{3,2},{4,5},{5,4},{6,7},{7,6},{8,9},{9,8},{10,11... | collective-permute-start | bytes 1769480 | tf_op jit(solution)/shard_map/ppermute | solution.py:48
  8.1 7.7 %all-to-all-start = ((bf16[16,32,1152]{2,1,0:T(8,128)(2,1)}), bf16[16,32,1152]{2,1,0:T(8,128)(2,1)S(1)}, u32[]{:S(2)}, u32[]{:S(2)}) async-start(bf16[16,32,1152]{2,1,0:T(8,128)(2,1)} %bitcast.4), calls=%async_computation | async-start | bytes 2359296 | tf_op jit(solution)/shard_map/all_to_all | solution.py:75
  15.8 1.4 collective-permute-start.10
  18.7 1.3 fusion
  20.1 2.8 %collective-permute-start.3 = (bf16[2,32,1152]{2,1,0:T(8,128)(2,1)S(1)}, bf16[2,32,1152]{2,1,0:T(8,128)(2,1)S(1)}, u32[]{:S(2)}, u32[]{:S(2)}) collective-permute-start(bf16[2,32,1152]{2,1,0:T(8,128)(2,1)S(1)} %get-tuple-element.62), channel_id=1, source_target_pairs={{0,12},{4,0},{8,4},{12,8},{1,13},{5,1},{9,5},{13,9},{2,14},{6,2},{... | collective-permute-start | bytes 442376 | tf_op jit(solution)/shard_map/ppermute | solution.py:56
  24.7 0.9 collective-permute-done.3
  25.6 3.0 %collective-permute-done.2 = bf16[2,32,1152]{2,1,0:T(8,128)(2,1)S(1)} collective-permute-done((bf16[2,32,1152]{2,1,0:T(8,128)(2,1)S(1)}, bf16[2,32,1152]{2,1,0:T(8,128)(2,1)S(1)}, u32[]{:S(2)}, u32[]{:S(2)}) %collective-permute-start.2) | collective-permute-done | bytes 147488 | tf_op jit(solution)/shard_map/ppermute | solution.py:56
  28.7 3.8 %collective-permute-done.1 = bf16[2,32,1152]{2,1,0:T(8,128)(2,1)S(1)} collective-permute-done((bf16[2,32,1152]{2,1,0:T(8,128)(2,1)S(1)}, bf16[2,32,1152]{2,1,0:T(8,128)(2,1)S(1)}, u32[]{:S(2)}, u32[]{:S(2)}) %collective-permute-start.1) | collective-permute-done | bytes 147488 | tf_op jit(solution)/shard_map/ppermute | solution.py:56
  32.6 2.5 %collective-permute-start.4 = (bf16[2,32,1152]{2,1,0:T(8,128)(2,1)S(1)}, bf16[2,32,1152]{2,1,0:T(8,128)(2,1)S(1)}, u32[]{:S(2)}, u32[]{:S(2)}) collective-permute-start(bf16[2,32,1152]{2,1,0:T(8,128)(2,1)S(1)} %fusion.7), channel_id=1, source_target_pairs={{0,2},{2,0},{16,18},{18,16},{1,3},{3,1},{17,19},{19,17},{4,6},{6,4... | collective-permute-start | bytes 442376 | tf_op jit(solution)/shard_map/ppermute | solution.py:71
  35.6 9.1 %collective-permute-done.4 = bf16[2,32,1152]{2,1,0:T(8,128)(2,1)S(1)} collective-permute-done((bf16[2,32,1152]{2,1,0:T(8,128)(2,1)S(1)}, bf16[2,32,1152]{2,1,0:T(8,128)(2,1)S(1)}, u32[]{:S(2)}, u32[]{:S(2)}) %collective-permute-start.4) | collective-permute-done | bytes 147488 | tf_op jit(solution)/shard_map/ppermute | solution.py:71
  44.8 5.2 %collective-permute-done.5 = bf16[2,32,1152]{2,1,0:T(8,128)(2,1)S(1)} collective-permute-done((bf16[2,32,1152]{2,1,0:T(8,128)(2,1)S(1)}, bf16[2,32,1152]{2,1,0:T(8,128)(2,1)S(1)}, u32[]{:S(2)}, u32[]{:S(2)}) %collective-permute-start.5) | collective-permute-done | bytes 147488 | tf_op jit(solution)/shard_map/ppermute | solution.py:71
  50.1 1.0 spread.2
  51.1 6.0 %all-to-all-start.1 = ((bf16[8,32,1152]{2,1,0:T(8,128)(2,1)}), bf16[8,32,1152]{2,1,0:T(8,128)(2,1)S(1)}, u32[]{:S(2)}, u32[]{:S(2)}) async-start(bf16[8,32,1152]{2,1,0:T(8,128)(2,1)} %get-tuple-element.34), calls=%async_computation.1 | async-start | bytes 1179648 | tf_op jit(solution)/shard_map/all_to_all | solution.py:75
  57.2 1.4 collective-permute-start.7
  58.6 6.2 %collective-permute-done.9 = bf16[2,2,32,1152]{3,2,1,0:T(8,128)(2,1)S(1)} collective-permute-done((bf16[2,2,32,1152]{3,2,1,0:T(8,128)(2,1)S(1)}, bf16[2,2,32,1152]{3,2,1,0:T(8,128)(2,1)S(1)}, u32[]{:S(2)}, u32[]{:S(2)}) %collective-permute-start.9) | collective-permute-done | bytes 294944 | tf_op jit(solution)/shard_map/ppermute | solution.py:56
  64.7 1.0 collective-permute-done.8
  65.7 8.2 %collective-permute-done.7 = bf16[2,2,32,1152]{3,2,1,0:T(8,128)(2,1)S(1)} collective-permute-done((bf16[2,2,32,1152]{3,2,1,0:T(8,128)(2,1)S(1)}, bf16[2,2,32,1152]{3,2,1,0:T(8,128)(2,1)S(1)}, u32[]{:S(2)}, u32[]{:S(2)}) %collective-permute-start.7) | collective-permute-done | bytes 294944 | tf_op jit(solution)/shard_map/ppermute | solution.py:56
  74.1 2.3 %all-to-all-done.1 = bf16[8,32,1152]{2,1,0:T(8,128)(2,1)S(1)} async-done(((bf16[8,32,1152]{2,1,0:T(8,128)(2,1)}), bf16[8,32,1152]{2,1,0:T(8,128)(2,1)S(1)}, u32[]{:S(2)}, u32[]{:S(2)}) %all-to-all-start.1) | async-done | bytes 589856 | tf_op jit(solution)/shard_map/all_to_all | solution.py:75
  77.0 3.4 %score.1 = (f32[256,1152]{1,0:T(8,128)S(1)}, bf16[256,1152]{1,0:T(8,128)(2,1)S(1)}, bf16[512,1152]{1,0:T(8,128)(2,1)S(1)}, f32[1,256]{1,0:T(1,128)S(1)}) custom-call(f32[2]{0:T(128)S(1)} %pad_maximum_fusion.5.params, s32[2]{0:T(128)S(1)} %pad_add_fusion.1.base, bf16[512,1152]{1,0:T(8,128)(2,1)S(1)} %bitcast.83, bf16[256,1152]{1,0:T(8,128)(2,1)S(1)} %bitcast.79, ...), custom_call_target="tpu_custom_call" | custom-call | tf_op jit(solution)/shard_map/score/pallas_call | solution.py:156
  80.4 4.7 %score_rest.1 = (bf16[256,1152]{1,0:T(8,128)(2,1)}, bf16[512,1152]{1,0:T(8,128)(2,1)}, bf16[8,1152]{1,0:T(8,128)(2,1)S(1)}) custom-call(f32[2]{0:T(128)S(1)} %pad_maximum_fusion.5.params, s32[2]{0:T(128)S(1)} %pad_add_fusion.1.base, bf16[512,1152]{1,0:T(8,128)(2,1)S(1)} %collective-permute-done.11.image, bf16[256,1152]{1,0:T(8,128)(2,1)S(1)} %bitcast.80, ...), custom_call_target="tpu_custom_call" | custom-call | tf_op jit(solution)/shard_map/score_rest/pallas_call | solution.py:172
  85.2 4.5 %all-to-all-start.2 = ((bf16[8,32,1152]{2,1,0:T(8,128)(2,1)}), bf16[8,32,1152]{2,1,0:T(8,128)(2,1)S(1)}, u32[]{:S(2)}, u32[]{:S(2)}) async-start(bf16[8,32,1152]{2,1,0:T(8,128)(2,1)} %bitcast.28), calls=%async_computation.2 | async-start | bytes 1179648 | tf_op jit(solution)/shard_map/all_to_all | solution.py:75
  89.7 1.5 add_convert_fusion
  91.4 2.1 %collective-permute-start.14 = (bf16[4,32,1152]{2,1,0:T(8,128)(2,1)S(1)}, bf16[4,32,1152]{2,1,0:T(8,128)(2,1)S(1)}, u32[]{:S(2)}, u32[]{:S(2)}) collective-permute-start(bf16[4,32,1152]{2,1,0:T(8,128)(2,1)S(1)} %bitcast.92), channel_id=1, source_target_pairs={{0,8},{4,12},{8,0},{12,4},{1,9},{5,13},{9,1},{13,5},{2,10},{6,14},... | collective-permute-start | bytes 884744 | tf_op jit(solution)/shard_map/ppermute | solution.py:56
  94.1 14.9 %all-to-all-done.2.parts = bf16[8,32,1152]{2,1,0:T(8,128)(2,1)S(1)} async-done(((bf16[8,32,1152]{2,1,0:T(8,128)(2,1)}), bf16[8,32,1152]{2,1,0:T(8,128)(2,1)S(1)}, u32[]{:S(2)}, u32[]{:S(2)}) %all-to-all-start.2) | async-done | bytes 589856 | tf_op jit(solution)/shard_map/all_to_all | solution.py:75
  109.0 1.2 spread.3
  110.2 3.7 %all-to-all-start.4 = ((bf16[16,32,1152]{2,1,0:T(8,128)(2,1)}), bf16[16,32,1152]{2,1,0:T(8,128)(2,1)S(1)}, u32[]{:S(2)}, u32[]{:S(2)}) async-start(bf16[16,32,1152]{2,1,0:T(8,128)(2,1)} %get-tuple-element.47), calls=%async_computation.4 | async-start | bytes 2359296 | tf_op jit(solution)/shard_map/all_to_all | solution.py:75
  114.2 2.2 %collective-permute-start.18 = (bf16[2,40,1152]{2,1,0:T(8,128)(2,1)S(1)}, bf16[2,40,1152]{2,1,0:T(8,128)(2,1)S(1)}, u32[]{:S(2)}, u32[]{:S(2)}) collective-permute-start(bf16[2,40,1152]{2,1,0:T(8,128)(2,1)S(1)} %get-tuple-element.65), channel_id=1, source_target_pairs={{0,18},{2,16},{16,2},{18,0},{1,19},{3,17},{17,3},{19,1},{4,22},{6,... | collective-permute-start | bytes 552968 | tf_op jit(solution)/shard_map/ppermute | solution.py:71
  116.4 1.8 %collective-permute-start.16 = (bf16[2,40,1152]{2,1,0:T(8,128)(2,1)S(1)}, bf16[2,40,1152]{2,1,0:T(8,128)(2,1)S(1)}, u32[]{:S(2)}, u32[]{:S(2)}) collective-permute-start(bf16[2,40,1152]{2,1,0:T(8,128)(2,1)S(1)} %get-tuple-element.64), channel_id=1, source_target_pairs={{0,2},{2,0},{16,18},{18,16},{1,3},{3,1},{17,19},{19,17},{4,6},{6,4... | collective-permute-start | bytes 552968 | tf_op jit(solution)/shard_map/ppermute | solution.py:71
  118.1 3.1 %collective-permute-done.18 = bf16[2,40,1152]{2,1,0:T(8,128)(2,1)S(1)} collective-permute-done((bf16[2,40,1152]{2,1,0:T(8,128)(2,1)S(1)}, bf16[2,40,1152]{2,1,0:T(8,128)(2,1)S(1)}, u32[]{:S(2)}, u32[]{:S(2)}) %collective-permute-start.18) | collective-permute-done | bytes 184352 | tf_op jit(solution)/shard_map/ppermute | solution.py:71
  121.4 4.9 %collective-permute-done.16 = bf16[2,40,1152]{2,1,0:T(8,128)(2,1)S(1)} collective-permute-done((bf16[2,40,1152]{2,1,0:T(8,128)(2,1)S(1)}, bf16[2,40,1152]{2,1,0:T(8,128)(2,1)S(1)}, u32[]{:S(2)}, u32[]{:S(2)}) %collective-permute-start.16) | collective-permute-done | bytes 184352 | tf_op jit(solution)/shard_map/ppermute | solution.py:71
  126.4 1.0 collective-permute-start.21
  127.4 0.9 collective-permute-start.19
  128.3 2.8 %collective-permute-done.21 = bf16[2,40,1152]{2,1,0:T(8,128)(2,1)S(1)} collective-permute-done((bf16[2,40,1152]{2,1,0:T(8,128)(2,1)S(1)}, bf16[2,40,1152]{2,1,0:T(8,128)(2,1)S(1)}, u32[]{:S(2)}, u32[]{:S(2)}) %collective-permute-start.21) | collective-permute-done | bytes 184352 | tf_op jit(solution)/shard_map/ppermute | solution.py:56
  131.2 2.3 %collective-permute-done.20 = bf16[2,40,1152]{2,1,0:T(8,128)(2,1)S(1)} collective-permute-done((bf16[2,40,1152]{2,1,0:T(8,128)(2,1)S(1)}, bf16[2,40,1152]{2,1,0:T(8,128)(2,1)S(1)}, u32[]{:S(2)}, u32[]{:S(2)}) %collective-permute-start.20) | collective-permute-done | bytes 184352 | tf_op jit(solution)/shard_map/ppermute | solution.py:56
  133.4 5.4 %collective-permute-done.19 = bf16[2,40,1152]{2,1,0:T(8,128)(2,1)S(1)} collective-permute-done((bf16[2,40,1152]{2,1,0:T(8,128)(2,1)S(1)}, bf16[2,40,1152]{2,1,0:T(8,128)(2,1)S(1)}, u32[]{:S(2)}, u32[]{:S(2)}) %collective-permute-start.19) | collective-permute-done | bytes 184352 | tf_op jit(solution)/shard_map/ppermute | solution.py:56
  139.0 1.1 collective-permute-start.22
  140.2 1.7 collective-permute-done.22.other
  141.9 2.4 %image_weight.1 = (bf16[269,512]{1,0:T(8,128)(2,1)}, bf16[16,80,256]{2,1,0:T(8,128)(2,1)}) custom-call(s32[2]{0:T(128)S(1)} %pad_add_fusion.place, bf16[4,2,40,1152]{3,2,1,0:T(8,128)(2,1)S(1)} %pad_maximum_fusion.1.own, bf16[4,2,40,1152]{3,2,1,0:T(8,128)(2,1)S(1)} %collective-permute-done.22.other, bf16[272,512]{1,0:T(8,128)(2,1)S(1)} %pad.7.acts, ...), custom_call_target="tpu_custom_call" | custom-call | tf_op jit(solution)/shard_map/image_weight/pallas_call | solution.py:250
  144.3 2.3 %text_weight.1 = (bf16[269,512]{1,0:T(8,128)(2,1)}, bf16[4,2,80,256]{3,2,1,0:T(8,128)(2,1)S(1)}, bf16[4,2,80,256]{3,2,1,0:T(8,128)(2,1)S(1)}) custom-call(s32[2]{0:T(128)S(1)} %pad_add_fusion.place, bf16[512,1152]{1,0:T(8,128)(2,1)S(1)} %bitcast.81, bf16[272,512]{1,0:T(8,128)(2,1)S(1)} %pad.8.acts, bf16[269,1152]{1,0:T(8,128)(2,1)S(1)} %copy-done), custom_call_target="tpu_custom_call" | custom-call | tf_op jit(solution)/shard_map/text_weight/pallas_call | solution.py:276
  146.6 2.0 %collective-permute-start.23 = (bf16[4,2,80,256]{3,2,1,0:T(8,128)(2,1)S(1)}, bf16[4,2,80,256]{3,2,1,0:T(8,128)(2,1)S(1)}, u32[]{:S(2)}, u32[]{:S(2)}) collective-permute-start(bf16[4,2,80,256]{3,2,1,0:T(8,128)(2,1)S(1)} %get-tuple-element.50), channel_id=1, source_target_pairs={{0,1},{1,0},{2,3},{3,2},{4,5},{5,4},{6,7},{7,6},{8,9},{9,8},{10,11... | collective-permute-start | bytes 983048 | tf_op jit(solution)/shard_map/ppermute | solution.py:48
  148.7 4.4 %all-to-all-start.3 = ((bf16[16,80,256]{2,1,0:T(8,128)(2,1)}), bf16[16,80,256]{2,1,0:T(8,128)(2,1)S(1)}, u32[]{:S(2)}, u32[]{:S(2)}) async-start(bf16[16,80,256]{2,1,0:T(8,128)(2,1)} %get-tuple-element.45), calls=%async_computation.3 | async-start | bytes 1310720 | tf_op jit(solution)/shard_map/all_to_all | solution.py:75
  154.8 2.1 %collective-permute-done.26 = bf16[2,80,256]{2,1,0:T(8,128)(2,1)S(1)} collective-permute-done((bf16[2,80,256]{2,1,0:T(8,128)(2,1)S(1)}, bf16[2,80,256]{2,1,0:T(8,128)(2,1)S(1)}, u32[]{:S(2)}, u32[]{:S(2)}) %collective-permute-start.26) | collective-permute-done | bytes 81952 | tf_op jit(solution)/shard_map/ppermute | solution.py:56
  156.9 1.7 %collective-permute-done.25 = bf16[2,80,256]{2,1,0:T(8,128)(2,1)S(1)} collective-permute-done((bf16[2,80,256]{2,1,0:T(8,128)(2,1)S(1)}, bf16[2,80,256]{2,1,0:T(8,128)(2,1)S(1)}, u32[]{:S(2)}, u32[]{:S(2)}) %collective-permute-start.25) | collective-permute-done | bytes 81952 | tf_op jit(solution)/shard_map/ppermute | solution.py:56
  158.6 2.5 %collective-permute-done.24 = bf16[2,80,256]{2,1,0:T(8,128)(2,1)S(1)} collective-permute-done((bf16[2,80,256]{2,1,0:T(8,128)(2,1)S(1)}, bf16[2,80,256]{2,1,0:T(8,128)(2,1)S(1)}, u32[]{:S(2)}, u32[]{:S(2)}) %collective-permute-start.24) | collective-permute-done | bytes 81952 | tf_op jit(solution)/shard_map/ppermute | solution.py:56
  161.3 2.5 %collective-permute-start.27 = (bf16[80,256]{1,0:T(8,128)(2,1)S(1)}, bf16[80,256]{1,0:T(8,128)(2,1)S(1)}, u32[]{:S(2)}, u32[]{:S(2)}) collective-permute-start(bf16[80,256]{1,0:T(8,128)(2,1)S(1)} %get-tuple-element.70), channel_id=1, source_target_pairs={{0,2},{2,0},{1,3},{3,1},{4,6},{6,4},{5,7},{7,5},{8,10},{10,8},{9,1... | collective-permute-start | bytes 122888 | tf_op jit(solution)/shard_map/ppermute | solution.py:48
  164.4 1.7 collective-permute-done.27
  166.8 4.8 %all-to-all-done.3.blocks = bf16[16,80,256]{2,1,0:T(8,128)(2,1)S(1)} async-done(((bf16[16,80,256]{2,1,0:T(8,128)(2,1)}), bf16[16,80,256]{2,1,0:T(8,128)(2,1)S(1)}, u32[]{:S(2)}, u32[]{:S(2)}) %all-to-all-start.3) | async-done | bytes 655392 | tf_op jit(solution)/shard_map/all_to_all | solution.py:75
  (86 shorter events, 9.9 us)
Async XLA Ops:
  0.6 3.2 %copy-start.5 = (bf16[512,269]{0,1:T(8,128)(2,1)S(1)}, bf16[512,269]{0,1:T(8,128)(2,1)}, u32[]{:S(2)}) copy-start(bf16[512,269]{0,1:T(8,128)(2,1)} %param.10) | copy-start | bytes 826372
  0.6 3.2 %copy-start.1 = (bf16[269,1152]{1,0:T(8,128)(2,1)S(1)}, bf16[269,1152]{1,0:T(8,128)(2,1)}, u32[]{:S(2)}) copy-start(bf16[269,1152]{1,0:T(8,128)(2,1)} %proj.2) | copy-start | bytes 1859332
  4.7 3.4 %copy-start.4 = (bf16[512,1152]{1,0:T(8,128)(2,1)}, bf16[512,1152]{1,0:T(8,128)(2,1)S(1)}, u32[]{:S(2)}) copy-start(bf16[512,1152]{1,0:T(8,128)(2,1)S(1)} %convolution_convert_fusion) | copy-start | bytes 3538948
  4.8 11.0 %copy-start.9 = (s32[512]{0:T(512)S(1)}, s32[512]{0:T(512)}, u32[]{:S(2)}) copy-start(s32[512]{0:T(512)} %param.15) | copy-start | bytes 6148
  4.8 14.0 %collective-permute-start = (bf16[4,2,32,1152]{3,2,1,0:T(8,128)(2,1)S(1)}, bf16[4,2,32,1152]{3,2,1,0:T(8,128)(2,1)S(1)}, u32[]{:S(2)}, u32[]{:S(2)}) collective-permute-start(bf16[4,2,32,1152]{3,2,1,0:T(8,128)(2,1)S(1)} %dynamic-slice_bitcast_fusion), channel_id=1, source_target_pairs={{0,1},{1,0},{2,3},{3,2},{4,5},{5,4},{6,7},{7,6},{8,9},{9,8},{10,11... | collective-permute-start | bytes 1769480 | tf_op jit(solution)/shard_map/ppermute | solution.py:48
  8.1 42.0 %all-to-all-start = ((bf16[16,32,1152]{2,1,0:T(8,128)(2,1)}), bf16[16,32,1152]{2,1,0:T(8,128)(2,1)S(1)}, u32[]{:S(2)}, u32[]{:S(2)}) async-start(bf16[16,32,1152]{2,1,0:T(8,128)(2,1)} %bitcast.4), calls=%async_computation | async-start | bytes 2359296 | tf_op jit(solution)/shard_map/all_to_all | solution.py:75
  15.8 8.2 %collective-permute-start.10 = (s32[512]{0:T(512)S(1)}, s32[512]{0:T(512)S(1)}, u32[]{:S(2)}, u32[]{:S(2)}) collective-permute-start(s32[512]{0:T(512)S(1)} %copy-done.9), channel_id=1, source_target_pairs={{0,16},{16,0},{1,17},{17,1},{2,18},{18,2},{3,19},{19,3},{4,20},{20... | collective-permute-start | bytes 6152 | tf_op jit(solution)/shard_map/ppermute | solution.py:48
  18.7 5.2 %copy-start.8 = (bf16[32,1152]{1,0:T(8,128)(2,1)S(1)}, bf16[32,1152]{1,0:T(8,128)(2,1)}, u32[]{:S(2)}) copy-start(bf16[32,1152]{1,0:T(8,128)(2,1)} %param.9) | copy-start | bytes 221188
  20.1 5.6 %collective-permute-start.3 = (bf16[2,32,1152]{2,1,0:T(8,128)(2,1)S(1)}, bf16[2,32,1152]{2,1,0:T(8,128)(2,1)S(1)}, u32[]{:S(2)}, u32[]{:S(2)}) collective-permute-start(bf16[2,32,1152]{2,1,0:T(8,128)(2,1)S(1)} %get-tuple-element.62), channel_id=1, source_target_pairs={{0,12},{4,0},{8,4},{12,8},{1,13},{5,1},{9,5},{13,9},{2,14},{6,2},{... | collective-permute-start | bytes 442376 | tf_op jit(solution)/shard_map/ppermute | solution.py:56
  22.9 5.8 %collective-permute-start.2 = (bf16[2,32,1152]{2,1,0:T(8,128)(2,1)S(1)}, bf16[2,32,1152]{2,1,0:T(8,128)(2,1)S(1)}, u32[]{:S(2)}, u32[]{:S(2)}) collective-permute-start(bf16[2,32,1152]{2,1,0:T(8,128)(2,1)S(1)} %get-tuple-element.63), channel_id=1, source_target_pairs={{0,8},{4,12},{8,0},{12,4},{1,9},{5,13},{9,1},{13,5},{2,10},{6,14},... | collective-permute-start | bytes 442376 | tf_op jit(solution)/shard_map/ppermute | solution.py:56
  23.2 9.2 %collective-permute-start.1 = (bf16[2,32,1152]{2,1,0:T(8,128)(2,1)S(1)}, bf16[2,32,1152]{2,1,0:T(8,128)(2,1)S(1)}, u32[]{:S(2)}, u32[]{:S(2)}) collective-permute-start(bf16[2,32,1152]{2,1,0:T(8,128)(2,1)S(1)} %get-tuple-element.61), channel_id=1, source_target_pairs={{0,4},{4,8},{8,12},{12,0},{1,5},{5,9},{9,13},{13,1},{2,6},{6,10},{... | collective-permute-start | bytes 442376 | tf_op jit(solution)/shard_map/ppermute | solution.py:56
  24.7 25.4 %copy-start.3 = (bf16[32,1152]{1,0:T(8,128)(2,1)S(1)}, bf16[32,1152]{1,0:T(8,128)(2,1)}, u32[]{:S(2)}) copy-start(bf16[32,1152]{1,0:T(8,128)(2,1)} %base.1) | copy-start | bytes 221188
  32.6 12.2 %collective-permute-start.4 = (bf16[2,32,1152]{2,1,0:T(8,128)(2,1)S(1)}, bf16[2,32,1152]{2,1,0:T(8,128)(2,1)S(1)}, u32[]{:S(2)}, u32[]{:S(2)}) collective-permute-start(bf16[2,32,1152]{2,1,0:T(8,128)(2,1)S(1)} %fusion.7), channel_id=1, source_target_pairs={{0,2},{2,0},{16,18},{18,16},{1,3},{3,1},{17,19},{19,17},{4,6},{6,4... | collective-permute-start | bytes 442376 | tf_op jit(solution)/shard_map/ppermute | solution.py:71
  35.2 9.5 %collective-permute-start.6 = (bf16[2,32,1152]{2,1,0:T(8,128)(2,1)S(1)}, bf16[2,32,1152]{2,1,0:T(8,128)(2,1)S(1)}, u32[]{:S(2)}, u32[]{:S(2)}) collective-permute-start(bf16[2,32,1152]{2,1,0:T(8,128)(2,1)S(1)} %fusion.7), channel_id=1, source_target_pairs={{0,18},{2,16},{16,2},{18,0},{1,19},{3,17},{17,3},{19,1},{4,22},{6,... | collective-permute-start | bytes 442376 | tf_op jit(solution)/shard_map/ppermute | solution.py:71
  35.6 14.4 %collective-permute-start.5 = (bf16[2,32,1152]{2,1,0:T(8,128)(2,1)S(1)}, bf16[2,32,1152]{2,1,0:T(8,128)(2,1)S(1)}, u32[]{:S(2)}, u32[]{:S(2)}) collective-permute-start(bf16[2,32,1152]{2,1,0:T(8,128)(2,1)S(1)} %fusion.7), channel_id=1, source_target_pairs={{0,16},{2,18},{16,0},{18,2},{1,17},{3,19},{17,1},{19,3},{4,20},{6,... | collective-permute-start | bytes 442376 | tf_op jit(solution)/shard_map/ppermute | solution.py:71
  51.1 25.3 %all-to-all-start.1 = ((bf16[8,32,1152]{2,1,0:T(8,128)(2,1)}), bf16[8,32,1152]{2,1,0:T(8,128)(2,1)S(1)}, u32[]{:S(2)}, u32[]{:S(2)}) async-start(bf16[8,32,1152]{2,1,0:T(8,128)(2,1)} %get-tuple-element.34), calls=%async_computation.1 | async-start | bytes 1179648 | tf_op jit(solution)/shard_map/all_to_all | solution.py:75
  57.1 7.6 %collective-permute-start.9 = (bf16[2,2,32,1152]{3,2,1,0:T(8,128)(2,1)S(1)}, bf16[2,2,32,1152]{3,2,1,0:T(8,128)(2,1)S(1)}, u32[]{:S(2)}, u32[]{:S(2)}) collective-permute-start(bf16[2,2,32,1152]{3,2,1,0:T(8,128)(2,1)S(1)} %pad_maximum_fusion.3), channel_id=1, source_target_pairs={{0,12},{4,0},{8,4},{12,8},{1,13},{5,1},{9,5},{13,9},{2,14},{6,2},{... | collective-permute-start | bytes 884744 | tf_op jit(solution)/shard_map/ppermute | solution.py:56
  57.1 8.6 %collective-permute-start.8 = (bf16[2,2,32,1152]{3,2,1,0:T(8,128)(2,1)S(1)}, bf16[2,2,32,1152]{3,2,1,0:T(8,128)(2,1)S(1)}, u32[]{:S(2)}, u32[]{:S(2)}) collective-permute-start(bf16[2,2,32,1152]{3,2,1,0:T(8,128)(2,1)S(1)} %pad_maximum_fusion.3), channel_id=1, source_target_pairs={{0,8},{4,12},{8,0},{12,4},{1,9},{5,13},{9,1},{13,5},{2,10},{6,14},... | collective-permute-start | bytes 884744 | tf_op jit(solution)/shard_map/ppermute | solution.py:56
  57.2 16.7 %collective-permute-start.7 = (bf16[2,2,32,1152]{3,2,1,0:T(8,128)(2,1)S(1)}, bf16[2,2,32,1152]{3,2,1,0:T(8,128)(2,1)S(1)}, u32[]{:S(2)}, u32[]{:S(2)}) collective-permute-start(bf16[2,2,32,1152]{3,2,1,0:T(8,128)(2,1)S(1)} %pad_maximum_fusion.3), channel_id=1, source_target_pairs={{0,4},{4,8},{8,12},{12,0},{1,5},{5,9},{9,13},{13,1},{2,6},{6,10},{... | collective-permute-start | bytes 884744 | tf_op jit(solution)/shard_map/ppermute | solution.py:56
  76.5 4.0 %collective-permute-start.11 = (bf16[512,1152]{1,0:T(8,128)(2,1)S(1)}, bf16[512,1152]{1,0:T(8,128)(2,1)S(1)}, u32[]{:S(2)}, u32[]{:S(2)}) collective-permute-start(bf16[512,1152]{1,0:T(8,128)(2,1)S(1)} %bitcast.82), channel_id=1, source_target_pairs={{0,1},{1,0},{2,3},{3,2},{4,5},{5,4},{6,7},{7,6},{8,9},{9,8},{10,11... | collective-permute-start | bytes 3538952 | tf_op jit(solution)/shard_map/ppermute | solution.py:48
  85.1 4.5 %collective-permute-start.12 = (bf16[512,1152]{1,0:T(8,128)(2,1)}, bf16[512,1152]{1,0:T(8,128)(2,1)}, u32[]{:S(2)}, u32[]{:S(2)}) collective-permute-start(bf16[512,1152]{1,0:T(8,128)(2,1)} %get-tuple-element.40), channel_id=1, source_target_pairs={{0,1},{1,0},{2,3},{3,2},{4,5},{5,4},{6,7},{7,6},{8,9},{9,8},{10,11... | collective-permute-start | bytes 3538952 | tf_op jit(solution)/shard_map/ppermute | solution.py:48
  85.2 23.9 %all-to-all-start.2 = ((bf16[8,32,1152]{2,1,0:T(8,128)(2,1)}), bf16[8,32,1152]{2,1,0:T(8,128)(2,1)S(1)}, u32[]{:S(2)}, u32[]{:S(2)}) async-start(bf16[8,32,1152]{2,1,0:T(8,128)(2,1)} %bitcast.28), calls=%async_computation.2 | async-start | bytes 1179648 | tf_op jit(solution)/shard_map/all_to_all | solution.py:75
  91.3 22.6 %collective-permute-start.15 = (bf16[4,32,1152]{2,1,0:T(8,128)(2,1)S(1)}, bf16[4,32,1152]{2,1,0:T(8,128)(2,1)S(1)}, u32[]{:S(2)}, u32[]{:S(2)}) collective-permute-start(bf16[4,32,1152]{2,1,0:T(8,128)(2,1)S(1)} %bitcast.93), channel_id=1, source_target_pairs={{0,4},{4,8},{8,12},{12,0},{1,5},{5,9},{9,13},{13,1},{2,6},{6,10},{... | collective-permute-start | bytes 884744 | tf_op jit(solution)/shard_map/ppermute | solution.py:56
  91.4 22.5 %collective-permute-start.14 = (bf16[4,32,1152]{2,1,0:T(8,128)(2,1)S(1)}, bf16[4,32,1152]{2,1,0:T(8,128)(2,1)S(1)}, u32[]{:S(2)}, u32[]{:S(2)}) collective-permute-start(bf16[4,32,1152]{2,1,0:T(8,128)(2,1)S(1)} %bitcast.92), channel_id=1, source_target_pairs={{0,8},{4,12},{8,0},{12,4},{1,9},{5,13},{9,1},{13,5},{2,10},{6,14},... | collective-permute-start | bytes 884744 | tf_op jit(solution)/shard_map/ppermute | solution.py:56
  93.5 20.5 %collective-permute-start.13 = (bf16[4,32,1152]{2,1,0:T(8,128)(2,1)S(1)}, bf16[4,32,1152]{2,1,0:T(8,128)(2,1)S(1)}, u32[]{:S(2)}, u32[]{:S(2)}) collective-permute-start(bf16[4,32,1152]{2,1,0:T(8,128)(2,1)S(1)} %bitcast.91), channel_id=1, source_target_pairs={{0,12},{4,0},{8,4},{12,8},{1,13},{5,1},{9,5},{13,9},{2,14},{6,2},{... | collective-permute-start | bytes 884744 | tf_op jit(solution)/shard_map/ppermute | solution.py:56
  110.2 34.1 %all-to-all-start.4 = ((bf16[16,32,1152]{2,1,0:T(8,128)(2,1)}), bf16[16,32,1152]{2,1,0:T(8,128)(2,1)S(1)}, u32[]{:S(2)}, u32[]{:S(2)}) async-start(bf16[16,32,1152]{2,1,0:T(8,128)(2,1)} %get-tuple-element.47), calls=%async_computation.4 | async-start | bytes 2359296 | tf_op jit(solution)/shard_map/all_to_all | solution.py:75
  114.2 7.0 %collective-permute-start.18 = (bf16[2,40,1152]{2,1,0:T(8,128)(2,1)S(1)}, bf16[2,40,1152]{2,1,0:T(8,128)(2,1)S(1)}, u32[]{:S(2)}, u32[]{:S(2)}) collective-permute-start(bf16[2,40,1152]{2,1,0:T(8,128)(2,1)S(1)} %get-tuple-element.65), channel_id=1, source_target_pairs={{0,18},{2,16},{16,2},{18,0},{1,19},{3,17},{17,3},{19,1},{4,22},{6,... | collective-permute-start | bytes 552968 | tf_op jit(solution)/shard_map/ppermute | solution.py:71
  116.3 5.1 %collective-permute-start.17 = (bf16[2,40,1152]{2,1,0:T(8,128)(2,1)S(1)}, bf16[2,40,1152]{2,1,0:T(8,128)(2,1)S(1)}, u32[]{:S(2)}, u32[]{:S(2)}) collective-permute-start(bf16[2,40,1152]{2,1,0:T(8,128)(2,1)S(1)} %get-tuple-element.65), channel_id=1, source_target_pairs={{0,16},{2,18},{16,0},{18,2},{1,17},{3,19},{17,1},{19,3},{4,20},{6,... | collective-permute-start | bytes 552968 | tf_op jit(solution)/shard_map/ppermute | solution.py:71
  116.3 23.7 %copy-start.6 = (bf16[512,269]{0,1:T(8,128)(2,1)S(1)}, bf16[512,269]{0,1:T(8,128)(2,1)}, u32[]{:S(2)}) copy-start(bf16[512,269]{0,1:T(8,128)(2,1)} %param.10) | copy-start | bytes 826372
  116.4 9.9 %collective-permute-start.16 = (bf16[2,40,1152]{2,1,0:T(8,128)(2,1)S(1)}, bf16[2,40,1152]{2,1,0:T(8,128)(2,1)S(1)}, u32[]{:S(2)}, u32[]{:S(2)}) collective-permute-start(bf16[2,40,1152]{2,1,0:T(8,128)(2,1)S(1)} %get-tuple-element.64), channel_id=1, source_target_pairs={{0,2},{2,0},{16,18},{18,16},{1,3},{3,1},{17,19},{19,17},{4,6},{6,4... | collective-permute-start | bytes 552968 | tf_op jit(solution)/shard_map/ppermute | solution.py:71
  126.4 13.7 %copy-start.7 = (bf16[512,269]{0,1:T(8,128)(2,1)S(1)}, bf16[512,269]{0,1:T(8,128)(2,1)}, u32[]{:S(2)}) copy-start(bf16[512,269]{0,1:T(8,128)(2,1)} %param.13) | copy-start | bytes 826372
  126.4 4.8 %collective-permute-start.21 = (bf16[2,40,1152]{2,1,0:T(8,128)(2,1)S(1)}, bf16[2,40,1152]{2,1,0:T(8,128)(2,1)S(1)}, u32[]{:S(2)}, u32[]{:S(2)}) collective-permute-start(bf16[2,40,1152]{2,1,0:T(8,128)(2,1)S(1)} %add_convert_fusion.2), channel_id=1, source_target_pairs={{0,12},{4,0},{8,4},{12,8},{1,13},{5,1},{9,5},{13,9},{2,14},{6,2},{... | collective-permute-start | bytes 552968 | tf_op jit(solution)/shard_map/ppermute | solution.py:56
  127.4 6.0 %collective-permute-start.20 = (bf16[2,40,1152]{2,1,0:T(8,128)(2,1)S(1)}, bf16[2,40,1152]{2,1,0:T(8,128)(2,1)S(1)}, u32[]{:S(2)}, u32[]{:S(2)}) collective-permute-start(bf16[2,40,1152]{2,1,0:T(8,128)(2,1)S(1)} %add_convert_fusion.2), channel_id=1, source_target_pairs={{0,8},{4,12},{8,0},{12,4},{1,9},{5,13},{9,1},{13,5},{2,10},{6,14},... | collective-permute-start | bytes 552968 | tf_op jit(solution)/shard_map/ppermute | solution.py:56
  127.4 11.4 %collective-permute-start.19 = (bf16[2,40,1152]{2,1,0:T(8,128)(2,1)S(1)}, bf16[2,40,1152]{2,1,0:T(8,128)(2,1)S(1)}, u32[]{:S(2)}, u32[]{:S(2)}) collective-permute-start(bf16[2,40,1152]{2,1,0:T(8,128)(2,1)S(1)} %add_convert_fusion.2), channel_id=1, source_target_pairs={{0,4},{4,8},{8,12},{12,0},{1,5},{5,9},{9,13},{13,1},{2,6},{6,10},{... | collective-permute-start | bytes 552968 | tf_op jit(solution)/shard_map/ppermute | solution.py:56
  138.9 3.1 %copy-start.2 = (bf16[269,1152]{1,0:T(8,128)(2,1)S(1)}, bf16[269,1152]{1,0:T(8,128)(2,1)}, u32[]{:S(2)}) copy-start(bf16[269,1152]{1,0:T(8,128)(2,1)} %proj.2) | copy-start | bytes 1859332
  139.0 3.0 %collective-permute-start.22 = (bf16[4,2,40,1152]{3,2,1,0:T(8,128)(2,1)S(1)}, bf16[4,2,40,1152]{3,2,1,0:T(8,128)(2,1)S(1)}, u32[]{:S(2)}, u32[]{:S(2)}) collective-permute-start(bf16[4,2,40,1152]{3,2,1,0:T(8,128)(2,1)S(1)} %pad_maximum_fusion.1.own), channel_id=1, source_target_pairs={{0,1},{1,0},{2,3},{3,2},{4,5},{5,4},{6,7},{7,6},{8,9},{9,8},{10,11... | collective-permute-start | bytes 2211848 | tf_op jit(solution)/shard_map/ppermute | solution.py:48
  140.2 4.1 %copy-start = (bf16[269,1152]{1,0:T(8,128)(2,1)S(1)}, bf16[269,1152]{1,0:T(8,128)(2,1)}, u32[]{:S(2)}) copy-start(bf16[269,1152]{1,0:T(8,128)(2,1)} %proj.3) | copy-start | bytes 1859332
  146.6 6.4 %collective-permute-start.23 = (bf16[4,2,80,256]{3,2,1,0:T(8,128)(2,1)S(1)}, bf16[4,2,80,256]{3,2,1,0:T(8,128)(2,1)S(1)}, u32[]{:S(2)}, u32[]{:S(2)}) collective-permute-start(bf16[4,2,80,256]{3,2,1,0:T(8,128)(2,1)S(1)} %get-tuple-element.50), channel_id=1, source_target_pairs={{0,1},{1,0},{2,3},{3,2},{4,5},{5,4},{6,7},{7,6},{8,9},{9,8},{10,11... | collective-permute-start | bytes 983048 | tf_op jit(solution)/shard_map/ppermute | solution.py:48
  148.7 23.0 %all-to-all-start.3 = ((bf16[16,80,256]{2,1,0:T(8,128)(2,1)}), bf16[16,80,256]{2,1,0:T(8,128)(2,1)S(1)}, u32[]{:S(2)}, u32[]{:S(2)}) async-start(bf16[16,80,256]{2,1,0:T(8,128)(2,1)} %get-tuple-element.45), calls=%async_computation.3 | async-start | bytes 1310720 | tf_op jit(solution)/shard_map/all_to_all | solution.py:75
  153.2 3.7 %collective-permute-start.26 = (bf16[2,80,256]{2,1,0:T(8,128)(2,1)S(1)}, bf16[2,80,256]{2,1,0:T(8,128)(2,1)S(1)}, u32[]{:S(2)}, u32[]{:S(2)}) collective-permute-start(bf16[2,80,256]{2,1,0:T(8,128)(2,1)S(1)} %get-tuple-element.67), channel_id=1, source_target_pairs={{0,12},{4,0},{8,4},{12,8},{1,13},{5,1},{9,5},{13,9},{2,14},{6,2},{... | collective-permute-start | bytes 245768 | tf_op jit(solution)/shard_map/ppermute | solution.py:56
  153.8 4.8 %collective-permute-start.25 = (bf16[2,80,256]{2,1,0:T(8,128)(2,1)S(1)}, bf16[2,80,256]{2,1,0:T(8,128)(2,1)S(1)}, u32[]{:S(2)}, u32[]{:S(2)}) collective-permute-start(bf16[2,80,256]{2,1,0:T(8,128)(2,1)S(1)} %get-tuple-element.68), channel_id=1, source_target_pairs={{0,8},{4,12},{8,0},{12,4},{1,9},{5,13},{9,1},{13,5},{2,10},{6,14},... | collective-permute-start | bytes 245768 | tf_op jit(solution)/shard_map/ppermute | solution.py:56
  154.1 7.0 %collective-permute-start.24 = (bf16[2,80,256]{2,1,0:T(8,128)(2,1)S(1)}, bf16[2,80,256]{2,1,0:T(8,128)(2,1)S(1)}, u32[]{:S(2)}, u32[]{:S(2)}) collective-permute-start(bf16[2,80,256]{2,1,0:T(8,128)(2,1)S(1)} %get-tuple-element.66), channel_id=1, source_target_pairs={{0,4},{4,8},{8,12},{12,0},{1,5},{5,9},{9,13},{13,1},{2,6},{6,10},{... | collective-permute-start | bytes 245768 | tf_op jit(solution)/shard_map/ppermute | solution.py:56
  161.3 4.8 %collective-permute-start.27 = (bf16[80,256]{1,0:T(8,128)(2,1)S(1)}, bf16[80,256]{1,0:T(8,128)(2,1)S(1)}, u32[]{:S(2)}, u32[]{:S(2)}) collective-permute-start(bf16[80,256]{1,0:T(8,128)(2,1)S(1)} %get-tuple-element.70), channel_id=1, source_target_pairs={{0,2},{2,0},{1,3},{3,1},{4,6},{6,4},{5,7},{7,5},{8,10},{10,8},{9,1... | collective-permute-start | bytes 122888 | tf_op jit(solution)/shard_map/ppermute | solution.py:48

commit v3 on v2

--- a/solution.py
+++ b/solution.py
@@ -99,7 +99,7 @@
     )(parts, base)
 
 
-CHUNK = 256
+CHUNK = 512
 VMEM = pl.BlockSpec(memory_space=pltpu.VMEM)
 SMEM = pl.BlockSpec(memory_space=pltpu.SMEM)
 
@@ -117,14 +117,19 @@
         hit = labels[:, part] == columns
         small = jnp.exp(-jnp.abs(scores))
         signed = jnp.where(hit, -scores, scores)
-        terms = jnp.maximum(signed, 0.0) + jnp.log1p(small)
-        loss = loss + jnp.sum(terms, axis=0, keepdims=True)
+        loss = loss + jnp.sum(jnp.maximum(signed, 0.0), axis=0, keepdims=True)
+        product = small
+        for _ in range(3):
+            height = product.shape[0] // 2
+            upper, lower = product[:height], product[height:]
+            product = upper + lower + upper * lower
+        loss = loss + jnp.sum(jnp.log1p(product), axis=0, keepdims=True)
         sigmoid = jnp.where(scores >= 0.0, 1.0, small) / (1.0 + small)
         slope = (sigmoid - hit.astype(f32)).astype(bf16)
         total = total + dot(slope, image_unit)
-        upstream = scale * contract_rows(slope, unit)
+        upstream = contract_rows(slope, unit)
         along = jnp.sum(wide_unit * upstream, axis=-1, keepdims=True)
-        image_parts[part, :] = (inverse * (upstream - wide_unit * along)).astype(bf16)
+        image_parts[part, :] = (scale * inverse * (upstream - wide_unit * along)).astype(bf16)
     return total, loss
 
 

time: 176 us -> 175 us (level)
  no operation moved by 1% of the time
where the time goes in v3:
time: 175 us; the launch traced here: 173 us
  waiting for transfers between devices  88.3 us (50%)
  starting transfers between devices  55.5 us (32%)
  Pallas kernels  15.3 us (9%)
  between operations  4.16 us (2%)
  other arithmetic  4.11 us (2%)
  matrix products  4.02 us (2%)
    ppermute x15, waiting for transfers between devices, shift(): lax.ppermute(block, axis, [(i, (i + step) % count) for i in range(count)])  40.3 us
    all_to_all x5, starting transfers between devices, exchange(): return lax.all_to_all(blocks, axis, 0, 0)  26.4 us
    ppermute x6, waiting for transfers between devices, turn_x(): lax.ppermute(block, ('xl', 'xh'), [(i, i ^ 2 * a + b) for i in range(4)])  22.5 us
    all_to_all x5, waiting for transfers between devices, exchange(): return lax.all_to_all(blocks, axis, 0, 0)  22.1 us
    ppermute x15, starting transfers between devices, shift(): lax.ppermute(block, axis, [(i, (i + step) % count) for i in range(count)])  11.3 us
    ppermute x7, starting transfers between devices, swap(): return lax.ppermute(block, axis, SWAP)  11 us
    ppermute x6, starting transfers between devices, turn_x(): lax.ppermute(block, ('xl', 'xh'), [(i, i ^ 2 * a + b) for i in range(4)])  6.83 us
    pallas_call x1, Pallas kernels, rest_call(): pl.pallas_call(rest_kernel, out_shape=(like(text, bf16), like(image, bf16...  4.05 us
  transfers between devices with their start and end apart: 33, of which 22 were waited for; matrix products, arithmetic and copies ran while one was open for 3% of the time, Pallas kernels for 4%

profile of v3, /device:TPU:1, one launch (start us, length us, event | category | flops | bytes accessed | tf_op | source)
XLA Modules:
  0.0 173.1 jit_solution(16694207408002453042)
XLA Ops:
  0.7 3.2 %convolution_convert_fusion.1 = bf16[512,1152]{1,0:T(8,128)(2,1)} fusion(bf16[512,269]{0,1:T(8,128)(2,1)} %param.13, bf16[269,1152]{1,0:T(8,128)(2,1)} %proj.3), kind=kOutput, calls=%fused_computation.2 | convolution fusion | flops 317915136 | bytes 2074880 | tf_op jit(solution)/shard_map/dot_general | solution.py:32
  3.8 0.9 convolution_convert_fusion
  4.8 3.3 %collective-permute-start = (bf16[4,2,32,1152]{3,2,1,0:T(8,128)(2,1)S(1)}, bf16[4,2,32,1152]{3,2,1,0:T(8,128)(2,1)S(1)}, u32[]{:S(2)}, u32[]{:S(2)}) collective-permute-start(bf16[4,2,32,1152]{3,2,1,0:T(8,128)(2,1)S(1)} %dynamic-slice_bitcast_fusion), channel_id=1, source_target_pairs={{0,1},{1,0},{2,3},{3,2},{4,5},{5,4},{6,7},{7,6},{8,9},{9,8},{10,11... | collective-permute-start | bytes 1769480 | tf_op jit(solution)/shard_map/ppermute | solution.py:48
  8.1 7.7 %all-to-all-start = ((bf16[16,32,1152]{2,1,0:T(8,128)(2,1)}), bf16[16,32,1152]{2,1,0:T(8,128)(2,1)S(1)}, u32[]{:S(2)}, u32[]{:S(2)}) async-start(bf16[16,32,1152]{2,1,0:T(8,128)(2,1)} %bitcast.4), calls=%async_computation | async-start | bytes 2359296 | tf_op jit(solution)/shard_map/all_to_all | solution.py:75
  15.8 1.4 collective-permute-start.10
  18.7 1.3 fusion
  20.1 2.8 %collective-permute-start.3 = (bf16[2,32,1152]{2,1,0:T(8,128)(2,1)S(1)}, bf16[2,32,1152]{2,1,0:T(8,128)(2,1)S(1)}, u32[]{:S(2)}, u32[]{:S(2)}) collective-permute-start(bf16[2,32,1152]{2,1,0:T(8,128)(2,1)S(1)} %get-tuple-element.62), channel_id=1, source_target_pairs={{0,12},{4,0},{8,4},{12,8},{1,13},{5,1},{9,5},{13,9},{2,14},{6,2},{... | collective-permute-start | bytes 442376 | tf_op jit(solution)/shard_map/ppermute | solution.py:56
  24.7 0.9 collective-permute-done.3
  25.6 3.0 %collective-permute-done.2 = bf16[2,32,1152]{2,1,0:T(8,128)(2,1)S(1)} collective-permute-done((bf16[2,32,1152]{2,1,0:T(8,128)(2,1)S(1)}, bf16[2,32,1152]{2,1,0:T(8,128)(2,1)S(1)}, u32[]{:S(2)}, u32[]{:S(2)}) %collective-permute-start.2) | collective-permute-done | bytes 147488 | tf_op jit(solution)/shard_map/ppermute | solution.py:56
  28.7 3.8 %collective-permute-done.1 = bf16[2,32,1152]{2,1,0:T(8,128)(2,1)S(1)} collective-permute-done((bf16[2,32,1152]{2,1,0:T(8,128)(2,1)S(1)}, bf16[2,32,1152]{2,1,0:T(8,128)(2,1)S(1)}, u32[]{:S(2)}, u32[]{:S(2)}) %collective-permute-start.1) | collective-permute-done | bytes 147488 | tf_op jit(solution)/shard_map/ppermute | solution.py:56
  32.6 2.5 %collective-permute-start.4 = (bf16[2,32,1152]{2,1,0:T(8,128)(2,1)S(1)}, bf16[2,32,1152]{2,1,0:T(8,128)(2,1)S(1)}, u32[]{:S(2)}, u32[]{:S(2)}) collective-permute-start(bf16[2,32,1152]{2,1,0:T(8,128)(2,1)S(1)} %fusion.7), channel_id=1, source_target_pairs={{0,2},{2,0},{16,18},{18,16},{1,3},{3,1},{17,19},{19,17},{4,6},{6,4... | collective-permute-start | bytes 442376 | tf_op jit(solution)/shard_map/ppermute | solution.py:71
  35.6 9.1 %collective-permute-done.4 = bf16[2,32,1152]{2,1,0:T(8,128)(2,1)S(1)} collective-permute-done((bf16[2,32,1152]{2,1,0:T(8,128)(2,1)S(1)}, bf16[2,32,1152]{2,1,0:T(8,128)(2,1)S(1)}, u32[]{:S(2)}, u32[]{:S(2)}) %collective-permute-start.4) | collective-permute-done | bytes 147488 | tf_op jit(solution)/shard_map/ppermute | solution.py:71
  44.8 5.2 %collective-permute-done.5 = bf16[2,32,1152]{2,1,0:T(8,128)(2,1)S(1)} collective-permute-done((bf16[2,32,1152]{2,1,0:T(8,128)(2,1)S(1)}, bf16[2,32,1152]{2,1,0:T(8,128)(2,1)S(1)}, u32[]{:S(2)}, u32[]{:S(2)}) %collective-permute-start.5) | collective-permute-done | bytes 147488 | tf_op jit(solution)/shard_map/ppermute | solution.py:71
  50.1 1.0 spread.2
  51.1 6.0 %all-to-all-start.1 = ((bf16[8,32,1152]{2,1,0:T(8,128)(2,1)}), bf16[8,32,1152]{2,1,0:T(8,128)(2,1)S(1)}, u32[]{:S(2)}, u32[]{:S(2)}) async-start(bf16[8,32,1152]{2,1,0:T(8,128)(2,1)} %get-tuple-element.34), calls=%async_computation.1 | async-start | bytes 1179648 | tf_op jit(solution)/shard_map/all_to_all | solution.py:75
  57.2 1.4 collective-permute-start.7
  58.6 6.2 %collective-permute-done.9 = bf16[2,2,32,1152]{3,2,1,0:T(8,128)(2,1)S(1)} collective-permute-done((bf16[2,2,32,1152]{3,2,1,0:T(8,128)(2,1)S(1)}, bf16[2,2,32,1152]{3,2,1,0:T(8,128)(2,1)S(1)}, u32[]{:S(2)}, u32[]{:S(2)}) %collective-permute-start.9) | collective-permute-done | bytes 294944 | tf_op jit(solution)/shard_map/ppermute | solution.py:56
  64.7 1.0 collective-permute-done.8
  65.7 8.2 %collective-permute-done.7 = bf16[2,2,32,1152]{3,2,1,0:T(8,128)(2,1)S(1)} collective-permute-done((bf16[2,2,32,1152]{3,2,1,0:T(8,128)(2,1)S(1)}, bf16[2,2,32,1152]{3,2,1,0:T(8,128)(2,1)S(1)}, u32[]{:S(2)}, u32[]{:S(2)}) %collective-permute-start.7) | collective-permute-done | bytes 294944 | tf_op jit(solution)/shard_map/ppermute | solution.py:56
  74.1 2.3 %all-to-all-done.1 = bf16[8,32,1152]{2,1,0:T(8,128)(2,1)S(1)} async-done(((bf16[8,32,1152]{2,1,0:T(8,128)(2,1)}), bf16[8,32,1152]{2,1,0:T(8,128)(2,1)S(1)}, u32[]{:S(2)}, u32[]{:S(2)}) %all-to-all-start.1) | async-done | bytes 589856 | tf_op jit(solution)/shard_map/all_to_all | solution.py:75
  77.0 2.8 %score.1 = (f32[256,1152]{1,0:T(8,128)S(1)}, bf16[256,1152]{1,0:T(8,128)(2,1)S(1)}, bf16[512,1152]{1,0:T(8,128)(2,1)S(1)}, f32[1,512]{1,0:T(1,128)S(1)}) custom-call(f32[2]{0:T(128)S(1)} %pad_maximum_fusion.5.params, s32[2]{0:T(128)S(1)} %pad_add_fusion.1.base, bf16[512,1152]{1,0:T(8,128)(2,1)S(1)} %bitcast.83, bf16[256,1152]{1,0:T(8,128)(2,1)S(1)} %bitcast.79, ...), custom_call_target="tpu_custom_call" | custom-call | tf_op jit(solution)/shard_map/score/pallas_call | solution.py:161
  79.8 4.1 %score_rest.1 = (bf16[256,1152]{1,0:T(8,128)(2,1)}, bf16[512,1152]{1,0:T(8,128)(2,1)}, bf16[8,1152]{1,0:T(8,128)(2,1)S(1)}) custom-call(f32[2]{0:T(128)S(1)} %pad_maximum_fusion.5.params, s32[2]{0:T(128)S(1)} %pad_add_fusion.1.base, bf16[512,1152]{1,0:T(8,128)(2,1)S(1)} %collective-permute-done.11.image, bf16[256,1152]{1,0:T(8,128)(2,1)S(1)} %bitcast.80, ...), custom_call_target="tpu_custom_call" | custom-call | tf_op jit(solution)/shard_map/score_rest/pallas_call | solution.py:177
  83.9 4.5 %all-to-all-start.2 = ((bf16[8,32,1152]{2,1,0:T(8,128)(2,1)}), bf16[8,32,1152]{2,1,0:T(8,128)(2,1)S(1)}, u32[]{:S(2)}, u32[]{:S(2)}) async-start(bf16[8,32,1152]{2,1,0:T(8,128)(2,1)} %bitcast.28), calls=%async_computation.2 | async-start | bytes 1179648 | tf_op jit(solution)/shard_map/all_to_all | solution.py:75
  88.4 1.5 add_convert_fusion
  90.1 2.1 %collective-permute-start.14 = (bf16[4,32,1152]{2,1,0:T(8,128)(2,1)S(1)}, bf16[4,32,1152]{2,1,0:T(8,128)(2,1)S(1)}, u32[]{:S(2)}, u32[]{:S(2)}) collective-permute-start(bf16[4,32,1152]{2,1,0:T(8,128)(2,1)S(1)} %bitcast.92), channel_id=1, source_target_pairs={{0,8},{4,12},{8,0},{12,4},{1,9},{5,13},{9,1},{13,5},{2,10},{6,14},... | collective-permute-start | bytes 884744 | tf_op jit(solution)/shard_map/ppermute | solution.py:56
  92.8 14.9 %all-to-all-done.2.parts = bf16[8,32,1152]{2,1,0:T(8,128)(2,1)S(1)} async-done(((bf16[8,32,1152]{2,1,0:T(8,128)(2,1)}), bf16[8,32,1152]{2,1,0:T(8,128)(2,1)S(1)}, u32[]{:S(2)}, u32[]{:S(2)}) %all-to-all-start.2) | async-done | bytes 589856 | tf_op jit(solution)/shard_map/all_to_all | solution.py:75
  107.7 1.2 spread.3
  108.9 3.7 %all-to-all-start.4 = ((bf16[16,32,1152]{2,1,0:T(8,128)(2,1)}), bf16[16,32,1152]{2,1,0:T(8,128)(2,1)S(1)}, u32[]{:S(2)}, u32[]{:S(2)}) async-start(bf16[16,32,1152]{2,1,0:T(8,128)(2,1)} %get-tuple-element.47), calls=%async_computation.4 | async-start | bytes 2359296 | tf_op jit(solution)/shard_map/all_to_all | solution.py:75
  112.9 2.2 %collective-permute-start.18 = (bf16[2,40,1152]{2,1,0:T(8,128)(2,1)S(1)}, bf16[2,40,1152]{2,1,0:T(8,128)(2,1)S(1)}, u32[]{:S(2)}, u32[]{:S(2)}) collective-permute-start(bf16[2,40,1152]{2,1,0:T(8,128)(2,1)S(1)} %get-tuple-element.65), channel_id=1, source_target_pairs={{0,18},{2,16},{16,2},{18,0},{1,19},{3,17},{17,3},{19,1},{4,22},{6,... | collective-permute-start | bytes 552968 | tf_op jit(solution)/shard_map/ppermute | solution.py:71
  115.1 1.8 %collective-permute-start.16 = (bf16[2,40,1152]{2,1,0:T(8,128)(2,1)S(1)}, bf16[2,40,1152]{2,1,0:T(8,128)(2,1)S(1)}, u32[]{:S(2)}, u32[]{:S(2)}) collective-permute-start(bf16[2,40,1152]{2,1,0:T(8,128)(2,1)S(1)} %get-tuple-element.64), channel_id=1, source_target_pairs={{0,2},{2,0},{16,18},{18,16},{1,3},{3,1},{17,19},{19,17},{4,6},{6,4... | collective-permute-start | bytes 552968 | tf_op jit(solution)/shard_map/ppermute | solution.py:71
  116.8 3.1 %collective-permute-done.18 = bf16[2,40,1152]{2,1,0:T(8,128)(2,1)S(1)} collective-permute-done((bf16[2,40,1152]{2,1,0:T(8,128)(2,1)S(1)}, bf16[2,40,1152]{2,1,0:T(8,128)(2,1)S(1)}, u32[]{:S(2)}, u32[]{:S(2)}) %collective-permute-start.18) | collective-permute-done | bytes 184352 | tf_op jit(solution)/shard_map/ppermute | solution.py:71
  120.1 4.9 %collective-permute-done.16 = bf16[2,40,1152]{2,1,0:T(8,128)(2,1)S(1)} collective-permute-done((bf16[2,40,1152]{2,1,0:T(8,128)(2,1)S(1)}, bf16[2,40,1152]{2,1,0:T(8,128)(2,1)S(1)}, u32[]{:S(2)}, u32[]{:S(2)}) %collective-permute-start.16) | collective-permute-done | bytes 184352 | tf_op jit(solution)/shard_map/ppermute | solution.py:71
  125.1 1.0 collective-permute-start.21
  126.8 3.1 %collective-permute-done.21 = bf16[2,40,1152]{2,1,0:T(8,128)(2,1)S(1)} collective-permute-done((bf16[2,40,1152]{2,1,0:T(8,128)(2,1)S(1)}, bf16[2,40,1152]{2,1,0:T(8,128)(2,1)S(1)}, u32[]{:S(2)}, u32[]{:S(2)}) %collective-permute-start.21) | collective-permute-done | bytes 184352 | tf_op jit(solution)/shard_map/ppermute | solution.py:56
  129.9 2.3 %collective-permute-done.20 = bf16[2,40,1152]{2,1,0:T(8,128)(2,1)S(1)} collective-permute-done((bf16[2,40,1152]{2,1,0:T(8,128)(2,1)S(1)}, bf16[2,40,1152]{2,1,0:T(8,128)(2,1)S(1)}, u32[]{:S(2)}, u32[]{:S(2)}) %collective-permute-start.20) | collective-permute-done | bytes 184352 | tf_op jit(solution)/shard_map/ppermute | solution.py:56
  132.1 5.4 %collective-permute-done.19 = bf16[2,40,1152]{2,1,0:T(8,128)(2,1)S(1)} collective-permute-done((bf16[2,40,1152]{2,1,0:T(8,128)(2,1)S(1)}, bf16[2,40,1152]{2,1,0:T(8,128)(2,1)S(1)}, u32[]{:S(2)}, u32[]{:S(2)}) %collective-permute-start.19) | collective-permute-done | bytes 184352 | tf_op jit(solution)/shard_map/ppermute | solution.py:56
  137.7 1.3 collective-permute-start.22
  139.2 1.7 collective-permute-done.22.other
  140.9 2.4 %image_weight.1 = (bf16[269,512]{1,0:T(8,128)(2,1)}, bf16[16,80,256]{2,1,0:T(8,128)(2,1)}) custom-call(s32[2]{0:T(128)S(1)} %pad_add_fusion.place, bf16[4,2,40,1152]{3,2,1,0:T(8,128)(2,1)S(1)} %pad_maximum_fusion.1.own, bf16[4,2,40,1152]{3,2,1,0:T(8,128)(2,1)S(1)} %collective-permute-done.22.other, bf16[272,512]{1,0:T(8,128)(2,1)S(1)} %pad.7.acts, ...), custom_call_target="tpu_custom_call" | custom-call | tf_op jit(solution)/shard_map/image_weight/pallas_call | solution.py:255
  143.3 2.3 %text_weight.1 = (bf16[269,512]{1,0:T(8,128)(2,1)}, bf16[4,2,80,256]{3,2,1,0:T(8,128)(2,1)S(1)}, bf16[4,2,80,256]{3,2,1,0:T(8,128)(2,1)S(1)}) custom-call(s32[2]{0:T(128)S(1)} %pad_add_fusion.place, bf16[512,1152]{1,0:T(8,128)(2,1)S(1)} %bitcast.81, bf16[272,512]{1,0:T(8,128)(2,1)S(1)} %pad.8.acts, bf16[269,1152]{1,0:T(8,128)(2,1)S(1)} %copy-done), custom_call_target="tpu_custom_call" | custom-call | tf_op jit(solution)/shard_map/text_weight/pallas_call | solution.py:281
  145.6 1.8 %collective-permute-start.23 = (bf16[4,2,80,256]{3,2,1,0:T(8,128)(2,1)S(1)}, bf16[4,2,80,256]{3,2,1,0:T(8,128)(2,1)S(1)}, u32[]{:S(2)}, u32[]{:S(2)}) collective-permute-start(bf16[4,2,80,256]{3,2,1,0:T(8,128)(2,1)S(1)} %get-tuple-element.50), channel_id=1, source_target_pairs={{0,1},{1,0},{2,3},{3,2},{4,5},{5,4},{6,7},{7,6},{8,9},{9,8},{10,11... | collective-permute-start | bytes 983048 | tf_op jit(solution)/shard_map/ppermute | solution.py:48
  147.4 4.6 %all-to-all-start.3 = ((bf16[16,80,256]{2,1,0:T(8,128)(2,1)}), bf16[16,80,256]{2,1,0:T(8,128)(2,1)S(1)}, u32[]{:S(2)}, u32[]{:S(2)}) async-start(bf16[16,80,256]{2,1,0:T(8,128)(2,1)} %get-tuple-element.45), calls=%async_computation.3 | async-start | bytes 1310720 | tf_op jit(solution)/shard_map/all_to_all | solution.py:75
  153.7 2.1 %collective-permute-done.26 = bf16[2,80,256]{2,1,0:T(8,128)(2,1)S(1)} collective-permute-done((bf16[2,80,256]{2,1,0:T(8,128)(2,1)S(1)}, bf16[2,80,256]{2,1,0:T(8,128)(2,1)S(1)}, u32[]{:S(2)}, u32[]{:S(2)}) %collective-permute-start.26) | collective-permute-done | bytes 81952 | tf_op jit(solution)/shard_map/ppermute | solution.py:56
  155.8 1.7 %collective-permute-done.25 = bf16[2,80,256]{2,1,0:T(8,128)(2,1)S(1)} collective-permute-done((bf16[2,80,256]{2,1,0:T(8,128)(2,1)S(1)}, bf16[2,80,256]{2,1,0:T(8,128)(2,1)S(1)}, u32[]{:S(2)}, u32[]{:S(2)}) %collective-permute-start.25) | collective-permute-done | bytes 81952 | tf_op jit(solution)/shard_map/ppermute | solution.py:56
  157.5 2.5 %collective-permute-done.24 = bf16[2,80,256]{2,1,0:T(8,128)(2,1)S(1)} collective-permute-done((bf16[2,80,256]{2,1,0:T(8,128)(2,1)S(1)}, bf16[2,80,256]{2,1,0:T(8,128)(2,1)S(1)}, u32[]{:S(2)}, u32[]{:S(2)}) %collective-permute-start.24) | collective-permute-done | bytes 81952 | tf_op jit(solution)/shard_map/ppermute | solution.py:56
  160.2 2.5 %collective-permute-start.27 = (bf16[80,256]{1,0:T(8,128)(2,1)S(1)}, bf16[80,256]{1,0:T(8,128)(2,1)S(1)}, u32[]{:S(2)}, u32[]{:S(2)}) collective-permute-start(bf16[80,256]{1,0:T(8,128)(2,1)S(1)} %get-tuple-element.70), channel_id=1, source_target_pairs={{0,2},{2,0},{1,3},{3,1},{4,6},{6,4},{5,7},{7,5},{8,10},{10,8},{9,1... | collective-permute-start | bytes 122888 | tf_op jit(solution)/shard_map/ppermute | solution.py:48
  163.3 1.7 collective-permute-done.27
  165.8 4.8 %all-to-all-done.3.blocks = bf16[16,80,256]{2,1,0:T(8,128)(2,1)S(1)} async-done(((bf16[16,80,256]{2,1,0:T(8,128)(2,1)}), bf16[16,80,256]{2,1,0:T(8,128)(2,1)S(1)}, u32[]{:S(2)}, u32[]{:S(2)}) %all-to-all-start.3) | async-done | bytes 655392 | tf_op jit(solution)/shard_map/all_to_all | solution.py:75
  (86 shorter events, 9.7 us)
Async XLA Ops:
  0.6 3.2 %copy-start.5 = (bf16[512,269]{0,1:T(8,128)(2,1)S(1)}, bf16[512,269]{0,1:T(8,128)(2,1)}, u32[]{:S(2)}) copy-start(bf16[512,269]{0,1:T(8,128)(2,1)} %param.10) | copy-start | bytes 826372
  0.6 3.2 %copy-start.1 = (bf16[269,1152]{1,0:T(8,128)(2,1)S(1)}, bf16[269,1152]{1,0:T(8,128)(2,1)}, u32[]{:S(2)}) copy-start(bf16[269,1152]{1,0:T(8,128)(2,1)} %proj.2) | copy-start | bytes 1859332
  4.7 3.4 %copy-start.4 = (bf16[512,1152]{1,0:T(8,128)(2,1)}, bf16[512,1152]{1,0:T(8,128)(2,1)S(1)}, u32[]{:S(2)}) copy-start(bf16[512,1152]{1,0:T(8,128)(2,1)S(1)} %convolution_convert_fusion) | copy-start | bytes 3538948
  4.8 11.0 %copy-start.9 = (s32[512]{0:T(512)S(1)}, s32[512]{0:T(512)}, u32[]{:S(2)}) copy-start(s32[512]{0:T(512)} %param.15) | copy-start | bytes 6148
  4.8 14.0 %collective-permute-start = (bf16[4,2,32,1152]{3,2,1,0:T(8,128)(2,1)S(1)}, bf16[4,2,32,1152]{3,2,1,0:T(8,128)(2,1)S(1)}, u32[]{:S(2)}, u32[]{:S(2)}) collective-permute-start(bf16[4,2,32,1152]{3,2,1,0:T(8,128)(2,1)S(1)} %dynamic-slice_bitcast_fusion), channel_id=1, source_target_pairs={{0,1},{1,0},{2,3},{3,2},{4,5},{5,4},{6,7},{7,6},{8,9},{9,8},{10,11... | collective-permute-start | bytes 1769480 | tf_op jit(solution)/shard_map/ppermute | solution.py:48
  8.1 42.0 %all-to-all-start = ((bf16[16,32,1152]{2,1,0:T(8,128)(2,1)}), bf16[16,32,1152]{2,1,0:T(8,128)(2,1)S(1)}, u32[]{:S(2)}, u32[]{:S(2)}) async-start(bf16[16,32,1152]{2,1,0:T(8,128)(2,1)} %bitcast.4), calls=%async_computation | async-start | bytes 2359296 | tf_op jit(solution)/shard_map/all_to_all | solution.py:75
  15.8 8.2 %collective-permute-start.10 = (s32[512]{0:T(512)S(1)}, s32[512]{0:T(512)S(1)}, u32[]{:S(2)}, u32[]{:S(2)}) collective-permute-start(s32[512]{0:T(512)S(1)} %copy-done.9), channel_id=1, source_target_pairs={{0,16},{16,0},{1,17},{17,1},{2,18},{18,2},{3,19},{19,3},{4,20},{20... | collective-permute-start | bytes 6152 | tf_op jit(solution)/shard_map/ppermute | solution.py:48
  18.7 5.2 %copy-start.8 = (bf16[32,1152]{1,0:T(8,128)(2,1)S(1)}, bf16[32,1152]{1,0:T(8,128)(2,1)}, u32[]{:S(2)}) copy-start(bf16[32,1152]{1,0:T(8,128)(2,1)} %param.9) | copy-start | bytes 221188
  20.1 5.6 %collective-permute-start.3 = (bf16[2,32,1152]{2,1,0:T(8,128)(2,1)S(1)}, bf16[2,32,1152]{2,1,0:T(8,128)(2,1)S(1)}, u32[]{:S(2)}, u32[]{:S(2)}) collective-permute-start(bf16[2,32,1152]{2,1,0:T(8,128)(2,1)S(1)} %get-tuple-element.62), channel_id=1, source_target_pairs={{0,12},{4,0},{8,4},{12,8},{1,13},{5,1},{9,5},{13,9},{2,14},{6,2},{... | collective-permute-start | bytes 442376 | tf_op jit(solution)/shard_map/ppermute | solution.py:56
  22.9 5.8 %collective-permute-start.2 = (bf16[2,32,1152]{2,1,0:T(8,128)(2,1)S(1)}, bf16[2,32,1152]{2,1,0:T(8,128)(2,1)S(1)}, u32[]{:S(2)}, u32[]{:S(2)}) collective-permute-start(bf16[2,32,1152]{2,1,0:T(8,128)(2,1)S(1)} %get-tuple-element.63), channel_id=1, source_target_pairs={{0,8},{4,12},{8,0},{12,4},{1,9},{5,13},{9,1},{13,5},{2,10},{6,14},... | collective-permute-start | bytes 442376 | tf_op jit(solution)/shard_map/ppermute | solution.py:56
  23.2 9.2 %collective-permute-start.1 = (bf16[2,32,1152]{2,1,0:T(8,128)(2,1)S(1)}, bf16[2,32,1152]{2,1,0:T(8,128)(2,1)S(1)}, u32[]{:S(2)}, u32[]{:S(2)}) collective-permute-start(bf16[2,32,1152]{2,1,0:T(8,128)(2,1)S(1)} %get-tuple-element.61), channel_id=1, source_target_pairs={{0,4},{4,8},{8,12},{12,0},{1,5},{5,9},{9,13},{13,1},{2,6},{6,10},{... | collective-permute-start | bytes 442376 | tf_op jit(solution)/shard_map/ppermute | solution.py:56
  24.7 25.4 %copy-start.3 = (bf16[32,1152]{1,0:T(8,128)(2,1)S(1)}, bf16[32,1152]{1,0:T(8,128)(2,1)}, u32[]{:S(2)}) copy-start(bf16[32,1152]{1,0:T(8,128)(2,1)} %base.1) | copy-start | bytes 221188
  32.6 12.2 %collective-permute-start.4 = (bf16[2,32,1152]{2,1,0:T(8,128)(2,1)S(1)}, bf16[2,32,1152]{2,1,0:T(8,128)(2,1)S(1)}, u32[]{:S(2)}, u32[]{:S(2)}) collective-permute-start(bf16[2,32,1152]{2,1,0:T(8,128)(2,1)S(1)} %fusion.7), channel_id=1, source_target_pairs={{0,2},{2,0},{16,18},{18,16},{1,3},{3,1},{17,19},{19,17},{4,6},{6,4... | collective-permute-start | bytes 442376 | tf_op jit(solution)/shard_map/ppermute | solution.py:71
  35.2 9.5 %collective-permute-start.6 = (bf16[2,32,1152]{2,1,0:T(8,128)(2,1)S(1)}, bf16[2,32,1152]{2,1,0:T(8,128)(2,1)S(1)}, u32[]{:S(2)}, u32[]{:S(2)}) collective-permute-start(bf16[2,32,1152]{2,1,0:T(8,128)(2,1)S(1)} %fusion.7), channel_id=1, source_target_pairs={{0,18},{2,16},{16,2},{18,0},{1,19},{3,17},{17,3},{19,1},{4,22},{6,... | collective-permute-start | bytes 442376 | tf_op jit(solution)/shard_map/ppermute | solution.py:71
  35.6 14.4 %collective-permute-start.5 = (bf16[2,32,1152]{2,1,0:T(8,128)(2,1)S(1)}, bf16[2,32,1152]{2,1,0:T(8,128)(2,1)S(1)}, u32[]{:S(2)}, u32[]{:S(2)}) collective-permute-start(bf16[2,32,1152]{2,1,0:T(8,128)(2,1)S(1)} %fusion.7), channel_id=1, source_target_pairs={{0,16},{2,18},{16,0},{18,2},{1,17},{3,19},{17,1},{19,3},{4,20},{6,... | collective-permute-start | bytes 442376 | tf_op jit(solution)/shard_map/ppermute | solution.py:71
  51.1 25.3 %all-to-all-start.1 = ((bf16[8,32,1152]{2,1,0:T(8,128)(2,1)}), bf16[8,32,1152]{2,1,0:T(8,128)(2,1)S(1)}, u32[]{:S(2)}, u32[]{:S(2)}) async-start(bf16[8,32,1152]{2,1,0:T(8,128)(2,1)} %get-tuple-element.34), calls=%async_computation.1 | async-start | bytes 1179648 | tf_op jit(solution)/shard_map/all_to_all | solution.py:75
  57.1 7.6 %collective-permute-start.9 = (bf16[2,2,32,1152]{3,2,1,0:T(8,128)(2,1)S(1)}, bf16[2,2,32,1152]{3,2,1,0:T(8,128)(2,1)S(1)}, u32[]{:S(2)}, u32[]{:S(2)}) collective-permute-start(bf16[2,2,32,1152]{3,2,1,0:T(8,128)(2,1)S(1)} %pad_maximum_fusion.3), channel_id=1, source_target_pairs={{0,12},{4,0},{8,4},{12,8},{1,13},{5,1},{9,5},{13,9},{2,14},{6,2},{... | collective-permute-start | bytes 884744 | tf_op jit(solution)/shard_map/ppermute | solution.py:56
  57.1 8.6 %collective-permute-start.8 = (bf16[2,2,32,1152]{3,2,1,0:T(8,128)(2,1)S(1)}, bf16[2,2,32,1152]{3,2,1,0:T(8,128)(2,1)S(1)}, u32[]{:S(2)}, u32[]{:S(2)}) collective-permute-start(bf16[2,2,32,1152]{3,2,1,0:T(8,128)(2,1)S(1)} %pad_maximum_fusion.3), channel_id=1, source_target_pairs={{0,8},{4,12},{8,0},{12,4},{1,9},{5,13},{9,1},{13,5},{2,10},{6,14},... | collective-permute-start | bytes 884744 | tf_op jit(solution)/shard_map/ppermute | solution.py:56
  57.2 16.7 %collective-permute-start.7 = (bf16[2,2,32,1152]{3,2,1,0:T(8,128)(2,1)S(1)}, bf16[2,2,32,1152]{3,2,1,0:T(8,128)(2,1)S(1)}, u32[]{:S(2)}, u32[]{:S(2)}) collective-permute-start(bf16[2,2,32,1152]{3,2,1,0:T(8,128)(2,1)S(1)} %pad_maximum_fusion.3), channel_id=1, source_target_pairs={{0,4},{4,8},{8,12},{12,0},{1,5},{5,9},{9,13},{13,1},{2,6},{6,10},{... | collective-permute-start | bytes 884744 | tf_op jit(solution)/shard_map/ppermute | solution.py:56
  76.5 3.3 %collective-permute-start.11 = (bf16[512,1152]{1,0:T(8,128)(2,1)S(1)}, bf16[512,1152]{1,0:T(8,128)(2,1)S(1)}, u32[]{:S(2)}, u32[]{:S(2)}) collective-permute-start(bf16[512,1152]{1,0:T(8,128)(2,1)S(1)} %bitcast.82), channel_id=1, source_target_pairs={{0,1},{1,0},{2,3},{3,2},{4,5},{5,4},{6,7},{7,6},{8,9},{9,8},{10,11... | collective-permute-start | bytes 3538952 | tf_op jit(solution)/shard_map/ppermute | solution.py:48
  83.8 4.5 %collective-permute-start.12 = (bf16[512,1152]{1,0:T(8,128)(2,1)}, bf16[512,1152]{1,0:T(8,128)(2,1)}, u32[]{:S(2)}, u32[]{:S(2)}) collective-permute-start(bf16[512,1152]{1,0:T(8,128)(2,1)} %get-tuple-element.40), channel_id=1, source_target_pairs={{0,1},{1,0},{2,3},{3,2},{4,5},{5,4},{6,7},{7,6},{8,9},{9,8},{10,11... | collective-permute-start | bytes 3538952 | tf_op jit(solution)/shard_map/ppermute | solution.py:48
  83.9 23.9 %all-to-all-start.2 = ((bf16[8,32,1152]{2,1,0:T(8,128)(2,1)}), bf16[8,32,1152]{2,1,0:T(8,128)(2,1)S(1)}, u32[]{:S(2)}, u32[]{:S(2)}) async-start(bf16[8,32,1152]{2,1,0:T(8,128)(2,1)} %bitcast.28), calls=%async_computation.2 | async-start | bytes 1179648 | tf_op jit(solution)/shard_map/all_to_all | solution.py:75
  90.0 22.6 %collective-permute-start.15 = (bf16[4,32,1152]{2,1,0:T(8,128)(2,1)S(1)}, bf16[4,32,1152]{2,1,0:T(8,128)(2,1)S(1)}, u32[]{:S(2)}, u32[]{:S(2)}) collective-permute-start(bf16[4,32,1152]{2,1,0:T(8,128)(2,1)S(1)} %bitcast.93), channel_id=1, source_target_pairs={{0,4},{4,8},{8,12},{12,0},{1,5},{5,9},{9,13},{13,1},{2,6},{6,10},{... | collective-permute-start | bytes 884744 | tf_op jit(solution)/shard_map/ppermute | solution.py:56
  90.1 22.5 %collective-permute-start.14 = (bf16[4,32,1152]{2,1,0:T(8,128)(2,1)S(1)}, bf16[4,32,1152]{2,1,0:T(8,128)(2,1)S(1)}, u32[]{:S(2)}, u32[]{:S(2)}) collective-permute-start(bf16[4,32,1152]{2,1,0:T(8,128)(2,1)S(1)} %bitcast.92), channel_id=1, source_target_pairs={{0,8},{4,12},{8,0},{12,4},{1,9},{5,13},{9,1},{13,5},{2,10},{6,14},... | collective-permute-start | bytes 884744 | tf_op jit(solution)/shard_map/ppermute | solution.py:56
  92.2 20.5 %collective-permute-start.13 = (bf16[4,32,1152]{2,1,0:T(8,128)(2,1)S(1)}, bf16[4,32,1152]{2,1,0:T(8,128)(2,1)S(1)}, u32[]{:S(2)}, u32[]{:S(2)}) collective-permute-start(bf16[4,32,1152]{2,1,0:T(8,128)(2,1)S(1)} %bitcast.91), channel_id=1, source_target_pairs={{0,12},{4,0},{8,4},{12,8},{1,13},{5,1},{9,5},{13,9},{2,14},{6,2},{... | collective-permute-start | bytes 884744 | tf_op jit(solution)/shard_map/ppermute | solution.py:56
  108.9 34.3 %all-to-all-start.4 = ((bf16[16,32,1152]{2,1,0:T(8,128)(2,1)}), bf16[16,32,1152]{2,1,0:T(8,128)(2,1)S(1)}, u32[]{:S(2)}, u32[]{:S(2)}) async-start(bf16[16,32,1152]{2,1,0:T(8,128)(2,1)} %get-tuple-element.47), calls=%async_computation.4 | async-start | bytes 2359296 | tf_op jit(solution)/shard_map/all_to_all | solution.py:75
  112.9 7.0 %collective-permute-start.18 = (bf16[2,40,1152]{2,1,0:T(8,128)(2,1)S(1)}, bf16[2,40,1152]{2,1,0:T(8,128)(2,1)S(1)}, u32[]{:S(2)}, u32[]{:S(2)}) collective-permute-start(bf16[2,40,1152]{2,1,0:T(8,128)(2,1)S(1)} %get-tuple-element.65), channel_id=1, source_target_pairs={{0,18},{2,16},{16,2},{18,0},{1,19},{3,17},{17,3},{19,1},{4,22},{6,... | collective-permute-start | bytes 552968 | tf_op jit(solution)/shard_map/ppermute | solution.py:71
  115.0 5.1 %collective-permute-start.17 = (bf16[2,40,1152]{2,1,0:T(8,128)(2,1)S(1)}, bf16[2,40,1152]{2,1,0:T(8,128)(2,1)S(1)}, u32[]{:S(2)}, u32[]{:S(2)}) collective-permute-start(bf16[2,40,1152]{2,1,0:T(8,128)(2,1)S(1)} %get-tuple-element.65), channel_id=1, source_target_pairs={{0,16},{2,18},{16,0},{18,2},{1,17},{3,19},{17,1},{19,3},{4,20},{6,... | collective-permute-start | bytes 552968 | tf_op jit(solution)/shard_map/ppermute | solution.py:71
  115.0 24.0 %copy-start.6 = (bf16[512,269]{0,1:T(8,128)(2,1)S(1)}, bf16[512,269]{0,1:T(8,128)(2,1)}, u32[]{:S(2)}) copy-start(bf16[512,269]{0,1:T(8,128)(2,1)} %param.10) | copy-start | bytes 826372
  115.1 9.9 %collective-permute-start.16 = (bf16[2,40,1152]{2,1,0:T(8,128)(2,1)S(1)}, bf16[2,40,1152]{2,1,0:T(8,128)(2,1)S(1)}, u32[]{:S(2)}, u32[]{:S(2)}) collective-permute-start(bf16[2,40,1152]{2,1,0:T(8,128)(2,1)S(1)} %get-tuple-element.64), channel_id=1, source_target_pairs={{0,2},{2,0},{16,18},{18,16},{1,3},{3,1},{17,19},{19,17},{4,6},{6,4... | collective-permute-start | bytes 552968 | tf_op jit(solution)/shard_map/ppermute | solution.py:71
  125.1 13.9 %copy-start.7 = (bf16[512,269]{0,1:T(8,128)(2,1)S(1)}, bf16[512,269]{0,1:T(8,128)(2,1)}, u32[]{:S(2)}) copy-start(bf16[512,269]{0,1:T(8,128)(2,1)} %param.13) | copy-start | bytes 826372
  125.1 4.8 %collective-permute-start.21 = (bf16[2,40,1152]{2,1,0:T(8,128)(2,1)S(1)}, bf16[2,40,1152]{2,1,0:T(8,128)(2,1)S(1)}, u32[]{:S(2)}, u32[]{:S(2)}) collective-permute-start(bf16[2,40,1152]{2,1,0:T(8,128)(2,1)S(1)} %add_convert_fusion.2), channel_id=1, source_target_pairs={{0,12},{4,0},{8,4},{12,8},{1,13},{5,1},{9,5},{13,9},{2,14},{6,2},{... | collective-permute-start | bytes 552968 | tf_op jit(solution)/shard_map/ppermute | solution.py:56
  126.1 6.0 %collective-permute-start.20 = (bf16[2,40,1152]{2,1,0:T(8,128)(2,1)S(1)}, bf16[2,40,1152]{2,1,0:T(8,128)(2,1)S(1)}, u32[]{:S(2)}, u32[]{:S(2)}) collective-permute-start(bf16[2,40,1152]{2,1,0:T(8,128)(2,1)S(1)} %add_convert_fusion.2), channel_id=1, source_target_pairs={{0,8},{4,12},{8,0},{12,4},{1,9},{5,13},{9,1},{13,5},{2,10},{6,14},... | collective-permute-start | bytes 552968 | tf_op jit(solution)/shard_map/ppermute | solution.py:56
  126.1 11.4 %collective-permute-start.19 = (bf16[2,40,1152]{2,1,0:T(8,128)(2,1)S(1)}, bf16[2,40,1152]{2,1,0:T(8,128)(2,1)S(1)}, u32[]{:S(2)}, u32[]{:S(2)}) collective-permute-start(bf16[2,40,1152]{2,1,0:T(8,128)(2,1)S(1)} %add_convert_fusion.2), channel_id=1, source_target_pairs={{0,4},{4,8},{8,12},{12,0},{1,5},{5,9},{9,13},{13,1},{2,6},{6,10},{... | collective-permute-start | bytes 552968 | tf_op jit(solution)/shard_map/ppermute | solution.py:56
  137.6 3.3 %copy-start.2 = (bf16[269,1152]{1,0:T(8,128)(2,1)S(1)}, bf16[269,1152]{1,0:T(8,128)(2,1)}, u32[]{:S(2)}) copy-start(bf16[269,1152]{1,0:T(8,128)(2,1)} %proj.2) | copy-start | bytes 1859332
  137.7 3.2 %collective-permute-start.22 = (bf16[4,2,40,1152]{3,2,1,0:T(8,128)(2,1)S(1)}, bf16[4,2,40,1152]{3,2,1,0:T(8,128)(2,1)S(1)}, u32[]{:S(2)}, u32[]{:S(2)}) collective-permute-start(bf16[4,2,40,1152]{3,2,1,0:T(8,128)(2,1)S(1)} %pad_maximum_fusion.1.own), channel_id=1, source_target_pairs={{0,1},{1,0},{2,3},{3,2},{4,5},{5,4},{6,7},{7,6},{8,9},{9,8},{10,11... | collective-permute-start | bytes 2211848 | tf_op jit(solution)/shard_map/ppermute | solution.py:48
  139.2 4.1 %copy-start = (bf16[269,1152]{1,0:T(8,128)(2,1)S(1)}, bf16[269,1152]{1,0:T(8,128)(2,1)}, u32[]{:S(2)}) copy-start(bf16[269,1152]{1,0:T(8,128)(2,1)} %proj.3) | copy-start | bytes 1859332
  145.6 6.4 %collective-permute-start.23 = (bf16[4,2,80,256]{3,2,1,0:T(8,128)(2,1)S(1)}, bf16[4,2,80,256]{3,2,1,0:T(8,128)(2,1)S(1)}, u32[]{:S(2)}, u32[]{:S(2)}) collective-permute-start(bf16[4,2,80,256]{3,2,1,0:T(8,128)(2,1)S(1)} %get-tuple-element.50), channel_id=1, source_target_pairs={{0,1},{1,0},{2,3},{3,2},{4,5},{5,4},{6,7},{7,6},{8,9},{9,8},{10,11... | collective-permute-start | bytes 983048 | tf_op jit(solution)/shard_map/ppermute | solution.py:48
  147.4 23.2 %all-to-all-start.3 = ((bf16[16,80,256]{2,1,0:T(8,128)(2,1)}), bf16[16,80,256]{2,1,0:T(8,128)(2,1)S(1)}, u32[]{:S(2)}, u32[]{:S(2)}) async-start(bf16[16,80,256]{2,1,0:T(8,128)(2,1)} %get-tuple-element.45), calls=%async_computation.3 | async-start | bytes 1310720 | tf_op jit(solution)/shard_map/all_to_all | solution.py:75
  152.1 3.7 %collective-permute-start.26 = (bf16[2,80,256]{2,1,0:T(8,128)(2,1)S(1)}, bf16[2,80,256]{2,1,0:T(8,128)(2,1)S(1)}, u32[]{:S(2)}, u32[]{:S(2)}) collective-permute-start(bf16[2,80,256]{2,1,0:T(8,128)(2,1)S(1)} %get-tuple-element.67), channel_id=1, source_target_pairs={{0,12},{4,0},{8,4},{12,8},{1,13},{5,1},{9,5},{13,9},{2,14},{6,2},{... | collective-permute-start | bytes 245768 | tf_op jit(solution)/shard_map/ppermute | solution.py:56
  152.7 4.8 %collective-permute-start.25 = (bf16[2,80,256]{2,1,0:T(8,128)(2,1)S(1)}, bf16[2,80,256]{2,1,0:T(8,128)(2,1)S(1)}, u32[]{:S(2)}, u32[]{:S(2)}) collective-permute-start(bf16[2,80,256]{2,1,0:T(8,128)(2,1)S(1)} %get-tuple-element.68), channel_id=1, source_target_pairs={{0,8},{4,12},{8,0},{12,4},{1,9},{5,13},{9,1},{13,5},{2,10},{6,14},... | collective-permute-start | bytes 245768 | tf_op jit(solution)/shard_map/ppermute | solution.py:56
  153.1 7.0 %collective-permute-start.24 = (bf16[2,80,256]{2,1,0:T(8,128)(2,1)S(1)}, bf16[2,80,256]{2,1,0:T(8,128)(2,1)S(1)}, u32[]{:S(2)}, u32[]{:S(2)}) collective-permute-start(bf16[2,80,256]{2,1,0:T(8,128)(2,1)S(1)} %get-tuple-element.66), channel_id=1, source_target_pairs={{0,4},{4,8},{8,12},{12,0},{1,5},{5,9},{9,13},{13,1},{2,6},{6,10},{... | collective-permute-start | bytes 245768 | tf_op jit(solution)/shard_map/ppermute | solution.py:56
  160.2 4.8 %collective-permute-start.27 = (bf16[80,256]{1,0:T(8,128)(2,1)S(1)}, bf16[80,256]{1,0:T(8,128)(2,1)S(1)}, u32[]{:S(2)}, u32[]{:S(2)}) collective-permute-start(bf16[80,256]{1,0:T(8,128)(2,1)S(1)} %get-tuple-element.70), channel_id=1, source_target_pairs={{0,2},{2,0},{1,3},{3,1},{4,6},{6,4},{5,7},{7,5},{8,10},{10,8},{9,1... | collective-permute-start | bytes 122888 | tf_op jit(solution)/shard_map/ppermute | solution.py:48

commit v4 on v3

--- a/solution.py
+++ b/solution.py
@@ -241,7 +241,7 @@
             back[at, k, c] = own[d, k, :rows]
             back[at, k, 1 - c] = other[d, k, :rows]
             for part in (own, other):
-                loss = loss + part[d, k, rows:].astype(f32)[:, :128]
+                loss = loss + part[d, k, :, :128].astype(f32)[rows:]
     total = jnp.sum(jnp.sum(loss, axis=1, keepdims=True), axis=0, keepdims=True)
     high = total.astype(bf16).astype(f32)
     grad = back[...].reshape(-1, width)

time: 175 us -> 175 us (level)
  no operation moved by 1% of the time
where the time goes in v4:
time: 175 us; the launch traced here: 173 us
  waiting for transfers between devices  88.3 us (50%)
  starting transfers between devices  55.5 us (32%)
  Pallas kernels  15.3 us (9%)
  between operations  4.16 us (2%)
  other arithmetic  4.11 us (2%)
  matrix products  4.02 us (2%)
    ppermute x15, waiting for transfers between devices, shift(): lax.ppermute(block, axis, [(i, (i + step) % count) for i in range(count)])  40.3 us
    all_to_all x5, starting transfers between devices, exchange(): return lax.all_to_all(blocks, axis, 0, 0)  26.4 us
    ppermute x6, waiting for transfers between devices, turn_x(): lax.ppermute(block, ('xl', 'xh'), [(i, i ^ 2 * a + b) for i in range(4)])  22.5 us
    all_to_all x5, waiting for transfers between devices, exchange(): return lax.all_to_all(blocks, axis, 0, 0)  22.1 us
    ppermute x15, starting transfers between devices, shift(): lax.ppermute(block, axis, [(i, (i + step) % count) for i in range(count)])  11.3 us
    ppermute x7, starting transfers between devices, swap(): return lax.ppermute(block, axis, SWAP)  11 us
    ppermute x6, starting transfers between devices, turn_x(): lax.ppermute(block, ('xl', 'xh'), [(i, i ^ 2 * a + b) for i in range(4)])  6.83 us
    pallas_call x1, Pallas kernels, rest_call(): pl.pallas_call(rest_kernel, out_shape=(like(text, bf16), like(image, bf16...  4.05 us
  transfers between devices with their start and end apart: 33, of which 22 were waited for; matrix products, arithmetic and copies ran while one was open for 3% of the time, Pallas kernels for 4%

profile of v4, /device:TPU:1, one launch (start us, length us, event | category | flops | bytes accessed | tf_op | source)
XLA Modules:
  0.0 173.1 jit_solution(16694207408002453042)
XLA Ops:
  0.7 3.2 %convolution_convert_fusion.1 = bf16[512,1152]{1,0:T(8,128)(2,1)} fusion(bf16[512,269]{0,1:T(8,128)(2,1)} %param.13, bf16[269,1152]{1,0:T(8,128)(2,1)} %proj.3), kind=kOutput, calls=%fused_computation.2 | convolution fusion | flops 317915136 | bytes 2074880 | tf_op jit(solution)/shard_map/dot_general | solution.py:32
  3.8 0.9 convolution_convert_fusion
  4.8 3.3 %collective-permute-start = (bf16[4,2,32,1152]{3,2,1,0:T(8,128)(2,1)S(1)}, bf16[4,2,32,1152]{3,2,1,0:T(8,128)(2,1)S(1)}, u32[]{:S(2)}, u32[]{:S(2)}) collective-permute-start(bf16[4,2,32,1152]{3,2,1,0:T(8,128)(2,1)S(1)} %dynamic-slice_bitcast_fusion), channel_id=1, source_target_pairs={{0,1},{1,0},{2,3},{3,2},{4,5},{5,4},{6,7},{7,6},{8,9},{9,8},{10,11... | collective-permute-start | bytes 1769480 | tf_op jit(solution)/shard_map/ppermute | solution.py:48
  8.1 7.7 %all-to-all-start = ((bf16[16,32,1152]{2,1,0:T(8,128)(2,1)}), bf16[16,32,1152]{2,1,0:T(8,128)(2,1)S(1)}, u32[]{:S(2)}, u32[]{:S(2)}) async-start(bf16[16,32,1152]{2,1,0:T(8,128)(2,1)} %bitcast.4), calls=%async_computation | async-start | bytes 2359296 | tf_op jit(solution)/shard_map/all_to_all | solution.py:75
  15.8 1.4 collective-permute-start.10
  18.7 1.3 fusion
  20.1 2.8 %collective-permute-start.3 = (bf16[2,32,1152]{2,1,0:T(8,128)(2,1)S(1)}, bf16[2,32,1152]{2,1,0:T(8,128)(2,1)S(1)}, u32[]{:S(2)}, u32[]{:S(2)}) collective-permute-start(bf16[2,32,1152]{2,1,0:T(8,128)(2,1)S(1)} %get-tuple-element.62), channel_id=1, source_target_pairs={{0,12},{4,0},{8,4},{12,8},{1,13},{5,1},{9,5},{13,9},{2,14},{6,2},{... | collective-permute-start | bytes 442376 | tf_op jit(solution)/shard_map/ppermute | solution.py:56
  24.7 0.9 collective-permute-done.3
  25.6 3.0 %collective-permute-done.2 = bf16[2,32,1152]{2,1,0:T(8,128)(2,1)S(1)} collective-permute-done((bf16[2,32,1152]{2,1,0:T(8,128)(2,1)S(1)}, bf16[2,32,1152]{2,1,0:T(8,128)(2,1)S(1)}, u32[]{:S(2)}, u32[]{:S(2)}) %collective-permute-start.2) | collective-permute-done | bytes 147488 | tf_op jit(solution)/shard_map/ppermute | solution.py:56
  28.7 3.8 %collective-permute-done.1 = bf16[2,32,1152]{2,1,0:T(8,128)(2,1)S(1)} collective-permute-done((bf16[2,32,1152]{2,1,0:T(8,128)(2,1)S(1)}, bf16[2,32,1152]{2,1,0:T(8,128)(2,1)S(1)}, u32[]{:S(2)}, u32[]{:S(2)}) %collective-permute-start.1) | collective-permute-done | bytes 147488 | tf_op jit(solution)/shard_map/ppermute | solution.py:56
  32.6 2.5 %collective-permute-start.4 = (bf16[2,32,1152]{2,1,0:T(8,128)(2,1)S(1)}, bf16[2,32,1152]{2,1,0:T(8,128)(2,1)S(1)}, u32[]{:S(2)}, u32[]{:S(2)}) collective-permute-start(bf16[2,32,1152]{2,1,0:T(8,128)(2,1)S(1)} %fusion.7), channel_id=1, source_target_pairs={{0,2},{2,0},{16,18},{18,16},{1,3},{3,1},{17,19},{19,17},{4,6},{6,4... | collective-permute-start | bytes 442376 | tf_op jit(solution)/shard_map/ppermute | solution.py:71
  35.6 9.1 %collective-permute-done.4 = bf16[2,32,1152]{2,1,0:T(8,128)(2,1)S(1)} collective-permute-done((bf16[2,32,1152]{2,1,0:T(8,128)(2,1)S(1)}, bf16[2,32,1152]{2,1,0:T(8,128)(2,1)S(1)}, u32[]{:S(2)}, u32[]{:S(2)}) %collective-permute-start.4) | collective-permute-done | bytes 147488 | tf_op jit(solution)/shard_map/ppermute | solution.py:71
  44.8 5.2 %collective-permute-done.5 = bf16[2,32,1152]{2,1,0:T(8,128)(2,1)S(1)} collective-permute-done((bf16[2,32,1152]{2,1,0:T(8,128)(2,1)S(1)}, bf16[2,32,1152]{2,1,0:T(8,128)(2,1)S(1)}, u32[]{:S(2)}, u32[]{:S(2)}) %collective-permute-start.5) | collective-permute-done | bytes 147488 | tf_op jit(solution)/shard_map/ppermute | solution.py:71
  50.1 1.0 spread.2
  51.1 6.0 %all-to-all-start.1 = ((bf16[8,32,1152]{2,1,0:T(8,128)(2,1)}), bf16[8,32,1152]{2,1,0:T(8,128)(2,1)S(1)}, u32[]{:S(2)}, u32[]{:S(2)}) async-start(bf16[8,32,1152]{2,1,0:T(8,128)(2,1)} %get-tuple-element.34), calls=%async_computation.1 | async-start | bytes 1179648 | tf_op jit(solution)/shard_map/all_to_all | solution.py:75
  57.2 1.4 collective-permute-start.7
  58.6 6.2 %collective-permute-done.9 = bf16[2,2,32,1152]{3,2,1,0:T(8,128)(2,1)S(1)} collective-permute-done((bf16[2,2,32,1152]{3,2,1,0:T(8,128)(2,1)S(1)}, bf16[2,2,32,1152]{3,2,1,0:T(8,128)(2,1)S(1)}, u32[]{:S(2)}, u32[]{:S(2)}) %collective-permute-start.9) | collective-permute-done | bytes 294944 | tf_op jit(solution)/shard_map/ppermute | solution.py:56
  64.7 1.0 collective-permute-done.8
  65.7 8.2 %collective-permute-done.7 = bf16[2,2,32,1152]{3,2,1,0:T(8,128)(2,1)S(1)} collective-permute-done((bf16[2,2,32,1152]{3,2,1,0:T(8,128)(2,1)S(1)}, bf16[2,2,32,1152]{3,2,1,0:T(8,128)(2,1)S(1)}, u32[]{:S(2)}, u32[]{:S(2)}) %collective-permute-start.7) | collective-permute-done | bytes 294944 | tf_op jit(solution)/shard_map/ppermute | solution.py:56
  74.1 2.3 %all-to-all-done.1 = bf16[8,32,1152]{2,1,0:T(8,128)(2,1)S(1)} async-done(((bf16[8,32,1152]{2,1,0:T(8,128)(2,1)}), bf16[8,32,1152]{2,1,0:T(8,128)(2,1)S(1)}, u32[]{:S(2)}, u32[]{:S(2)}) %all-to-all-start.1) | async-done | bytes 589856 | tf_op jit(solution)/shard_map/all_to_all | solution.py:75
  77.0 2.8 %score.1 = (f32[256,1152]{1,0:T(8,128)S(1)}, bf16[256,1152]{1,0:T(8,128)(2,1)S(1)}, bf16[512,1152]{1,0:T(8,128)(2,1)S(1)}, f32[1,512]{1,0:T(1,128)S(1)}) custom-call(f32[2]{0:T(128)S(1)} %pad_maximum_fusion.5.params, s32[2]{0:T(128)S(1)} %pad_add_fusion.1.base, bf16[512,1152]{1,0:T(8,128)(2,1)S(1)} %bitcast.83, bf16[256,1152]{1,0:T(8,128)(2,1)S(1)} %bitcast.79, ...), custom_call_target="tpu_custom_call" | custom-call | tf_op jit(solution)/shard_map/score/pallas_call | solution.py:161
  79.8 4.1 %score_rest.1 = (bf16[256,1152]{1,0:T(8,128)(2,1)}, bf16[512,1152]{1,0:T(8,128)(2,1)}, bf16[8,1152]{1,0:T(8,128)(2,1)S(1)}) custom-call(f32[2]{0:T(128)S(1)} %pad_maximum_fusion.5.params, s32[2]{0:T(128)S(1)} %pad_add_fusion.1.base, bf16[512,1152]{1,0:T(8,128)(2,1)S(1)} %collective-permute-done.11.image, bf16[256,1152]{1,0:T(8,128)(2,1)S(1)} %bitcast.80, ...), custom_call_target="tpu_custom_call" | custom-call | tf_op jit(solution)/shard_map/score_rest/pallas_call | solution.py:177
  83.9 4.5 %all-to-all-start.2 = ((bf16[8,32,1152]{2,1,0:T(8,128)(2,1)}), bf16[8,32,1152]{2,1,0:T(8,128)(2,1)S(1)}, u32[]{:S(2)}, u32[]{:S(2)}) async-start(bf16[8,32,1152]{2,1,0:T(8,128)(2,1)} %bitcast.28), calls=%async_computation.2 | async-start | bytes 1179648 | tf_op jit(solution)/shard_map/all_to_all | solution.py:75
  88.4 1.5 add_convert_fusion
  90.1 2.1 %collective-permute-start.14 = (bf16[4,32,1152]{2,1,0:T(8,128)(2,1)S(1)}, bf16[4,32,1152]{2,1,0:T(8,128)(2,1)S(1)}, u32[]{:S(2)}, u32[]{:S(2)}) collective-permute-start(bf16[4,32,1152]{2,1,0:T(8,128)(2,1)S(1)} %bitcast.92), channel_id=1, source_target_pairs={{0,8},{4,12},{8,0},{12,4},{1,9},{5,13},{9,1},{13,5},{2,10},{6,14},... | collective-permute-start | bytes 884744 | tf_op jit(solution)/shard_map/ppermute | solution.py:56
  92.8 14.9 %all-to-all-done.2.parts = bf16[8,32,1152]{2,1,0:T(8,128)(2,1)S(1)} async-done(((bf16[8,32,1152]{2,1,0:T(8,128)(2,1)}), bf16[8,32,1152]{2,1,0:T(8,128)(2,1)S(1)}, u32[]{:S(2)}, u32[]{:S(2)}) %all-to-all-start.2) | async-done | bytes 589856 | tf_op jit(solution)/shard_map/all_to_all | solution.py:75
  107.7 1.2 spread.3
  108.9 3.7 %all-to-all-start.4 = ((bf16[16,32,1152]{2,1,0:T(8,128)(2,1)}), bf16[16,32,1152]{2,1,0:T(8,128)(2,1)S(1)}, u32[]{:S(2)}, u32[]{:S(2)}) async-start(bf16[16,32,1152]{2,1,0:T(8,128)(2,1)} %get-tuple-element.47), calls=%async_computation.4 | async-start | bytes 2359296 | tf_op jit(solution)/shard_map/all_to_all | solution.py:75
  112.9 2.2 %collective-permute-start.18 = (bf16[2,40,1152]{2,1,0:T(8,128)(2,1)S(1)}, bf16[2,40,1152]{2,1,0:T(8,128)(2,1)S(1)}, u32[]{:S(2)}, u32[]{:S(2)}) collective-permute-start(bf16[2,40,1152]{2,1,0:T(8,128)(2,1)S(1)} %get-tuple-element.65), channel_id=1, source_target_pairs={{0,18},{2,16},{16,2},{18,0},{1,19},{3,17},{17,3},{19,1},{4,22},{6,... | collective-permute-start | bytes 552968 | tf_op jit(solution)/shard_map/ppermute | solution.py:71
  115.1 1.8 %collective-permute-start.16 = (bf16[2,40,1152]{2,1,0:T(8,128)(2,1)S(1)}, bf16[2,40,1152]{2,1,0:T(8,128)(2,1)S(1)}, u32[]{:S(2)}, u32[]{:S(2)}) collective-permute-start(bf16[2,40,1152]{2,1,0:T(8,128)(2,1)S(1)} %get-tuple-element.64), channel_id=1, source_target_pairs={{0,2},{2,0},{16,18},{18,16},{1,3},{3,1},{17,19},{19,17},{4,6},{6,4... | collective-permute-start | bytes 552968 | tf_op jit(solution)/shard_map/ppermute | solution.py:71
  116.8 3.1 %collective-permute-done.18 = bf16[2,40,1152]{2,1,0:T(8,128)(2,1)S(1)} collective-permute-done((bf16[2,40,1152]{2,1,0:T(8,128)(2,1)S(1)}, bf16[2,40,1152]{2,1,0:T(8,128)(2,1)S(1)}, u32[]{:S(2)}, u32[]{:S(2)}) %collective-permute-start.18) | collective-permute-done | bytes 184352 | tf_op jit(solution)/shard_map/ppermute | solution.py:71
  120.1 4.9 %collective-permute-done.16 = bf16[2,40,1152]{2,1,0:T(8,128)(2,1)S(1)} collective-permute-done((bf16[2,40,1152]{2,1,0:T(8,128)(2,1)S(1)}, bf16[2,40,1152]{2,1,0:T(8,128)(2,1)S(1)}, u32[]{:S(2)}, u32[]{:S(2)}) %collective-permute-start.16) | collective-permute-done | bytes 184352 | tf_op jit(solution)/shard_map/ppermute | solution.py:71
  125.1 1.0 collective-permute-start.21
  126.8 3.1 %collective-permute-done.21 = bf16[2,40,1152]{2,1,0:T(8,128)(2,1)S(1)} collective-permute-done((bf16[2,40,1152]{2,1,0:T(8,128)(2,1)S(1)}, bf16[2,40,1152]{2,1,0:T(8,128)(2,1)S(1)}, u32[]{:S(2)}, u32[]{:S(2)}) %collective-permute-start.21) | collective-permute-done | bytes 184352 | tf_op jit(solution)/shard_map/ppermute | solution.py:56
  129.9 2.3 %collective-permute-done.20 = bf16[2,40,1152]{2,1,0:T(8,128)(2,1)S(1)} collective-permute-done((bf16[2,40,1152]{2,1,0:T(8,128)(2,1)S(1)}, bf16[2,40,1152]{2,1,0:T(8,128)(2,1)S(1)}, u32[]{:S(2)}, u32[]{:S(2)}) %collective-permute-start.20) | collective-permute-done | bytes 184352 | tf_op jit(solution)/shard_map/ppermute | solution.py:56
  132.1 5.4 %collective-permute-done.19 = bf16[2,40,1152]{2,1,0:T(8,128)(2,1)S(1)} collective-permute-done((bf16[2,40,1152]{2,1,0:T(8,128)(2,1)S(1)}, bf16[2,40,1152]{2,1,0:T(8,128)(2,1)S(1)}, u32[]{:S(2)}, u32[]{:S(2)}) %collective-permute-start.19) | collective-permute-done | bytes 184352 | tf_op jit(solution)/shard_map/ppermute | solution.py:56
  137.7 1.3 collective-permute-start.22
  139.2 1.7 collective-permute-done.22.other
  140.9 2.4 %image_weight.1 = (bf16[269,512]{1,0:T(8,128)(2,1)}, bf16[16,80,256]{2,1,0:T(8,128)(2,1)}) custom-call(s32[2]{0:T(128)S(1)} %pad_add_fusion.place, bf16[4,2,40,1152]{3,2,1,0:T(8,128)(2,1)S(1)} %pad_maximum_fusion.1.own, bf16[4,2,40,1152]{3,2,1,0:T(8,128)(2,1)S(1)} %collective-permute-done.22.other, bf16[272,512]{1,0:T(8,128)(2,1)S(1)} %pad.7.acts, ...), custom_call_target="tpu_custom_call" | custom-call | tf_op jit(solution)/shard_map/image_weight/pallas_call | solution.py:255
  143.3 2.3 %text_weight.1 = (bf16[269,512]{1,0:T(8,128)(2,1)}, bf16[4,2,80,256]{3,2,1,0:T(8,128)(2,1)S(1)}, bf16[4,2,80,256]{3,2,1,0:T(8,128)(2,1)S(1)}) custom-call(s32[2]{0:T(128)S(1)} %pad_add_fusion.place, bf16[512,1152]{1,0:T(8,128)(2,1)S(1)} %bitcast.81, bf16[272,512]{1,0:T(8,128)(2,1)S(1)} %pad.8.acts, bf16[269,1152]{1,0:T(8,128)(2,1)S(1)} %copy-done), custom_call_target="tpu_custom_call" | custom-call | tf_op jit(solution)/shard_map/text_weight/pallas_call | solution.py:281
  145.6 1.8 %collective-permute-start.23 = (bf16[4,2,80,256]{3,2,1,0:T(8,128)(2,1)S(1)}, bf16[4,2,80,256]{3,2,1,0:T(8,128)(2,1)S(1)}, u32[]{:S(2)}, u32[]{:S(2)}) collective-permute-start(bf16[4,2,80,256]{3,2,1,0:T(8,128)(2,1)S(1)} %get-tuple-element.50), channel_id=1, source_target_pairs={{0,1},{1,0},{2,3},{3,2},{4,5},{5,4},{6,7},{7,6},{8,9},{9,8},{10,11... | collective-permute-start | bytes 983048 | tf_op jit(solution)/shard_map/ppermute | solution.py:48
  147.4 4.6 %all-to-all-start.3 = ((bf16[16,80,256]{2,1,0:T(8,128)(2,1)}), bf16[16,80,256]{2,1,0:T(8,128)(2,1)S(1)}, u32[]{:S(2)}, u32[]{:S(2)}) async-start(bf16[16,80,256]{2,1,0:T(8,128)(2,1)} %get-tuple-element.45), calls=%async_computation.3 | async-start | bytes 1310720 | tf_op jit(solution)/shard_map/all_to_all | solution.py:75
  153.7 2.1 %collective-permute-done.26 = bf16[2,80,256]{2,1,0:T(8,128)(2,1)S(1)} collective-permute-done((bf16[2,80,256]{2,1,0:T(8,128)(2,1)S(1)}, bf16[2,80,256]{2,1,0:T(8,128)(2,1)S(1)}, u32[]{:S(2)}, u32[]{:S(2)}) %collective-permute-start.26) | collective-permute-done | bytes 81952 | tf_op jit(solution)/shard_map/ppermute | solution.py:56
  155.8 1.7 %collective-permute-done.25 = bf16[2,80,256]{2,1,0:T(8,128)(2,1)S(1)} collective-permute-done((bf16[2,80,256]{2,1,0:T(8,128)(2,1)S(1)}, bf16[2,80,256]{2,1,0:T(8,128)(2,1)S(1)}, u32[]{:S(2)}, u32[]{:S(2)}) %collective-permute-start.25) | collective-permute-done | bytes 81952 | tf_op jit(solution)/shard_map/ppermute | solution.py:56
  157.5 2.5 %collective-permute-done.24 = bf16[2,80,256]{2,1,0:T(8,128)(2,1)S(1)} collective-permute-done((bf16[2,80,256]{2,1,0:T(8,128)(2,1)S(1)}, bf16[2,80,256]{2,1,0:T(8,128)(2,1)S(1)}, u32[]{:S(2)}, u32[]{:S(2)}) %collective-permute-start.24) | collective-permute-done | bytes 81952 | tf_op jit(solution)/shard_map/ppermute | solution.py:56
  160.2 2.5 %collective-permute-start.27 = (bf16[80,256]{1,0:T(8,128)(2,1)S(1)}, bf16[80,256]{1,0:T(8,128)(2,1)S(1)}, u32[]{:S(2)}, u32[]{:S(2)}) collective-permute-start(bf16[80,256]{1,0:T(8,128)(2,1)S(1)} %get-tuple-element.70), channel_id=1, source_target_pairs={{0,2},{2,0},{1,3},{3,1},{4,6},{6,4},{5,7},{7,5},{8,10},{10,8},{9,1... | collective-permute-start | bytes 122888 | tf_op jit(solution)/shard_map/ppermute | solution.py:48
  163.3 1.7 collective-permute-done.27
  165.8 4.8 %all-to-all-done.3.blocks = bf16[16,80,256]{2,1,0:T(8,128)(2,1)S(1)} async-done(((bf16[16,80,256]{2,1,0:T(8,128)(2,1)}), bf16[16,80,256]{2,1,0:T(8,128)(2,1)S(1)}, u32[]{:S(2)}, u32[]{:S(2)}) %all-to-all-start.3) | async-done | bytes 655392 | tf_op jit(solution)/shard_map/all_to_all | solution.py:75
  (86 shorter events, 9.7 us)
Async XLA Ops:
  0.6 3.2 %copy-start.5 = (bf16[512,269]{0,1:T(8,128)(2,1)S(1)}, bf16[512,269]{0,1:T(8,128)(2,1)}, u32[]{:S(2)}) copy-start(bf16[512,269]{0,1:T(8,128)(2,1)} %param.10) | copy-start | bytes 826372
  0.6 3.2 %copy-start.1 = (bf16[269,1152]{1,0:T(8,128)(2,1)S(1)}, bf16[269,1152]{1,0:T(8,128)(2,1)}, u32[]{:S(2)}) copy-start(bf16[269,1152]{1,0:T(8,128)(2,1)} %proj.2) | copy-start | bytes 1859332
  4.7 3.4 %copy-start.4 = (bf16[512,1152]{1,0:T(8,128)(2,1)}, bf16[512,1152]{1,0:T(8,128)(2,1)S(1)}, u32[]{:S(2)}) copy-start(bf16[512,1152]{1,0:T(8,128)(2,1)S(1)} %convolution_convert_fusion) | copy-start | bytes 3538948
  4.8 11.0 %copy-start.9 = (s32[512]{0:T(512)S(1)}, s32[512]{0:T(512)}, u32[]{:S(2)}) copy-start(s32[512]{0:T(512)} %param.15) | copy-start | bytes 6148
  4.8 14.0 %collective-permute-start = (bf16[4,2,32,1152]{3,2,1,0:T(8,128)(2,1)S(1)}, bf16[4,2,32,1152]{3,2,1,0:T(8,128)(2,1)S(1)}, u32[]{:S(2)}, u32[]{:S(2)}) collective-permute-start(bf16[4,2,32,1152]{3,2,1,0:T(8,128)(2,1)S(1)} %dynamic-slice_bitcast_fusion), channel_id=1, source_target_pairs={{0,1},{1,0},{2,3},{3,2},{4,5},{5,4},{6,7},{7,6},{8,9},{9,8},{10,11... | collective-permute-start | bytes 1769480 | tf_op jit(solution)/shard_map/ppermute | solution.py:48
  8.1 42.0 %all-to-all-start = ((bf16[16,32,1152]{2,1,0:T(8,128)(2,1)}), bf16[16,32,1152]{2,1,0:T(8,128)(2,1)S(1)}, u32[]{:S(2)}, u32[]{:S(2)}) async-start(bf16[16,32,1152]{2,1,0:T(8,128)(2,1)} %bitcast.4), calls=%async_computation | async-start | bytes 2359296 | tf_op jit(solution)/shard_map/all_to_all | solution.py:75
  15.8 8.2 %collective-permute-start.10 = (s32[512]{0:T(512)S(1)}, s32[512]{0:T(512)S(1)}, u32[]{:S(2)}, u32[]{:S(2)}) collective-permute-start(s32[512]{0:T(512)S(1)} %copy-done.9), channel_id=1, source_target_pairs={{0,16},{16,0},{1,17},{17,1},{2,18},{18,2},{3,19},{19,3},{4,20},{20... | collective-permute-start | bytes 6152 | tf_op jit(solution)/shard_map/ppermute | solution.py:48
  18.7 5.2 %copy-start.8 = (bf16[32,1152]{1,0:T(8,128)(2,1)S(1)}, bf16[32,1152]{1,0:T(8,128)(2,1)}, u32[]{:S(2)}) copy-start(bf16[32,1152]{1,0:T(8,128)(2,1)} %param.9) | copy-start | bytes 221188
  20.1 5.6 %collective-permute-start.3 = (bf16[2,32,1152]{2,1,0:T(8,128)(2,1)S(1)}, bf16[2,32,1152]{2,1,0:T(8,128)(2,1)S(1)}, u32[]{:S(2)}, u32[]{:S(2)}) collective-permute-start(bf16[2,32,1152]{2,1,0:T(8,128)(2,1)S(1)} %get-tuple-element.62), channel_id=1, source_target_pairs={{0,12},{4,0},{8,4},{12,8},{1,13},{5,1},{9,5},{13,9},{2,14},{6,2},{... | collective-permute-start | bytes 442376 | tf_op jit(solution)/shard_map/ppermute | solution.py:56
  22.9 5.8 %collective-permute-start.2 = (bf16[2,32,1152]{2,1,0:T(8,128)(2,1)S(1)}, bf16[2,32,1152]{2,1,0:T(8,128)(2,1)S(1)}, u32[]{:S(2)}, u32[]{:S(2)}) collective-permute-start(bf16[2,32,1152]{2,1,0:T(8,128)(2,1)S(1)} %get-tuple-element.63), channel_id=1, source_target_pairs={{0,8},{4,12},{8,0},{12,4},{1,9},{5,13},{9,1},{13,5},{2,10},{6,14},... | collective-permute-start | bytes 442376 | tf_op jit(solution)/shard_map/ppermute | solution.py:56
  23.2 9.2 %collective-permute-start.1 = (bf16[2,32,1152]{2,1,0:T(8,128)(2,1)S(1)}, bf16[2,32,1152]{2,1,0:T(8,128)(2,1)S(1)}, u32[]{:S(2)}, u32[]{:S(2)}) collective-permute-start(bf16[2,32,1152]{2,1,0:T(8,128)(2,1)S(1)} %get-tuple-element.61), channel_id=1, source_target_pairs={{0,4},{4,8},{8,12},{12,0},{1,5},{5,9},{9,13},{13,1},{2,6},{6,10},{... | collective-permute-start | bytes 442376 | tf_op jit(solution)/shard_map/ppermute | solution.py:56
  24.7 25.4 %copy-start.3 = (bf16[32,1152]{1,0:T(8,128)(2,1)S(1)}, bf16[32,1152]{1,0:T(8,128)(2,1)}, u32[]{:S(2)}) copy-start(bf16[32,1152]{1,0:T(8,128)(2,1)} %base.1) | copy-start | bytes 221188
  32.6 12.2 %collective-permute-start.4 = (bf16[2,32,1152]{2,1,0:T(8,128)(2,1)S(1)}, bf16[2,32,1152]{2,1,0:T(8,128)(2,1)S(1)}, u32[]{:S(2)}, u32[]{:S(2)}) collective-permute-start(bf16[2,32,1152]{2,1,0:T(8,128)(2,1)S(1)} %fusion.7), channel_id=1, source_target_pairs={{0,2},{2,0},{16,18},{18,16},{1,3},{3,1},{17,19},{19,17},{4,6},{6,4... | collective-permute-start | bytes 442376 | tf_op jit(solution)/shard_map/ppermute | solution.py:71
  35.2 9.5 %collective-permute-start.6 = (bf16[2,32,1152]{2,1,0:T(8,128)(2,1)S(1)}, bf16[2,32,1152]{2,1,0:T(8,128)(2,1)S(1)}, u32[]{:S(2)}, u32[]{:S(2)}) collective-permute-start(bf16[2,32,1152]{2,1,0:T(8,128)(2,1)S(1)} %fusion.7), channel_id=1, source_target_pairs={{0,18},{2,16},{16,2},{18,0},{1,19},{3,17},{17,3},{19,1},{4,22},{6,... | collective-permute-start | bytes 442376 | tf_op jit(solution)/shard_map/ppermute | solution.py:71
  35.6 14.4 %collective-permute-start.5 = (bf16[2,32,1152]{2,1,0:T(8,128)(2,1)S(1)}, bf16[2,32,1152]{2,1,0:T(8,128)(2,1)S(1)}, u32[]{:S(2)}, u32[]{:S(2)}) collective-permute-start(bf16[2,32,1152]{2,1,0:T(8,128)(2,1)S(1)} %fusion.7), channel_id=1, source_target_pairs={{0,16},{2,18},{16,0},{18,2},{1,17},{3,19},{17,1},{19,3},{4,20},{6,... | collective-permute-start | bytes 442376 | tf_op jit(solution)/shard_map/ppermute | solution.py:71
  51.1 25.3 %all-to-all-start.1 = ((bf16[8,32,1152]{2,1,0:T(8,128)(2,1)}), bf16[8,32,1152]{2,1,0:T(8,128)(2,1)S(1)}, u32[]{:S(2)}, u32[]{:S(2)}) async-start(bf16[8,32,1152]{2,1,0:T(8,128)(2,1)} %get-tuple-element.34), calls=%async_computation.1 | async-start | bytes 1179648 | tf_op jit(solution)/shard_map/all_to_all | solution.py:75
  57.1 7.6 %collective-permute-start.9 = (bf16[2,2,32,1152]{3,2,1,0:T(8,128)(2,1)S(1)}, bf16[2,2,32,1152]{3,2,1,0:T(8,128)(2,1)S(1)}, u32[]{:S(2)}, u32[]{:S(2)}) collective-permute-start(bf16[2,2,32,1152]{3,2,1,0:T(8,128)(2,1)S(1)} %pad_maximum_fusion.3), channel_id=1, source_target_pairs={{0,12},{4,0},{8,4},{12,8},{1,13},{5,1},{9,5},{13,9},{2,14},{6,2},{... | collective-permute-start | bytes 884744 | tf_op jit(solution)/shard_map/ppermute | solution.py:56
  57.1 8.6 %collective-permute-start.8 = (bf16[2,2,32,1152]{3,2,1,0:T(8,128)(2,1)S(1)}, bf16[2,2,32,1152]{3,2,1,0:T(8,128)(2,1)S(1)}, u32[]{:S(2)}, u32[]{:S(2)}) collective-permute-start(bf16[2,2,32,1152]{3,2,1,0:T(8,128)(2,1)S(1)} %pad_maximum_fusion.3), channel_id=1, source_target_pairs={{0,8},{4,12},{8,0},{12,4},{1,9},{5,13},{9,1},{13,5},{2,10},{6,14},... | collective-permute-start | bytes 884744 | tf_op jit(solution)/shard_map/ppermute | solution.py:56
  57.2 16.7 %collective-permute-start.7 = (bf16[2,2,32,1152]{3,2,1,0:T(8,128)(2,1)S(1)}, bf16[2,2,32,1152]{3,2,1,0:T(8,128)(2,1)S(1)}, u32[]{:S(2)}, u32[]{:S(2)}) collective-permute-start(bf16[2,2,32,1152]{3,2,1,0:T(8,128)(2,1)S(1)} %pad_maximum_fusion.3), channel_id=1, source_target_pairs={{0,4},{4,8},{8,12},{12,0},{1,5},{5,9},{9,13},{13,1},{2,6},{6,10},{... | collective-permute-start | bytes 884744 | tf_op jit(solution)/shard_map/ppermute | solution.py:56
  76.5 3.3 %collective-permute-start.11 = (bf16[512,1152]{1,0:T(8,128)(2,1)S(1)}, bf16[512,1152]{1,0:T(8,128)(2,1)S(1)}, u32[]{:S(2)}, u32[]{:S(2)}) collective-permute-start(bf16[512,1152]{1,0:T(8,128)(2,1)S(1)} %bitcast.82), channel_id=1, source_target_pairs={{0,1},{1,0},{2,3},{3,2},{4,5},{5,4},{6,7},{7,6},{8,9},{9,8},{10,11... | collective-permute-start | bytes 3538952 | tf_op jit(solution)/shard_map/ppermute | solution.py:48
  83.8 4.5 %collective-permute-start.12 = (bf16[512,1152]{1,0:T(8,128)(2,1)}, bf16[512,1152]{1,0:T(8,128)(2,1)}, u32[]{:S(2)}, u32[]{:S(2)}) collective-permute-start(bf16[512,1152]{1,0:T(8,128)(2,1)} %get-tuple-element.40), channel_id=1, source_target_pairs={{0,1},{1,0},{2,3},{3,2},{4,5},{5,4},{6,7},{7,6},{8,9},{9,8},{10,11... | collective-permute-start | bytes 3538952 | tf_op jit(solution)/shard_map/ppermute | solution.py:48
  83.9 23.9 %all-to-all-start.2 = ((bf16[8,32,1152]{2,1,0:T(8,128)(2,1)}), bf16[8,32,1152]{2,1,0:T(8,128)(2,1)S(1)}, u32[]{:S(2)}, u32[]{:S(2)}) async-start(bf16[8,32,1152]{2,1,0:T(8,128)(2,1)} %bitcast.28), calls=%async_computation.2 | async-start | bytes 1179648 | tf_op jit(solution)/shard_map/all_to_all | solution.py:75
  90.0 22.6 %collective-permute-start.15 = (bf16[4,32,1152]{2,1,0:T(8,128)(2,1)S(1)}, bf16[4,32,1152]{2,1,0:T(8,128)(2,1)S(1)}, u32[]{:S(2)}, u32[]{:S(2)}) collective-permute-start(bf16[4,32,1152]{2,1,0:T(8,128)(2,1)S(1)} %bitcast.93), channel_id=1, source_target_pairs={{0,4},{4,8},{8,12},{12,0},{1,5},{5,9},{9,13},{13,1},{2,6},{6,10},{... | collective-permute-start | bytes 884744 | tf_op jit(solution)/shard_map/ppermute | solution.py:56
  90.1 22.5 %collective-permute-start.14 = (bf16[4,32,1152]{2,1,0:T(8,128)(2,1)S(1)}, bf16[4,32,1152]{2,1,0:T(8,128)(2,1)S(1)}, u32[]{:S(2)}, u32[]{:S(2)}) collective-permute-start(bf16[4,32,1152]{2,1,0:T(8,128)(2,1)S(1)} %bitcast.92), channel_id=1, source_target_pairs={{0,8},{4,12},{8,0},{12,4},{1,9},{5,13},{9,1},{13,5},{2,10},{6,14},... | collective-permute-start | bytes 884744 | tf_op jit(solution)/shard_map/ppermute | solution.py:56
  92.2 20.5 %collective-permute-start.13 = (bf16[4,32,1152]{2,1,0:T(8,128)(2,1)S(1)}, bf16[4,32,1152]{2,1,0:T(8,128)(2,1)S(1)}, u32[]{:S(2)}, u32[]{:S(2)}) collective-permute-start(bf16[4,32,1152]{2,1,0:T(8,128)(2,1)S(1)} %bitcast.91), channel_id=1, source_target_pairs={{0,12},{4,0},{8,4},{12,8},{1,13},{5,1},{9,5},{13,9},{2,14},{6,2},{... | collective-permute-start | bytes 884744 | tf_op jit(solution)/shard_map/ppermute | solution.py:56
  108.9 34.3 %all-to-all-start.4 = ((bf16[16,32,1152]{2,1,0:T(8,128)(2,1)}), bf16[16,32,1152]{2,1,0:T(8,128)(2,1)S(1)}, u32[]{:S(2)}, u32[]{:S(2)}) async-start(bf16[16,32,1152]{2,1,0:T(8,128)(2,1)} %get-tuple-element.47), calls=%async_computation.4 | async-start | bytes 2359296 | tf_op jit(solution)/shard_map/all_to_all | solution.py:75
  112.9 7.0 %collective-permute-start.18 = (bf16[2,40,1152]{2,1,0:T(8,128)(2,1)S(1)}, bf16[2,40,1152]{2,1,0:T(8,128)(2,1)S(1)}, u32[]{:S(2)}, u32[]{:S(2)}) collective-permute-start(bf16[2,40,1152]{2,1,0:T(8,128)(2,1)S(1)} %get-tuple-element.65), channel_id=1, source_target_pairs={{0,18},{2,16},{16,2},{18,0},{1,19},{3,17},{17,3},{19,1},{4,22},{6,... | collective-permute-start | bytes 552968 | tf_op jit(solution)/shard_map/ppermute | solution.py:71
  115.0 5.1 %collective-permute-start.17 = (bf16[2,40,1152]{2,1,0:T(8,128)(2,1)S(1)}, bf16[2,40,1152]{2,1,0:T(8,128)(2,1)S(1)}, u32[]{:S(2)}, u32[]{:S(2)}) collective-permute-start(bf16[2,40,1152]{2,1,0:T(8,128)(2,1)S(1)} %get-tuple-element.65), channel_id=1, source_target_pairs={{0,16},{2,18},{16,0},{18,2},{1,17},{3,19},{17,1},{19,3},{4,20},{6,... | collective-permute-start | bytes 552968 | tf_op jit(solution)/shard_map/ppermute | solution.py:71
  115.0 24.0 %copy-start.6 = (bf16[512,269]{0,1:T(8,128)(2,1)S(1)}, bf16[512,269]{0,1:T(8,128)(2,1)}, u32[]{:S(2)}) copy-start(bf16[512,269]{0,1:T(8,128)(2,1)} %param.10) | copy-start | bytes 826372
  115.1 9.9 %collective-permute-start.16 = (bf16[2,40,1152]{2,1,0:T(8,128)(2,1)S(1)}, bf16[2,40,1152]{2,1,0:T(8,128)(2,1)S(1)}, u32[]{:S(2)}, u32[]{:S(2)}) collective-permute-start(bf16[2,40,1152]{2,1,0:T(8,128)(2,1)S(1)} %get-tuple-element.64), channel_id=1, source_target_pairs={{0,2},{2,0},{16,18},{18,16},{1,3},{3,1},{17,19},{19,17},{4,6},{6,4... | collective-permute-start | bytes 552968 | tf_op jit(solution)/shard_map/ppermute | solution.py:71
  125.1 13.9 %copy-start.7 = (bf16[512,269]{0,1:T(8,128)(2,1)S(1)}, bf16[512,269]{0,1:T(8,128)(2,1)}, u32[]{:S(2)}) copy-start(bf16[512,269]{0,1:T(8,128)(2,1)} %param.13) | copy-start | bytes 826372
  125.1 4.8 %collective-permute-start.21 = (bf16[2,40,1152]{2,1,0:T(8,128)(2,1)S(1)}, bf16[2,40,1152]{2,1,0:T(8,128)(2,1)S(1)}, u32[]{:S(2)}, u32[]{:S(2)}) collective-permute-start(bf16[2,40,1152]{2,1,0:T(8,128)(2,1)S(1)} %add_convert_fusion.2), channel_id=1, source_target_pairs={{0,12},{4,0},{8,4},{12,8},{1,13},{5,1},{9,5},{13,9},{2,14},{6,2},{... | collective-permute-start | bytes 552968 | tf_op jit(solution)/shard_map/ppermute | solution.py:56
  126.1 6.0 %collective-permute-start.20 = (bf16[2,40,1152]{2,1,0:T(8,128)(2,1)S(1)}, bf16[2,40,1152]{2,1,0:T(8,128)(2,1)S(1)}, u32[]{:S(2)}, u32[]{:S(2)}) collective-permute-start(bf16[2,40,1152]{2,1,0:T(8,128)(2,1)S(1)} %add_convert_fusion.2), channel_id=1, source_target_pairs={{0,8},{4,12},{8,0},{12,4},{1,9},{5,13},{9,1},{13,5},{2,10},{6,14},... | collective-permute-start | bytes 552968 | tf_op jit(solution)/shard_map/ppermute | solution.py:56
  126.1 11.4 %collective-permute-start.19 = (bf16[2,40,1152]{2,1,0:T(8,128)(2,1)S(1)}, bf16[2,40,1152]{2,1,0:T(8,128)(2,1)S(1)}, u32[]{:S(2)}, u32[]{:S(2)}) collective-permute-start(bf16[2,40,1152]{2,1,0:T(8,128)(2,1)S(1)} %add_convert_fusion.2), channel_id=1, source_target_pairs={{0,4},{4,8},{8,12},{12,0},{1,5},{5,9},{9,13},{13,1},{2,6},{6,10},{... | collective-permute-start | bytes 552968 | tf_op jit(solution)/shard_map/ppermute | solution.py:56
  137.6 3.3 %copy-start.2 = (bf16[269,1152]{1,0:T(8,128)(2,1)S(1)}, bf16[269,1152]{1,0:T(8,128)(2,1)}, u32[]{:S(2)}) copy-start(bf16[269,1152]{1,0:T(8,128)(2,1)} %proj.2) | copy-start | bytes 1859332
  137.7 3.2 %collective-permute-start.22 = (bf16[4,2,40,1152]{3,2,1,0:T(8,128)(2,1)S(1)}, bf16[4,2,40,1152]{3,2,1,0:T(8,128)(2,1)S(1)}, u32[]{:S(2)}, u32[]{:S(2)}) collective-permute-start(bf16[4,2,40,1152]{3,2,1,0:T(8,128)(2,1)S(1)} %pad_maximum_fusion.1.own), channel_id=1, source_target_pairs={{0,1},{1,0},{2,3},{3,2},{4,5},{5,4},{6,7},{7,6},{8,9},{9,8},{10,11... | collective-permute-start | bytes 2211848 | tf_op jit(solution)/shard_map/ppermute | solution.py:48
  139.2 4.1 %copy-start = (bf16[269,1152]{1,0:T(8,128)(2,1)S(1)}, bf16[269,1152]{1,0:T(8,128)(2,1)}, u32[]{:S(2)}) copy-start(bf16[269,1152]{1,0:T(8,128)(2,1)} %proj.3) | copy-start | bytes 1859332
  145.6 6.4 %collective-permute-start.23 = (bf16[4,2,80,256]{3,2,1,0:T(8,128)(2,1)S(1)}, bf16[4,2,80,256]{3,2,1,0:T(8,128)(2,1)S(1)}, u32[]{:S(2)}, u32[]{:S(2)}) collective-permute-start(bf16[4,2,80,256]{3,2,1,0:T(8,128)(2,1)S(1)} %get-tuple-element.50), channel_id=1, source_target_pairs={{0,1},{1,0},{2,3},{3,2},{4,5},{5,4},{6,7},{7,6},{8,9},{9,8},{10,11... | collective-permute-start | bytes 983048 | tf_op jit(solution)/shard_map/ppermute | solution.py:48
  147.4 23.2 %all-to-all-start.3 = ((bf16[16,80,256]{2,1,0:T(8,128)(2,1)}), bf16[16,80,256]{2,1,0:T(8,128)(2,1)S(1)}, u32[]{:S(2)}, u32[]{:S(2)}) async-start(bf16[16,80,256]{2,1,0:T(8,128)(2,1)} %get-tuple-element.45), calls=%async_computation.3 | async-start | bytes 1310720 | tf_op jit(solution)/shard_map/all_to_all | solution.py:75
  152.1 3.7 %collective-permute-start.26 = (bf16[2,80,256]{2,1,0:T(8,128)(2,1)S(1)}, bf16[2,80,256]{2,1,0:T(8,128)(2,1)S(1)}, u32[]{:S(2)}, u32[]{:S(2)}) collective-permute-start(bf16[2,80,256]{2,1,0:T(8,128)(2,1)S(1)} %get-tuple-element.67), channel_id=1, source_target_pairs={{0,12},{4,0},{8,4},{12,8},{1,13},{5,1},{9,5},{13,9},{2,14},{6,2},{... | collective-permute-start | bytes 245768 | tf_op jit(solution)/shard_map/ppermute | solution.py:56
  152.7 4.8 %collective-permute-start.25 = (bf16[2,80,256]{2,1,0:T(8,128)(2,1)S(1)}, bf16[2,80,256]{2,1,0:T(8,128)(2,1)S(1)}, u32[]{:S(2)}, u32[]{:S(2)}) collective-permute-start(bf16[2,80,256]{2,1,0:T(8,128)(2,1)S(1)} %get-tuple-element.68), channel_id=1, source_target_pairs={{0,8},{4,12},{8,0},{12,4},{1,9},{5,13},{9,1},{13,5},{2,10},{6,14},... | collective-permute-start | bytes 245768 | tf_op jit(solution)/shard_map/ppermute | solution.py:56
  153.1 7.0 %collective-permute-start.24 = (bf16[2,80,256]{2,1,0:T(8,128)(2,1)S(1)}, bf16[2,80,256]{2,1,0:T(8,128)(2,1)S(1)}, u32[]{:S(2)}, u32[]{:S(2)}) collective-permute-start(bf16[2,80,256]{2,1,0:T(8,128)(2,1)S(1)} %get-tuple-element.66), channel_id=1, source_target_pairs={{0,4},{4,8},{8,12},{12,0},{1,5},{5,9},{9,13},{13,1},{2,6},{6,10},{... | collective-permute-start | bytes 245768 | tf_op jit(solution)/shard_map/ppermute | solution.py:56
  160.2 4.8 %collective-permute-start.27 = (bf16[80,256]{1,0:T(8,128)(2,1)S(1)}, bf16[80,256]{1,0:T(8,128)(2,1)S(1)}, u32[]{:S(2)}, u32[]{:S(2)}) collective-permute-start(bf16[80,256]{1,0:T(8,128)(2,1)S(1)} %get-tuple-element.70), channel_id=1, source_target_pairs={{0,2},{2,0},{1,3},{3,1},{4,6},{6,4},{5,7},{7,5},{8,10},{10,8},{9,1... | collective-permute-start | bytes 122888 | tf_op jit(solution)/shard_map/ppermute | solution.py:48

commit v5 on v4

--- a/solution.py
+++ b/solution.py
@@ -369,7 +369,7 @@
     )
     found = exchange(blocks, IMG)
 
-    text_back = exchange(after(copies, image_row), IMG).reshape(-1, width)
+    text_back = exchange(copies, IMG).reshape(-1, width)
     text_back = after(text_back, blocks)
     text_act_grad, mine, theirs = text_weight_call(
         place, text_back, jnp.pad(text_acts.T, wide), text_proj

time: 175 us -> 175 us (level)
  no operation moved by 1% of the time
where the time goes in v5:
time: 175 us; the launch traced here: 173 us
  waiting for transfers between devices  88.3 us (50%)
  starting transfers between devices  55.5 us (32%)
  Pallas kernels  15.3 us (9%)
  between operations  4.16 us (2%)
  other arithmetic  4.11 us (2%)
  matrix products  4.02 us (2%)
    ppermute x15, waiting for transfers between devices, shift(): lax.ppermute(block, axis, [(i, (i + step) % count) for i in range(count)])  40.3 us
    all_to_all x5, starting transfers between devices, exchange(): return lax.all_to_all(blocks, axis, 0, 0)  26.4 us
    ppermute x6, waiting for transfers between devices, turn_x(): lax.ppermute(block, ('xl', 'xh'), [(i, i ^ 2 * a + b) for i in range(4)])  22.5 us
    all_to_all x5, waiting for transfers between devices, exchange(): return lax.all_to_all(blocks, axis, 0, 0)  22.1 us
    ppermute x15, starting transfers between devices, shift(): lax.ppermute(block, axis, [(i, (i + step) % count) for i in range(count)])  11.3 us
    ppermute x7, starting transfers between devices, swap(): return lax.ppermute(block, axis, SWAP)  11 us
    ppermute x6, starting transfers between devices, turn_x(): lax.ppermute(block, ('xl', 'xh'), [(i, i ^ 2 * a + b) for i in range(4)])  6.83 us
    pallas_call x1, Pallas kernels, rest_call(): pl.pallas_call(rest_kernel, out_shape=(like(text, bf16), like(image, bf16...  4.05 us
  transfers between devices with their start and end apart: 33, of which 22 were waited for; matrix products, arithmetic and copies ran while one was open for 3% of the time, Pallas kernels for 4%

profile of v5, /device:TPU:1, one launch (start us, length us, event | category | flops | bytes accessed | tf_op | source)
XLA Modules:
  0.0 173.1 jit_solution(16694207408002453042)
XLA Ops:
  0.7 3.2 %convolution_convert_fusion.1 = bf16[512,1152]{1,0:T(8,128)(2,1)} fusion(bf16[512,269]{0,1:T(8,128)(2,1)} %param.13, bf16[269,1152]{1,0:T(8,128)(2,1)} %proj.3), kind=kOutput, calls=%fused_computation.2 | convolution fusion | flops 317915136 | bytes 2074880 | tf_op jit(solution)/shard_map/dot_general | solution.py:32
  3.8 0.9 convolution_convert_fusion
  4.8 3.3 %collective-permute-start = (bf16[4,2,32,1152]{3,2,1,0:T(8,128)(2,1)S(1)}, bf16[4,2,32,1152]{3,2,1,0:T(8,128)(2,1)S(1)}, u32[]{:S(2)}, u32[]{:S(2)}) collective-permute-start(bf16[4,2,32,1152]{3,2,1,0:T(8,128)(2,1)S(1)} %dynamic-slice_bitcast_fusion), channel_id=1, source_target_pairs={{0,1},{1,0},{2,3},{3,2},{4,5},{5,4},{6,7},{7,6},{8,9},{9,8},{10,11... | collective-permute-start | bytes 1769480 | tf_op jit(solution)/shard_map/ppermute | solution.py:48
  8.1 7.7 %all-to-all-start = ((bf16[16,32,1152]{2,1,0:T(8,128)(2,1)}), bf16[16,32,1152]{2,1,0:T(8,128)(2,1)S(1)}, u32[]{:S(2)}, u32[]{:S(2)}) async-start(bf16[16,32,1152]{2,1,0:T(8,128)(2,1)} %bitcast.4), calls=%async_computation | async-start | bytes 2359296 | tf_op jit(solution)/shard_map/all_to_all | solution.py:75
  15.8 1.4 collective-permute-start.10
  18.7 1.3 fusion
  20.1 2.8 %collective-permute-start.3 = (bf16[2,32,1152]{2,1,0:T(8,128)(2,1)S(1)}, bf16[2,32,1152]{2,1,0:T(8,128)(2,1)S(1)}, u32[]{:S(2)}, u32[]{:S(2)}) collective-permute-start(bf16[2,32,1152]{2,1,0:T(8,128)(2,1)S(1)} %get-tuple-element.60), channel_id=1, source_target_pairs={{0,12},{4,0},{8,4},{12,8},{1,13},{5,1},{9,5},{13,9},{2,14},{6,2},{... | collective-permute-start | bytes 442376 | tf_op jit(solution)/shard_map/ppermute | solution.py:56
  24.7 0.9 collective-permute-done.3
  25.6 3.0 %collective-permute-done.2 = bf16[2,32,1152]{2,1,0:T(8,128)(2,1)S(1)} collective-permute-done((bf16[2,32,1152]{2,1,0:T(8,128)(2,1)S(1)}, bf16[2,32,1152]{2,1,0:T(8,128)(2,1)S(1)}, u32[]{:S(2)}, u32[]{:S(2)}) %collective-permute-start.2) | collective-permute-done | bytes 147488 | tf_op jit(solution)/shard_map/ppermute | solution.py:56
  28.7 3.8 %collective-permute-done.1 = bf16[2,32,1152]{2,1,0:T(8,128)(2,1)S(1)} collective-permute-done((bf16[2,32,1152]{2,1,0:T(8,128)(2,1)S(1)}, bf16[2,32,1152]{2,1,0:T(8,128)(2,1)S(1)}, u32[]{:S(2)}, u32[]{:S(2)}) %collective-permute-start.1) | collective-permute-done | bytes 147488 | tf_op jit(solution)/shard_map/ppermute | solution.py:56
  32.6 2.5 %collective-permute-start.4 = (bf16[2,32,1152]{2,1,0:T(8,128)(2,1)S(1)}, bf16[2,32,1152]{2,1,0:T(8,128)(2,1)S(1)}, u32[]{:S(2)}, u32[]{:S(2)}) collective-permute-start(bf16[2,32,1152]{2,1,0:T(8,128)(2,1)S(1)} %fusion.7), channel_id=1, source_target_pairs={{0,2},{2,0},{16,18},{18,16},{1,3},{3,1},{17,19},{19,17},{4,6},{6,4... | collective-permute-start | bytes 442376 | tf_op jit(solution)/shard_map/ppermute | solution.py:71
  35.6 9.1 %collective-permute-done.4 = bf16[2,32,1152]{2,1,0:T(8,128)(2,1)S(1)} collective-permute-done((bf16[2,32,1152]{2,1,0:T(8,128)(2,1)S(1)}, bf16[2,32,1152]{2,1,0:T(8,128)(2,1)S(1)}, u32[]{:S(2)}, u32[]{:S(2)}) %collective-permute-start.4) | collective-permute-done | bytes 147488 | tf_op jit(solution)/shard_map/ppermute | solution.py:71
  44.8 5.2 %collective-permute-done.5 = bf16[2,32,1152]{2,1,0:T(8,128)(2,1)S(1)} collective-permute-done((bf16[2,32,1152]{2,1,0:T(8,128)(2,1)S(1)}, bf16[2,32,1152]{2,1,0:T(8,128)(2,1)S(1)}, u32[]{:S(2)}, u32[]{:S(2)}) %collective-permute-start.5) | collective-permute-done | bytes 147488 | tf_op jit(solution)/shard_map/ppermute | solution.py:71
  50.1 1.0 spread.2
  51.1 6.0 %all-to-all-start.1 = ((bf16[8,32,1152]{2,1,0:T(8,128)(2,1)}), bf16[8,32,1152]{2,1,0:T(8,128)(2,1)S(1)}, u32[]{:S(2)}, u32[]{:S(2)}) async-start(bf16[8,32,1152]{2,1,0:T(8,128)(2,1)} %get-tuple-element.33), calls=%async_computation.1 | async-start | bytes 1179648 | tf_op jit(solution)/shard_map/all_to_all | solution.py:75
  57.2 1.4 collective-permute-start.7
  58.6 6.2 %collective-permute-done.9 = bf16[2,2,32,1152]{3,2,1,0:T(8,128)(2,1)S(1)} collective-permute-done((bf16[2,2,32,1152]{3,2,1,0:T(8,128)(2,1)S(1)}, bf16[2,2,32,1152]{3,2,1,0:T(8,128)(2,1)S(1)}, u32[]{:S(2)}, u32[]{:S(2)}) %collective-permute-start.9) | collective-permute-done | bytes 294944 | tf_op jit(solution)/shard_map/ppermute | solution.py:56
  64.7 1.0 collective-permute-done.8
  65.7 8.2 %collective-permute-done.7 = bf16[2,2,32,1152]{3,2,1,0:T(8,128)(2,1)S(1)} collective-permute-done((bf16[2,2,32,1152]{3,2,1,0:T(8,128)(2,1)S(1)}, bf16[2,2,32,1152]{3,2,1,0:T(8,128)(2,1)S(1)}, u32[]{:S(2)}, u32[]{:S(2)}) %collective-permute-start.7) | collective-permute-done | bytes 294944 | tf_op jit(solution)/shard_map/ppermute | solution.py:56
  74.1 2.3 %all-to-all-done.1 = bf16[8,32,1152]{2,1,0:T(8,128)(2,1)S(1)} async-done(((bf16[8,32,1152]{2,1,0:T(8,128)(2,1)}), bf16[8,32,1152]{2,1,0:T(8,128)(2,1)S(1)}, u32[]{:S(2)}, u32[]{:S(2)}) %all-to-all-start.1) | async-done | bytes 589856 | tf_op jit(solution)/shard_map/all_to_all | solution.py:75
  77.0 2.8 %score.1 = (f32[256,1152]{1,0:T(8,128)S(1)}, bf16[256,1152]{1,0:T(8,128)(2,1)S(1)}, bf16[512,1152]{1,0:T(8,128)(2,1)S(1)}, f32[1,512]{1,0:T(1,128)S(1)}) custom-call(f32[2]{0:T(128)S(1)} %pad_maximum_fusion.5.params, s32[2]{0:T(128)S(1)} %pad_add_fusion.1.base, bf16[512,1152]{1,0:T(8,128)(2,1)S(1)} %bitcast.83, bf16[256,1152]{1,0:T(8,128)(2,1)S(1)} %bitcast.79, ...), custom_call_target="tpu_custom_call" | custom-call | tf_op jit(solution)/shard_map/score/pallas_call | solution.py:161
  79.8 4.1 %score_rest.1 = (bf16[256,1152]{1,0:T(8,128)(2,1)}, bf16[512,1152]{1,0:T(8,128)(2,1)}, bf16[8,1152]{1,0:T(8,128)(2,1)S(1)}) custom-call(f32[2]{0:T(128)S(1)} %pad_maximum_fusion.5.params, s32[2]{0:T(128)S(1)} %pad_add_fusion.1.base, bf16[512,1152]{1,0:T(8,128)(2,1)S(1)} %collective-permute-done.11.image, bf16[256,1152]{1,0:T(8,128)(2,1)S(1)} %bitcast.80, ...), custom_call_target="tpu_custom_call" | custom-call | tf_op jit(solution)/shard_map/score_rest/pallas_call | solution.py:177
  83.9 4.5 %all-to-all-start.2 = ((bf16[8,32,1152]{2,1,0:T(8,128)(2,1)}), bf16[8,32,1152]{2,1,0:T(8,128)(2,1)S(1)}, u32[]{:S(2)}, u32[]{:S(2)}) async-start(bf16[8,32,1152]{2,1,0:T(8,128)(2,1)} %bitcast.28), calls=%async_computation.2 | async-start | bytes 1179648 | tf_op jit(solution)/shard_map/all_to_all | solution.py:75
  88.4 1.5 add_convert_fusion
  90.1 2.1 %collective-permute-start.14 = (bf16[4,32,1152]{2,1,0:T(8,128)(2,1)S(1)}, bf16[4,32,1152]{2,1,0:T(8,128)(2,1)S(1)}, u32[]{:S(2)}, u32[]{:S(2)}) collective-permute-start(bf16[4,32,1152]{2,1,0:T(8,128)(2,1)S(1)} %bitcast.92), channel_id=1, source_target_pairs={{0,8},{4,12},{8,0},{12,4},{1,9},{5,13},{9,1},{13,5},{2,10},{6,14},... | collective-permute-start | bytes 884744 | tf_op jit(solution)/shard_map/ppermute | solution.py:56
  92.8 14.9 %all-to-all-done.2.parts = bf16[8,32,1152]{2,1,0:T(8,128)(2,1)S(1)} async-done(((bf16[8,32,1152]{2,1,0:T(8,128)(2,1)}), bf16[8,32,1152]{2,1,0:T(8,128)(2,1)S(1)}, u32[]{:S(2)}, u32[]{:S(2)}) %all-to-all-start.2) | async-done | bytes 589856 | tf_op jit(solution)/shard_map/all_to_all | solution.py:75
  107.7 1.2 spread.3
  108.9 3.7 %all-to-all-start.4 = ((bf16[16,32,1152]{2,1,0:T(8,128)(2,1)}), bf16[16,32,1152]{2,1,0:T(8,128)(2,1)S(1)}, u32[]{:S(2)}, u32[]{:S(2)}) async-start(bf16[16,32,1152]{2,1,0:T(8,128)(2,1)} %get-tuple-element.45), calls=%async_computation.4 | async-start | bytes 2359296 | tf_op jit(solution)/shard_map/all_to_all | solution.py:75
  112.9 2.2 %collective-permute-start.18 = (bf16[2,40,1152]{2,1,0:T(8,128)(2,1)S(1)}, bf16[2,40,1152]{2,1,0:T(8,128)(2,1)S(1)}, u32[]{:S(2)}, u32[]{:S(2)}) collective-permute-start(bf16[2,40,1152]{2,1,0:T(8,128)(2,1)S(1)} %get-tuple-element.63), channel_id=1, source_target_pairs={{0,18},{2,16},{16,2},{18,0},{1,19},{3,17},{17,3},{19,1},{4,22},{6,... | collective-permute-start | bytes 552968 | tf_op jit(solution)/shard_map/ppermute | solution.py:71
  115.1 1.8 %collective-permute-start.16 = (bf16[2,40,1152]{2,1,0:T(8,128)(2,1)S(1)}, bf16[2,40,1152]{2,1,0:T(8,128)(2,1)S(1)}, u32[]{:S(2)}, u32[]{:S(2)}) collective-permute-start(bf16[2,40,1152]{2,1,0:T(8,128)(2,1)S(1)} %get-tuple-element.62), channel_id=1, source_target_pairs={{0,2},{2,0},{16,18},{18,16},{1,3},{3,1},{17,19},{19,17},{4,6},{6,4... | collective-permute-start | bytes 552968 | tf_op jit(solution)/shard_map/ppermute | solution.py:71
  116.8 3.1 %collective-permute-done.18 = bf16[2,40,1152]{2,1,0:T(8,128)(2,1)S(1)} collective-permute-done((bf16[2,40,1152]{2,1,0:T(8,128)(2,1)S(1)}, bf16[2,40,1152]{2,1,0:T(8,128)(2,1)S(1)}, u32[]{:S(2)}, u32[]{:S(2)}) %collective-permute-start.18) | collective-permute-done | bytes 184352 | tf_op jit(solution)/shard_map/ppermute | solution.py:71
  120.1 4.9 %collective-permute-done.16 = bf16[2,40,1152]{2,1,0:T(8,128)(2,1)S(1)} collective-permute-done((bf16[2,40,1152]{2,1,0:T(8,128)(2,1)S(1)}, bf16[2,40,1152]{2,1,0:T(8,128)(2,1)S(1)}, u32[]{:S(2)}, u32[]{:S(2)}) %collective-permute-start.16) | collective-permute-done | bytes 184352 | tf_op jit(solution)/shard_map/ppermute | solution.py:71
  125.1 1.0 collective-permute-start.21
  126.8 3.1 %collective-permute-done.21 = bf16[2,40,1152]{2,1,0:T(8,128)(2,1)S(1)} collective-permute-done((bf16[2,40,1152]{2,1,0:T(8,128)(2,1)S(1)}, bf16[2,40,1152]{2,1,0:T(8,128)(2,1)S(1)}, u32[]{:S(2)}, u32[]{:S(2)}) %collective-permute-start.21) | collective-permute-done | bytes 184352 | tf_op jit(solution)/shard_map/ppermute | solution.py:56
  129.9 2.3 %collective-permute-done.20 = bf16[2,40,1152]{2,1,0:T(8,128)(2,1)S(1)} collective-permute-done((bf16[2,40,1152]{2,1,0:T(8,128)(2,1)S(1)}, bf16[2,40,1152]{2,1,0:T(8,128)(2,1)S(1)}, u32[]{:S(2)}, u32[]{:S(2)}) %collective-permute-start.20) | collective-permute-done | bytes 184352 | tf_op jit(solution)/shard_map/ppermute | solution.py:56
  132.1 5.4 %collective-permute-done.19 = bf16[2,40,1152]{2,1,0:T(8,128)(2,1)S(1)} collective-permute-done((bf16[2,40,1152]{2,1,0:T(8,128)(2,1)S(1)}, bf16[2,40,1152]{2,1,0:T(8,128)(2,1)S(1)}, u32[]{:S(2)}, u32[]{:S(2)}) %collective-permute-start.19) | collective-permute-done | bytes 184352 | tf_op jit(solution)/shard_map/ppermute | solution.py:56
  137.7 1.3 collective-permute-start.22
  139.2 1.7 collective-permute-done.22.other
  140.9 2.4 %image_weight.1 = (bf16[269,512]{1,0:T(8,128)(2,1)}, bf16[16,80,256]{2,1,0:T(8,128)(2,1)}) custom-call(s32[2]{0:T(128)S(1)} %pad_add_fusion.place, bf16[4,2,40,1152]{3,2,1,0:T(8,128)(2,1)S(1)} %pad_maximum_fusion.1.own, bf16[4,2,40,1152]{3,2,1,0:T(8,128)(2,1)S(1)} %collective-permute-done.22.other, bf16[272,512]{1,0:T(8,128)(2,1)S(1)} %pad.7.acts, ...), custom_call_target="tpu_custom_call" | custom-call | tf_op jit(solution)/shard_map/image_weight/pallas_call | solution.py:255
  143.3 2.3 %text_weight.1 = (bf16[269,512]{1,0:T(8,128)(2,1)}, bf16[4,2,80,256]{3,2,1,0:T(8,128)(2,1)S(1)}, bf16[4,2,80,256]{3,2,1,0:T(8,128)(2,1)S(1)}) custom-call(s32[2]{0:T(128)S(1)} %pad_add_fusion.place, bf16[512,1152]{1,0:T(8,128)(2,1)S(1)} %bitcast.81, bf16[272,512]{1,0:T(8,128)(2,1)S(1)} %pad.8.acts, bf16[269,1152]{1,0:T(8,128)(2,1)S(1)} %copy-done), custom_call_target="tpu_custom_call" | custom-call | tf_op jit(solution)/shard_map/text_weight/pallas_call | solution.py:281
  145.6 1.8 %collective-permute-start.23 = (bf16[4,2,80,256]{3,2,1,0:T(8,128)(2,1)S(1)}, bf16[4,2,80,256]{3,2,1,0:T(8,128)(2,1)S(1)}, u32[]{:S(2)}, u32[]{:S(2)}) collective-permute-start(bf16[4,2,80,256]{3,2,1,0:T(8,128)(2,1)S(1)} %get-tuple-element.48), channel_id=1, source_target_pairs={{0,1},{1,0},{2,3},{3,2},{4,5},{5,4},{6,7},{7,6},{8,9},{9,8},{10,11... | collective-permute-start | bytes 983048 | tf_op jit(solution)/shard_map/ppermute | solution.py:48
  147.4 4.6 %all-to-all-start.3 = ((bf16[16,80,256]{2,1,0:T(8,128)(2,1)}), bf16[16,80,256]{2,1,0:T(8,128)(2,1)S(1)}, u32[]{:S(2)}, u32[]{:S(2)}) async-start(bf16[16,80,256]{2,1,0:T(8,128)(2,1)} %get-tuple-element.44), calls=%async_computation.3 | async-start | bytes 1310720 | tf_op jit(solution)/shard_map/all_to_all | solution.py:75
  153.7 2.1 %collective-permute-done.26 = bf16[2,80,256]{2,1,0:T(8,128)(2,1)S(1)} collective-permute-done((bf16[2,80,256]{2,1,0:T(8,128)(2,1)S(1)}, bf16[2,80,256]{2,1,0:T(8,128)(2,1)S(1)}, u32[]{:S(2)}, u32[]{:S(2)}) %collective-permute-start.26) | collective-permute-done | bytes 81952 | tf_op jit(solution)/shard_map/ppermute | solution.py:56
  155.8 1.7 %collective-permute-done.25 = bf16[2,80,256]{2,1,0:T(8,128)(2,1)S(1)} collective-permute-done((bf16[2,80,256]{2,1,0:T(8,128)(2,1)S(1)}, bf16[2,80,256]{2,1,0:T(8,128)(2,1)S(1)}, u32[]{:S(2)}, u32[]{:S(2)}) %collective-permute-start.25) | collective-permute-done | bytes 81952 | tf_op jit(solution)/shard_map/ppermute | solution.py:56
  157.5 2.5 %collective-permute-done.24 = bf16[2,80,256]{2,1,0:T(8,128)(2,1)S(1)} collective-permute-done((bf16[2,80,256]{2,1,0:T(8,128)(2,1)S(1)}, bf16[2,80,256]{2,1,0:T(8,128)(2,1)S(1)}, u32[]{:S(2)}, u32[]{:S(2)}) %collective-permute-start.24) | collective-permute-done | bytes 81952 | tf_op jit(solution)/shard_map/ppermute | solution.py:56
  160.2 2.5 %collective-permute-start.27 = (bf16[80,256]{1,0:T(8,128)(2,1)S(1)}, bf16[80,256]{1,0:T(8,128)(2,1)S(1)}, u32[]{:S(2)}, u32[]{:S(2)}) collective-permute-start(bf16[80,256]{1,0:T(8,128)(2,1)S(1)} %get-tuple-element.68), channel_id=1, source_target_pairs={{0,2},{2,0},{1,3},{3,1},{4,6},{6,4},{5,7},{7,5},{8,10},{10,8},{9,1... | collective-permute-start | bytes 122888 | tf_op jit(solution)/shard_map/ppermute | solution.py:48
  163.3 1.7 collective-permute-done.27
  165.8 4.8 %all-to-all-done.3.blocks = bf16[16,80,256]{2,1,0:T(8,128)(2,1)S(1)} async-done(((bf16[16,80,256]{2,1,0:T(8,128)(2,1)}), bf16[16,80,256]{2,1,0:T(8,128)(2,1)S(1)}, u32[]{:S(2)}, u32[]{:S(2)}) %all-to-all-start.3) | async-done | bytes 655392 | tf_op jit(solution)/shard_map/all_to_all | solution.py:75
  (86 shorter events, 9.7 us)
Async XLA Ops:
  0.6 3.2 %copy-start.5 = (bf16[512,269]{0,1:T(8,128)(2,1)S(1)}, bf16[512,269]{0,1:T(8,128)(2,1)}, u32[]{:S(2)}) copy-start(bf16[512,269]{0,1:T(8,128)(2,1)} %param.10) | copy-start | bytes 826372
  0.6 3.2 %copy-start.1 = (bf16[269,1152]{1,0:T(8,128)(2,1)S(1)}, bf16[269,1152]{1,0:T(8,128)(2,1)}, u32[]{:S(2)}) copy-start(bf16[269,1152]{1,0:T(8,128)(2,1)} %proj.2) | copy-start | bytes 1859332
  4.7 3.4 %copy-start.4 = (bf16[512,1152]{1,0:T(8,128)(2,1)}, bf16[512,1152]{1,0:T(8,128)(2,1)S(1)}, u32[]{:S(2)}) copy-start(bf16[512,1152]{1,0:T(8,128)(2,1)S(1)} %convolution_convert_fusion) | copy-start | bytes 3538948
  4.8 11.0 %copy-start.9 = (s32[512]{0:T(512)S(1)}, s32[512]{0:T(512)}, u32[]{:S(2)}) copy-start(s32[512]{0:T(512)} %param.15) | copy-start | bytes 6148
  4.8 14.0 %collective-permute-start = (bf16[4,2,32,1152]{3,2,1,0:T(8,128)(2,1)S(1)}, bf16[4,2,32,1152]{3,2,1,0:T(8,128)(2,1)S(1)}, u32[]{:S(2)}, u32[]{:S(2)}) collective-permute-start(bf16[4,2,32,1152]{3,2,1,0:T(8,128)(2,1)S(1)} %dynamic-slice_bitcast_fusion), channel_id=1, source_target_pairs={{0,1},{1,0},{2,3},{3,2},{4,5},{5,4},{6,7},{7,6},{8,9},{9,8},{10,11... | collective-permute-start | bytes 1769480 | tf_op jit(solution)/shard_map/ppermute | solution.py:48
  8.1 42.0 %all-to-all-start = ((bf16[16,32,1152]{2,1,0:T(8,128)(2,1)}), bf16[16,32,1152]{2,1,0:T(8,128)(2,1)S(1)}, u32[]{:S(2)}, u32[]{:S(2)}) async-start(bf16[16,32,1152]{2,1,0:T(8,128)(2,1)} %bitcast.4), calls=%async_computation | async-start | bytes 2359296 | tf_op jit(solution)/shard_map/all_to_all | solution.py:75
  15.8 8.2 %collective-permute-start.10 = (s32[512]{0:T(512)S(1)}, s32[512]{0:T(512)S(1)}, u32[]{:S(2)}, u32[]{:S(2)}) collective-permute-start(s32[512]{0:T(512)S(1)} %copy-done.9), channel_id=1, source_target_pairs={{0,16},{16,0},{1,17},{17,1},{2,18},{18,2},{3,19},{19,3},{4,20},{20... | collective-permute-start | bytes 6152 | tf_op jit(solution)/shard_map/ppermute | solution.py:48
  18.7 5.2 %copy-start.8 = (bf16[32,1152]{1,0:T(8,128)(2,1)S(1)}, bf16[32,1152]{1,0:T(8,128)(2,1)}, u32[]{:S(2)}) copy-start(bf16[32,1152]{1,0:T(8,128)(2,1)} %param.9) | copy-start | bytes 221188
  20.1 5.6 %collective-permute-start.3 = (bf16[2,32,1152]{2,1,0:T(8,128)(2,1)S(1)}, bf16[2,32,1152]{2,1,0:T(8,128)(2,1)S(1)}, u32[]{:S(2)}, u32[]{:S(2)}) collective-permute-start(bf16[2,32,1152]{2,1,0:T(8,128)(2,1)S(1)} %get-tuple-element.60), channel_id=1, source_target_pairs={{0,12},{4,0},{8,4},{12,8},{1,13},{5,1},{9,5},{13,9},{2,14},{6,2},{... | collective-permute-start | bytes 442376 | tf_op jit(solution)/shard_map/ppermute | solution.py:56
  22.9 5.8 %collective-permute-start.2 = (bf16[2,32,1152]{2,1,0:T(8,128)(2,1)S(1)}, bf16[2,32,1152]{2,1,0:T(8,128)(2,1)S(1)}, u32[]{:S(2)}, u32[]{:S(2)}) collective-permute-start(bf16[2,32,1152]{2,1,0:T(8,128)(2,1)S(1)} %get-tuple-element.61), channel_id=1, source_target_pairs={{0,8},{4,12},{8,0},{12,4},{1,9},{5,13},{9,1},{13,5},{2,10},{6,14},... | collective-permute-start | bytes 442376 | tf_op jit(solution)/shard_map/ppermute | solution.py:56
  23.2 9.2 %collective-permute-start.1 = (bf16[2,32,1152]{2,1,0:T(8,128)(2,1)S(1)}, bf16[2,32,1152]{2,1,0:T(8,128)(2,1)S(1)}, u32[]{:S(2)}, u32[]{:S(2)}) collective-permute-start(bf16[2,32,1152]{2,1,0:T(8,128)(2,1)S(1)} %get-tuple-element.59), channel_id=1, source_target_pairs={{0,4},{4,8},{8,12},{12,0},{1,5},{5,9},{9,13},{13,1},{2,6},{6,10},{... | collective-permute-start | bytes 442376 | tf_op jit(solution)/shard_map/ppermute | solution.py:56
  24.7 25.4 %copy-start.3 = (bf16[32,1152]{1,0:T(8,128)(2,1)S(1)}, bf16[32,1152]{1,0:T(8,128)(2,1)}, u32[]{:S(2)}) copy-start(bf16[32,1152]{1,0:T(8,128)(2,1)} %base.1) | copy-start | bytes 221188
  32.6 12.2 %collective-permute-start.4 = (bf16[2,32,1152]{2,1,0:T(8,128)(2,1)S(1)}, bf16[2,32,1152]{2,1,0:T(8,128)(2,1)S(1)}, u32[]{:S(2)}, u32[]{:S(2)}) collective-permute-start(bf16[2,32,1152]{2,1,0:T(8,128)(2,1)S(1)} %fusion.7), channel_id=1, source_target_pairs={{0,2},{2,0},{16,18},{18,16},{1,3},{3,1},{17,19},{19,17},{4,6},{6,4... | collective-permute-start | bytes 442376 | tf_op jit(solution)/shard_map/ppermute | solution.py:71
  35.2 9.5 %collective-permute-start.6 = (bf16[2,32,1152]{2,1,0:T(8,128)(2,1)S(1)}, bf16[2,32,1152]{2,1,0:T(8,128)(2,1)S(1)}, u32[]{:S(2)}, u32[]{:S(2)}) collective-permute-start(bf16[2,32,1152]{2,1,0:T(8,128)(2,1)S(1)} %fusion.7), channel_id=1, source_target_pairs={{0,18},{2,16},{16,2},{18,0},{1,19},{3,17},{17,3},{19,1},{4,22},{6,... | collective-permute-start | bytes 442376 | tf_op jit(solution)/shard_map/ppermute | solution.py:71
  35.6 14.4 %collective-permute-start.5 = (bf16[2,32,1152]{2,1,0:T(8,128)(2,1)S(1)}, bf16[2,32,1152]{2,1,0:T(8,128)(2,1)S(1)}, u32[]{:S(2)}, u32[]{:S(2)}) collective-permute-start(bf16[2,32,1152]{2,1,0:T(8,128)(2,1)S(1)} %fusion.7), channel_id=1, source_target_pairs={{0,16},{2,18},{16,0},{18,2},{1,17},{3,19},{17,1},{19,3},{4,20},{6,... | collective-permute-start | bytes 442376 | tf_op jit(solution)/shard_map/ppermute | solution.py:71
  51.1 25.3 %all-to-all-start.1 = ((bf16[8,32,1152]{2,1,0:T(8,128)(2,1)}), bf16[8,32,1152]{2,1,0:T(8,128)(2,1)S(1)}, u32[]{:S(2)}, u32[]{:S(2)}) async-start(bf16[8,32,1152]{2,1,0:T(8,128)(2,1)} %get-tuple-element.33), calls=%async_computation.1 | async-start | bytes 1179648 | tf_op jit(solution)/shard_map/all_to_all | solution.py:75
  57.1 7.6 %collective-permute-start.9 = (bf16[2,2,32,1152]{3,2,1,0:T(8,128)(2,1)S(1)}, bf16[2,2,32,1152]{3,2,1,0:T(8,128)(2,1)S(1)}, u32[]{:S(2)}, u32[]{:S(2)}) collective-permute-start(bf16[2,2,32,1152]{3,2,1,0:T(8,128)(2,1)S(1)} %pad_maximum_fusion.2), channel_id=1, source_target_pairs={{0,12},{4,0},{8,4},{12,8},{1,13},{5,1},{9,5},{13,9},{2,14},{6,2},{... | collective-permute-start | bytes 884744 | tf_op jit(solution)/shard_map/ppermute | solution.py:56
  57.1 8.6 %collective-permute-start.8 = (bf16[2,2,32,1152]{3,2,1,0:T(8,128)(2,1)S(1)}, bf16[2,2,32,1152]{3,2,1,0:T(8,128)(2,1)S(1)}, u32[]{:S(2)}, u32[]{:S(2)}) collective-permute-start(bf16[2,2,32,1152]{3,2,1,0:T(8,128)(2,1)S(1)} %pad_maximum_fusion.2), channel_id=1, source_target_pairs={{0,8},{4,12},{8,0},{12,4},{1,9},{5,13},{9,1},{13,5},{2,10},{6,14},... | collective-permute-start | bytes 884744 | tf_op jit(solution)/shard_map/ppermute | solution.py:56
  57.2 16.7 %collective-permute-start.7 = (bf16[2,2,32,1152]{3,2,1,0:T(8,128)(2,1)S(1)}, bf16[2,2,32,1152]{3,2,1,0:T(8,128)(2,1)S(1)}, u32[]{:S(2)}, u32[]{:S(2)}) collective-permute-start(bf16[2,2,32,1152]{3,2,1,0:T(8,128)(2,1)S(1)} %pad_maximum_fusion.2), channel_id=1, source_target_pairs={{0,4},{4,8},{8,12},{12,0},{1,5},{5,9},{9,13},{13,1},{2,6},{6,10},{... | collective-permute-start | bytes 884744 | tf_op jit(solution)/shard_map/ppermute | solution.py:56
  76.5 3.3 %collective-permute-start.11 = (bf16[512,1152]{1,0:T(8,128)(2,1)S(1)}, bf16[512,1152]{1,0:T(8,128)(2,1)S(1)}, u32[]{:S(2)}, u32[]{:S(2)}) collective-permute-start(bf16[512,1152]{1,0:T(8,128)(2,1)S(1)} %bitcast.82), channel_id=1, source_target_pairs={{0,1},{1,0},{2,3},{3,2},{4,5},{5,4},{6,7},{7,6},{8,9},{9,8},{10,11... | collective-permute-start | bytes 3538952 | tf_op jit(solution)/shard_map/ppermute | solution.py:48
  83.8 4.5 %collective-permute-start.12 = (bf16[512,1152]{1,0:T(8,128)(2,1)}, bf16[512,1152]{1,0:T(8,128)(2,1)}, u32[]{:S(2)}, u32[]{:S(2)}) collective-permute-start(bf16[512,1152]{1,0:T(8,128)(2,1)} %get-tuple-element.39), channel_id=1, source_target_pairs={{0,1},{1,0},{2,3},{3,2},{4,5},{5,4},{6,7},{7,6},{8,9},{9,8},{10,11... | collective-permute-start | bytes 3538952 | tf_op jit(solution)/shard_map/ppermute | solution.py:48
  83.9 23.9 %all-to-all-start.2 = ((bf16[8,32,1152]{2,1,0:T(8,128)(2,1)}), bf16[8,32,1152]{2,1,0:T(8,128)(2,1)S(1)}, u32[]{:S(2)}, u32[]{:S(2)}) async-start(bf16[8,32,1152]{2,1,0:T(8,128)(2,1)} %bitcast.28), calls=%async_computation.2 | async-start | bytes 1179648 | tf_op jit(solution)/shard_map/all_to_all | solution.py:75
  90.0 22.6 %collective-permute-start.15 = (bf16[4,32,1152]{2,1,0:T(8,128)(2,1)S(1)}, bf16[4,32,1152]{2,1,0:T(8,128)(2,1)S(1)}, u32[]{:S(2)}, u32[]{:S(2)}) collective-permute-start(bf16[4,32,1152]{2,1,0:T(8,128)(2,1)S(1)} %bitcast.93), channel_id=1, source_target_pairs={{0,4},{4,8},{8,12},{12,0},{1,5},{5,9},{9,13},{13,1},{2,6},{6,10},{... | collective-permute-start | bytes 884744 | tf_op jit(solution)/shard_map/ppermute | solution.py:56
  90.1 22.5 %collective-permute-start.14 = (bf16[4,32,1152]{2,1,0:T(8,128)(2,1)S(1)}, bf16[4,32,1152]{2,1,0:T(8,128)(2,1)S(1)}, u32[]{:S(2)}, u32[]{:S(2)}) collective-permute-start(bf16[4,32,1152]{2,1,0:T(8,128)(2,1)S(1)} %bitcast.92), channel_id=1, source_target_pairs={{0,8},{4,12},{8,0},{12,4},{1,9},{5,13},{9,1},{13,5},{2,10},{6,14},... | collective-permute-start | bytes 884744 | tf_op jit(solution)/shard_map/ppermute | solution.py:56
  92.2 20.5 %collective-permute-start.13 = (bf16[4,32,1152]{2,1,0:T(8,128)(2,1)S(1)}, bf16[4,32,1152]{2,1,0:T(8,128)(2,1)S(1)}, u32[]{:S(2)}, u32[]{:S(2)}) collective-permute-start(bf16[4,32,1152]{2,1,0:T(8,128)(2,1)S(1)} %bitcast.91), channel_id=1, source_target_pairs={{0,12},{4,0},{8,4},{12,8},{1,13},{5,1},{9,5},{13,9},{2,14},{6,2},{... | collective-permute-start | bytes 884744 | tf_op jit(solution)/shard_map/ppermute | solution.py:56
  108.9 34.3 %all-to-all-start.4 = ((bf16[16,32,1152]{2,1,0:T(8,128)(2,1)}), bf16[16,32,1152]{2,1,0:T(8,128)(2,1)S(1)}, u32[]{:S(2)}, u32[]{:S(2)}) async-start(bf16[16,32,1152]{2,1,0:T(8,128)(2,1)} %get-tuple-element.45), calls=%async_computation.4 | async-start | bytes 2359296 | tf_op jit(solution)/shard_map/all_to_all | solution.py:75
  112.9 7.0 %collective-permute-start.18 = (bf16[2,40,1152]{2,1,0:T(8,128)(2,1)S(1)}, bf16[2,40,1152]{2,1,0:T(8,128)(2,1)S(1)}, u32[]{:S(2)}, u32[]{:S(2)}) collective-permute-start(bf16[2,40,1152]{2,1,0:T(8,128)(2,1)S(1)} %get-tuple-element.63), channel_id=1, source_target_pairs={{0,18},{2,16},{16,2},{18,0},{1,19},{3,17},{17,3},{19,1},{4,22},{6,... | collective-permute-start | bytes 552968 | tf_op jit(solution)/shard_map/ppermute | solution.py:71
  115.0 5.1 %collective-permute-start.17 = (bf16[2,40,1152]{2,1,0:T(8,128)(2,1)S(1)}, bf16[2,40,1152]{2,1,0:T(8,128)(2,1)S(1)}, u32[]{:S(2)}, u32[]{:S(2)}) collective-permute-start(bf16[2,40,1152]{2,1,0:T(8,128)(2,1)S(1)} %get-tuple-element.63), channel_id=1, source_target_pairs={{0,16},{2,18},{16,0},{18,2},{1,17},{3,19},{17,1},{19,3},{4,20},{6,... | collective-permute-start | bytes 552968 | tf_op jit(solution)/shard_map/ppermute | solution.py:71
  115.0 24.0 %copy-start.6 = (bf16[512,269]{0,1:T(8,128)(2,1)S(1)}, bf16[512,269]{0,1:T(8,128)(2,1)}, u32[]{:S(2)}) copy-start(bf16[512,269]{0,1:T(8,128)(2,1)} %param.10) | copy-start | bytes 826372
  115.1 9.9 %collective-permute-start.16 = (bf16[2,40,1152]{2,1,0:T(8,128)(2,1)S(1)}, bf16[2,40,1152]{2,1,0:T(8,128)(2,1)S(1)}, u32[]{:S(2)}, u32[]{:S(2)}) collective-permute-start(bf16[2,40,1152]{2,1,0:T(8,128)(2,1)S(1)} %get-tuple-element.62), channel_id=1, source_target_pairs={{0,2},{2,0},{16,18},{18,16},{1,3},{3,1},{17,19},{19,17},{4,6},{6,4... | collective-permute-start | bytes 552968 | tf_op jit(solution)/shard_map/ppermute | solution.py:71
  125.1 13.9 %copy-start.7 = (bf16[512,269]{0,1:T(8,128)(2,1)S(1)}, bf16[512,269]{0,1:T(8,128)(2,1)}, u32[]{:S(2)}) copy-start(bf16[512,269]{0,1:T(8,128)(2,1)} %param.13) | copy-start | bytes 826372
  125.1 4.8 %collective-permute-start.21 = (bf16[2,40,1152]{2,1,0:T(8,128)(2,1)S(1)}, bf16[2,40,1152]{2,1,0:T(8,128)(2,1)S(1)}, u32[]{:S(2)}, u32[]{:S(2)}) collective-permute-start(bf16[2,40,1152]{2,1,0:T(8,128)(2,1)S(1)} %add_convert_fusion.2), channel_id=1, source_target_pairs={{0,12},{4,0},{8,4},{12,8},{1,13},{5,1},{9,5},{13,9},{2,14},{6,2},{... | collective-permute-start | bytes 552968 | tf_op jit(solution)/shard_map/ppermute | solution.py:56
  126.1 6.0 %collective-permute-start.20 = (bf16[2,40,1152]{2,1,0:T(8,128)(2,1)S(1)}, bf16[2,40,1152]{2,1,0:T(8,128)(2,1)S(1)}, u32[]{:S(2)}, u32[]{:S(2)}) collective-permute-start(bf16[2,40,1152]{2,1,0:T(8,128)(2,1)S(1)} %add_convert_fusion.2), channel_id=1, source_target_pairs={{0,8},{4,12},{8,0},{12,4},{1,9},{5,13},{9,1},{13,5},{2,10},{6,14},... | collective-permute-start | bytes 552968 | tf_op jit(solution)/shard_map/ppermute | solution.py:56
  126.1 11.4 %collective-permute-start.19 = (bf16[2,40,1152]{2,1,0:T(8,128)(2,1)S(1)}, bf16[2,40,1152]{2,1,0:T(8,128)(2,1)S(1)}, u32[]{:S(2)}, u32[]{:S(2)}) collective-permute-start(bf16[2,40,1152]{2,1,0:T(8,128)(2,1)S(1)} %add_convert_fusion.2), channel_id=1, source_target_pairs={{0,4},{4,8},{8,12},{12,0},{1,5},{5,9},{9,13},{13,1},{2,6},{6,10},{... | collective-permute-start | bytes 552968 | tf_op jit(solution)/shard_map/ppermute | solution.py:56
  137.6 3.3 %copy-start.2 = (bf16[269,1152]{1,0:T(8,128)(2,1)S(1)}, bf16[269,1152]{1,0:T(8,128)(2,1)}, u32[]{:S(2)}) copy-start(bf16[269,1152]{1,0:T(8,128)(2,1)} %proj.2) | copy-start | bytes 1859332
  137.7 3.2 %collective-permute-start.22 = (bf16[4,2,40,1152]{3,2,1,0:T(8,128)(2,1)S(1)}, bf16[4,2,40,1152]{3,2,1,0:T(8,128)(2,1)S(1)}, u32[]{:S(2)}, u32[]{:S(2)}) collective-permute-start(bf16[4,2,40,1152]{3,2,1,0:T(8,128)(2,1)S(1)} %pad_maximum_fusion.1.own), channel_id=1, source_target_pairs={{0,1},{1,0},{2,3},{3,2},{4,5},{5,4},{6,7},{7,6},{8,9},{9,8},{10,11... | collective-permute-start | bytes 2211848 | tf_op jit(solution)/shard_map/ppermute | solution.py:48
  139.2 4.1 %copy-start = (bf16[269,1152]{1,0:T(8,128)(2,1)S(1)}, bf16[269,1152]{1,0:T(8,128)(2,1)}, u32[]{:S(2)}) copy-start(bf16[269,1152]{1,0:T(8,128)(2,1)} %proj.3) | copy-start | bytes 1859332
  145.6 6.4 %collective-permute-start.23 = (bf16[4,2,80,256]{3,2,1,0:T(8,128)(2,1)S(1)}, bf16[4,2,80,256]{3,2,1,0:T(8,128)(2,1)S(1)}, u32[]{:S(2)}, u32[]{:S(2)}) collective-permute-start(bf16[4,2,80,256]{3,2,1,0:T(8,128)(2,1)S(1)} %get-tuple-element.48), channel_id=1, source_target_pairs={{0,1},{1,0},{2,3},{3,2},{4,5},{5,4},{6,7},{7,6},{8,9},{9,8},{10,11... | collective-permute-start | bytes 983048 | tf_op jit(solution)/shard_map/ppermute | solution.py:48
  147.4 23.2 %all-to-all-start.3 = ((bf16[16,80,256]{2,1,0:T(8,128)(2,1)}), bf16[16,80,256]{2,1,0:T(8,128)(2,1)S(1)}, u32[]{:S(2)}, u32[]{:S(2)}) async-start(bf16[16,80,256]{2,1,0:T(8,128)(2,1)} %get-tuple-element.44), calls=%async_computation.3 | async-start | bytes 1310720 | tf_op jit(solution)/shard_map/all_to_all | solution.py:75
  152.1 3.7 %collective-permute-start.26 = (bf16[2,80,256]{2,1,0:T(8,128)(2,1)S(1)}, bf16[2,80,256]{2,1,0:T(8,128)(2,1)S(1)}, u32[]{:S(2)}, u32[]{:S(2)}) collective-permute-start(bf16[2,80,256]{2,1,0:T(8,128)(2,1)S(1)} %get-tuple-element.65), channel_id=1, source_target_pairs={{0,12},{4,0},{8,4},{12,8},{1,13},{5,1},{9,5},{13,9},{2,14},{6,2},{... | collective-permute-start | bytes 245768 | tf_op jit(solution)/shard_map/ppermute | solution.py:56
  152.7 4.8 %collective-permute-start.25 = (bf16[2,80,256]{2,1,0:T(8,128)(2,1)S(1)}, bf16[2,80,256]{2,1,0:T(8,128)(2,1)S(1)}, u32[]{:S(2)}, u32[]{:S(2)}) collective-permute-start(bf16[2,80,256]{2,1,0:T(8,128)(2,1)S(1)} %get-tuple-element.66), channel_id=1, source_target_pairs={{0,8},{4,12},{8,0},{12,4},{1,9},{5,13},{9,1},{13,5},{2,10},{6,14},... | collective-permute-start | bytes 245768 | tf_op jit(solution)/shard_map/ppermute | solution.py:56
  153.1 7.0 %collective-permute-start.24 = (bf16[2,80,256]{2,1,0:T(8,128)(2,1)S(1)}, bf16[2,80,256]{2,1,0:T(8,128)(2,1)S(1)}, u32[]{:S(2)}, u32[]{:S(2)}) collective-permute-start(bf16[2,80,256]{2,1,0:T(8,128)(2,1)S(1)} %get-tuple-element.64), channel_id=1, source_target_pairs={{0,4},{4,8},{8,12},{12,0},{1,5},{5,9},{9,13},{13,1},{2,6},{6,10},{... | collective-permute-start | bytes 245768 | tf_op jit(solution)/shard_map/ppermute | solution.py:56
  160.2 4.8 %collective-permute-start.27 = (bf16[80,256]{1,0:T(8,128)(2,1)S(1)}, bf16[80,256]{1,0:T(8,128)(2,1)S(1)}, u32[]{:S(2)}, u32[]{:S(2)}) collective-permute-start(bf16[80,256]{1,0:T(8,128)(2,1)S(1)} %get-tuple-element.68), channel_id=1, source_target_pairs={{0,2},{2,0},{1,3},{3,1},{4,6},{6,4},{5,7},{7,5},{8,10},{10,8},{9,1... | collective-permute-start | bytes 122888 | tf_op jit(solution)/shard_map/ppermute | solution.py:48
